TPU v7x, 32 devices: a whole 2x2x4 slice. The times are simulated.
32 devices in a mesh: rows: 4 (over y, x), blk: 8 (over z, core).
Axes of the slice: x: 2, y: 2, z: 4, core: 2. Of those that a mesh axis runs over, the one named last changes fastest.
Arguments:
- tokens: bfloat16 [4, 1024, 2048], P('rows', 'blk'), may hold values from -6 to 6
- segments: int32 [4, 1024], P('rows', 'blk'), may hold values from 0 to 4, as said below
- cotangent: bfloat16 [4, 1024, 2048], P('rows', 'blk'), may hold values from -6 to 6
- attend_gain: bfloat16 [2048], P(('rows', 'blk')), may hold values from 0.5 to 1.5
- attend_shift: bfloat16 [2048], P(('rows', 'blk')), may hold values from -3 to 3
- project_weight: bfloat16 [2048, 6144], P(('rows', 'blk')), may hold values from -0.125 to 0.125
- project_bias: bfloat16 [6144], P(('rows', 'blk')), may hold values from -3 to 3
- output_weight: bfloat16 [2048, 2048], P(('rows', 'blk')), may hold values from -0.75 to 0.75
- feed_gain: bfloat16 [2048], P(('rows', 'blk')), may hold values from 0.5 to 1.5
- feed_shift: bfloat16 [2048], P(('rows', 'blk')), may hold values from -3 to 3
- gate_weight: bfloat16 [2048, 5632], P(('rows', 'blk')), may hold values from -0.125 to 0.125
- up_weight: bfloat16 [2048, 5632], P(('rows', 'blk')), may hold values from -0.125 to 0.125
- down_weight: bfloat16 [5632, 2048], P(('rows', 'blk')), may hold values from -0.078125 to 0.078125
Outputs:
- output: bfloat16 [4, 1024, 2048], P('rows', 'blk')
- tokens_grad: float32 [4, 1024, 2048], P('rows', 'blk')
- attend_gain_grad: float32 [2048], P(('rows', 'blk'))
- attend_shift_grad: float32 [2048], P(('rows', 'blk'))
- project_weight_grad: float32 [2048, 6144], P(('rows', 'blk'))
- project_bias_grad: float32 [6144], P(('rows', 'blk'))
- output_weight_grad: float32 [2048, 2048], P(('rows', 'blk'))
- feed_gain_grad: float32 [2048], P(('rows', 'blk'))
- feed_shift_grad: float32 [2048], P(('rows', 'blk'))
- gate_weight_grad: float32 [2048, 5632], P(('rows', 'blk'))
- up_weight_grad: float32 [2048, 5632], P(('rows', 'blk'))
- down_weight_grad: float32 [5632, 2048], P(('rows', 'blk'))
Inputs may be any that keep to these rules, and one draw needn't show every extreme that they name: `segments`: in each sequence the segment ids start at 0, never fall and rise by one at each of four document starts; one document begins within the first 128 tokens and ends within the last 128 tokens, at least two tokens from either end.
All inputs are finite; a program needn't handle non-finite values.
Results may differ from a plain program's by a relative error of at most 0.039.
Values may be sent and summed in bfloat16 or wider, within the bound.
A program may use at most 312 MiB of HBM per device.

v0:
```python
import math

import jax
import jax.numpy as jnp
from jax import lax
from jax.sharding import PartitionSpec as P

HEADS = 32
ROT = 16


epsilon = 1e-05
rotary_base = 10000.0
masked_value = -1e30


def layer_norm(inputs, gain, shift):
    row_mean = jnp.mean(inputs, axis=-1, keepdims=True)
    centered = inputs - row_mean
    variance = jnp.mean(centered * centered, axis=-1, keepdims=True)
    return centered * lax.rsqrt(variance + epsilon) * gain + shift


def rotary(columns, places, head_count, rot_dims):
    head_width = columns.shape[-1] // head_count
    split_heads = columns.reshape(columns.shape[:-1] + (head_count, head_width))
    half_rot = rot_dims // 2
    frequency = jnp.power(
        rotary_base, -jnp.arange(half_rot, dtype=jnp.int32).astype(jnp.float32) / half_rot
    )
    angles = places.astype(jnp.float32)[..., None] * frequency
    cosine = jnp.cos(angles)[..., None, :]
    sine_part = jnp.sin(angles)[..., None, :]
    first_part = split_heads[..., :half_rot]
    second_part = split_heads[..., half_rot:rot_dims]
    rest_part = split_heads[..., rot_dims:]
    turned = jnp.concatenate(
        [
            first_part * cosine - second_part * sine_part,
            second_part * cosine + first_part * sine_part,
            rest_part,
        ],
        axis=-1,
    )
    return turned.reshape(columns.shape)


def places_of(row_segments, query_segments, query_index):
    doc_starts = jnp.sum(
        (row_segments[None, :] < query_segments[:, None]).astype(jnp.int32), axis=1
    )
    return query_index - doc_starts


def allowed(query_index, query_segments, key_index, key_segments):
    return (key_index[None, :] <= query_index[:, None]) & (
        key_segments[None, :] == query_segments[:, None]
    )


def project_heads(inputs, attend_set, places):
    model_width = inputs.shape[1]
    normed_first = layer_norm(
        inputs, attend_set[0].astype(jnp.float32), attend_set[1].astype(jnp.float32)
    ).astype(jnp.bfloat16)
    mixed_proj = jnp.dot(
        normed_first, attend_set[2], preferred_element_type=jnp.float32
    ) + attend_set[3].astype(jnp.float32)
    queries = rotary(mixed_proj[:, :model_width], places, HEADS, ROT).astype(jnp.bfloat16)
    key_rows = rotary(mixed_proj[:, model_width : 2 * model_width], places, HEADS, ROT).astype(
        jnp.bfloat16
    )
    value_rows = mixed_proj[:, 2 * model_width :].astype(jnp.bfloat16)
    return (normed_first, queries, key_rows, value_rows)


def feed_front(resid_mid, feed_set):
    normed_second = layer_norm(
        resid_mid, feed_set[0].astype(jnp.float32), feed_set[1].astype(jnp.float32)
    ).astype(jnp.bfloat16)
    gate_value = jnp.dot(normed_second, feed_set[2], preferred_element_type=jnp.float32)
    up_value = jnp.dot(normed_second, feed_set[3], preferred_element_type=jnp.float32)
    hidden = (jax.nn.silu(gate_value) * up_value).astype(jnp.bfloat16)
    return (normed_second, gate_value, up_value, hidden)


def body(
    tokens,
    segments,
    cotangent,
    attend_gain,
    attend_shift,
    project_weight,
    project_bias,
    output_weight,
    feed_gain,
    feed_shift,
    gate_weight,
    up_weight,
    down_weight,
):
    shard_rows = tokens.shape[1]
    model_width = tokens.shape[2]
    head_width = model_width // HEADS
    score_scale = 1.0 / math.sqrt(head_width)
    query_index = lax.axis_index("blk") * shard_rows + jnp.arange(shard_rows, dtype=jnp.int32)
    last_query = query_index[shard_rows - 1]
    first_key = query_index[0]
    own_segments = segments[0]
    all_segments = lax.all_gather(segments, "blk", axis=1, tiled=True)[0]
    places = places_of(all_segments, own_segments, query_index)
    inputs = tokens[0].astype(jnp.float32)

    def block_mask(block_start, block_rows):
        key_index = block_start + jnp.arange(block_rows, dtype=jnp.int32)
        key_segments = lax.dynamic_slice_in_dim(all_segments, block_start, block_rows, 0)
        return allowed(query_index, own_segments, key_index, key_segments)[None]

    attend_set = (
        lax.all_gather(attend_gain, ("rows", "blk"), axis=0, tiled=True),
        lax.all_gather(attend_shift, ("rows", "blk"), axis=0, tiled=True),
        lax.all_gather(project_weight, ("rows", "blk"), axis=0, tiled=True),
        lax.all_gather(project_bias, ("rows", "blk"), axis=0, tiled=True),
        lax.all_gather(output_weight, ("rows", "blk"), axis=0, tiled=True),
    )
    normed_first, queries, key_rows, value_rows = project_heads(inputs, attend_set, places)
    query_heads = queries.reshape(shard_rows, HEADS, head_width)
    initial = (
        jnp.full((HEADS, shard_rows), masked_value, jnp.float32),
        jnp.zeros((HEADS, shard_rows), jnp.float32),
        jnp.zeros((HEADS, shard_rows, head_width), jnp.float32),
    )
    key_piece = lax.all_gather(key_rows, "blk", axis=0, tiled=True)
    value_piece = lax.all_gather(value_rows, "blk", axis=0, tiled=True)
    piece_rows = key_piece.shape[0]
    block_rows = math.gcd(piece_rows, 512)

    def one_block(block_number, carry_state):
        block_start = block_number * block_rows

        def attend_block(state_in):
            running_top, row_total, summed = state_in
            key_block = lax.dynamic_slice_in_dim(
                key_piece, block_number * block_rows, block_rows, 0
            ).reshape(block_rows, HEADS, head_width)
            value_block = lax.dynamic_slice_in_dim(
                value_piece, block_number * block_rows, block_rows, 0
            ).reshape(block_rows, HEADS, head_width)
            allowed_mask = block_mask(block_start, block_rows)
            scores = (
                jnp.einsum(
                    "qhd,khd->hqk", query_heads, key_block, preferred_element_type=jnp.float32
                )
                * score_scale
            )
            scores = jnp.where(allowed_mask, scores, masked_value)
            new_top = jnp.maximum(running_top, jnp.max(scores, axis=2))
            weights = jnp.where(allowed_mask, jnp.exp(scores - new_top[:, :, None]), 0.0)
            decay_factor = jnp.exp(running_top - new_top)
            row_total = row_total * decay_factor + jnp.sum(weights, axis=2)
            summed = summed * decay_factor[:, :, None] + jnp.einsum(
                "hqk,khd->hqd",
                weights.astype(jnp.bfloat16),
                value_block,
                preferred_element_type=jnp.float32,
            )
            return (new_top, row_total, summed)

        return lax.cond(
            block_start > last_query, lambda kept_state: kept_state, attend_block, carry_state
        )

    running_top, row_total, summed = lax.fori_loop(0, piece_rows // block_rows, one_block, initial)
    attended = jnp.transpose(summed / row_total[:, :, None], (1, 0, 2)).reshape(
        shard_rows, model_width
    )
    log_total = running_top + jnp.log(row_total)
    attended_low = attended.astype(jnp.bfloat16)
    resid_mid = inputs + jnp.dot(attended_low, attend_set[4], preferred_element_type=jnp.float32)
    feed_set = (
        lax.all_gather(feed_gain, ("rows", "blk"), axis=0, tiled=True),
        lax.all_gather(feed_shift, ("rows", "blk"), axis=0, tiled=True),
        lax.all_gather(gate_weight, ("rows", "blk"), axis=0, tiled=True),
        lax.all_gather(up_weight, ("rows", "blk"), axis=0, tiled=True),
        lax.all_gather(down_weight, ("rows", "blk"), axis=0, tiled=True),
    )
    normed_second, gate_value, up_value, hidden = feed_front(resid_mid, feed_set)
    output = (resid_mid + jnp.dot(hidden, feed_set[4], preferred_element_type=jnp.float32)).astype(
        jnp.bfloat16
    )
    feed_set = (
        lax.all_gather(feed_gain, ("rows", "blk"), axis=0, tiled=True),
        lax.all_gather(feed_shift, ("rows", "blk"), axis=0, tiled=True),
        lax.all_gather(gate_weight, ("rows", "blk"), axis=0, tiled=True),
        lax.all_gather(up_weight, ("rows", "blk"), axis=0, tiled=True),
        lax.all_gather(down_weight, ("rows", "blk"), axis=0, tiled=True),
    )
    normed_second, gate_value, up_value, hidden = feed_front(resid_mid, feed_set)
    grad_out = cotangent[0].astype(jnp.float32)
    grad_branch = cotangent[0]
    down_grad = jnp.einsum("tf,td->fd", hidden, grad_branch, preferred_element_type=jnp.float32)
    grad_hidden = jnp.einsum(
        "td,fd->tf", grad_branch, feed_set[4], preferred_element_type=jnp.float32
    )
    gate_sigmoid = jax.nn.sigmoid(gate_value)
    grad_gate = (
        grad_hidden * up_value * gate_sigmoid * (1.0 + gate_value * (1.0 - gate_sigmoid))
    ).astype(jnp.bfloat16)
    grad_up = (grad_hidden * jax.nn.silu(gate_value)).astype(jnp.bfloat16)
    gate_grad = jnp.einsum(
        "td,tf->df", normed_second, grad_gate, preferred_element_type=jnp.float32
    )
    up_grad = jnp.einsum("td,tf->df", normed_second, grad_up, preferred_element_type=jnp.float32)
    grad_normed_second = jnp.einsum(
        "tf,df->td", grad_gate, feed_set[2], preferred_element_type=jnp.float32
    ) + jnp.einsum("tf,df->td", grad_up, feed_set[3], preferred_element_type=jnp.float32)
    normed_again, pullback = jax.vjp(
        layer_norm, resid_mid, feed_set[0].astype(jnp.float32), feed_set[1].astype(jnp.float32)
    )
    mid_part, feed_gain_part, feed_shift_part = pullback(grad_normed_second)
    grad_mid = grad_out + mid_part
    feed_grads = (
        lax.psum_scatter(feed_gain_part, ("rows", "blk"), scatter_dimension=0, tiled=True),
        lax.psum_scatter(feed_shift_part, ("rows", "blk"), scatter_dimension=0, tiled=True),
        lax.psum_scatter(gate_grad, ("rows", "blk"), scatter_dimension=0, tiled=True),
        lax.psum_scatter(up_grad, ("rows", "blk"), scatter_dimension=0, tiled=True),
        lax.psum_scatter(down_grad, ("rows", "blk"), scatter_dimension=0, tiled=True),
    )
    attend_set = (
        lax.all_gather(attend_gain, ("rows", "blk"), axis=0, tiled=True),
        lax.all_gather(attend_shift, ("rows", "blk"), axis=0, tiled=True),
        lax.all_gather(project_weight, ("rows", "blk"), axis=0, tiled=True),
        lax.all_gather(project_bias, ("rows", "blk"), axis=0, tiled=True),
        lax.all_gather(output_weight, ("rows", "blk"), axis=0, tiled=True),
    )
    normed_first, queries, key_rows, value_rows = project_heads(inputs, attend_set, places)
    query_back = queries.reshape(shard_rows, HEADS, head_width)
    grad_mid_low = grad_mid.astype(jnp.bfloat16)
    out_weight_grad = jnp.einsum(
        "td,te->de", attended_low, grad_mid_low, preferred_element_type=jnp.float32
    )
    grad_attended = jnp.einsum(
        "te,de->td", grad_mid_low, attend_set[4], preferred_element_type=jnp.float32
    ).astype(jnp.bfloat16)
    row_delta = jnp.transpose(
        jnp.sum(
            (grad_attended.astype(jnp.float32) * attended).reshape(shard_rows, HEADS, head_width),
            axis=2,
        )
    )
    grad_heads = grad_attended.reshape(shard_rows, HEADS, head_width)
    query_zeros = jnp.zeros((shard_rows, HEADS, head_width), jnp.float32)
    initial_back = (query_zeros,)
    attend_key_piece = lax.all_gather(key_rows, "blk", axis=0, tiled=True)
    attend_value_piece = lax.all_gather(value_rows, "blk", axis=0, tiled=True)
    piece_rows = attend_key_piece.shape[0]
    attend_block_rows = math.gcd(piece_rows, 512)

    def one_block(block_number, carry_state):
        block_start = block_number * attend_block_rows

        def attend_block(state_in):
            grad_queries = state_in[0]
            key_block = lax.dynamic_slice_in_dim(
                attend_key_piece, block_number * attend_block_rows, attend_block_rows, 0
            ).reshape(attend_block_rows, HEADS, head_width)
            value_block = lax.dynamic_slice_in_dim(
                attend_value_piece, block_number * attend_block_rows, attend_block_rows, 0
            ).reshape(attend_block_rows, HEADS, head_width)
            allowed_mask = block_mask(block_start, attend_block_rows)
            scores = (
                jnp.einsum(
                    "qhd,khd->hqk", query_back, key_block, preferred_element_type=jnp.float32
                )
                * score_scale
            )
            probs = jnp.where(allowed_mask, jnp.exp(scores - log_total[:, :, None]), 0.0)
            grad_probs = jnp.einsum(
                "qhd,khd->hqk", grad_heads, value_block, preferred_element_type=jnp.float32
            )
            grad_scores = (probs * (grad_probs - row_delta[:, :, None]) * score_scale).astype(
                jnp.bfloat16
            )
            grad_queries = grad_queries + jnp.einsum(
                "hqk,khd->qhd", grad_scores, key_block, preferred_element_type=jnp.float32
            )
            return (grad_queries,)

        return lax.cond(
            block_start > last_query, lambda kept_state: kept_state, attend_block, carry_state
        )

    folded_back = lax.fori_loop(0, piece_rows // attend_block_rows, one_block, initial_back)
    grad_queries = folded_back[0]
    key_heads = key_rows.reshape(shard_rows, HEADS, head_width)
    value_heads = value_rows.reshape(shard_rows, HEADS, head_width)
    owner_initial = (query_zeros, query_zeros)
    query_piece = lax.all_gather(
        queries.astype(jnp.float32).astype(jnp.bfloat16), "blk", axis=0, tiled=True
    ).astype(jnp.float32)
    grad_piece = lax.all_gather(
        grad_attended.astype(jnp.float32).astype(jnp.bfloat16), "blk", axis=0, tiled=True
    ).astype(jnp.float32)
    total_piece = lax.all_gather(
        jnp.transpose(log_total).astype(jnp.bfloat16), "blk", axis=0, tiled=True
    ).astype(jnp.float32)
    delta_piece = lax.all_gather(
        jnp.transpose(row_delta).astype(jnp.bfloat16), "blk", axis=0, tiled=True
    ).astype(jnp.float32)
    piece_rows = query_piece.shape[0]
    owner_block_rows = math.gcd(piece_rows, 512)

    def one_block(block_number, carry_state):
        block_start = block_number * owner_block_rows

        def owner_block(state_in):
            keys_acc, values_acc = state_in
            query_block = (
                lax.dynamic_slice_in_dim(
                    query_piece, block_number * owner_block_rows, owner_block_rows, 0
                )
                .astype(jnp.bfloat16)
                .reshape(owner_block_rows, HEADS, head_width)
            )
            grad_block = (
                lax.dynamic_slice_in_dim(
                    grad_piece, block_number * owner_block_rows, owner_block_rows, 0
                )
                .astype(jnp.bfloat16)
                .reshape(owner_block_rows, HEADS, head_width)
            )
            total_block = jnp.transpose(
                lax.dynamic_slice_in_dim(
                    total_piece, block_number * owner_block_rows, owner_block_rows, 0
                )
            )
            delta_block = jnp.transpose(
                lax.dynamic_slice_in_dim(
                    delta_piece, block_number * owner_block_rows, owner_block_rows, 0
                )
            )
            block_index = block_start + jnp.arange(owner_block_rows, dtype=jnp.int32)
            block_segments = lax.dynamic_slice_in_dim(
                all_segments, block_start, owner_block_rows, 0
            )
            allowed_mask = allowed(block_index, block_segments, query_index, own_segments)[None]
            scores = (
                jnp.einsum(
                    "qhd,khd->hqk", query_block, key_heads, preferred_element_type=jnp.float32
                )
                * score_scale
            )
            probs = jnp.where(allowed_mask, jnp.exp(scores - total_block[:, :, None]), 0.0)
            values_acc = values_acc + jnp.einsum(
                "hqk,qhd->khd",
                probs.astype(jnp.bfloat16),
                grad_block,
                preferred_element_type=jnp.float32,
            )
            grad_probs = jnp.einsum(
                "qhd,khd->hqk", grad_block, value_heads, preferred_element_type=jnp.float32
            )
            grad_scores = (probs * (grad_probs - delta_block[:, :, None]) * score_scale).astype(
                jnp.bfloat16
            )
            keys_acc = keys_acc + jnp.einsum(
                "hqk,qhd->khd", grad_scores, query_block, preferred_element_type=jnp.float32
            )
            return (keys_acc, values_acc)

        return lax.cond(
            block_start + owner_block_rows - 1 < first_key,
            lambda kept_state: kept_state,
            owner_block,
            carry_state,
        )

    keys_acc, values_acc = lax.fori_loop(
        0, piece_rows // owner_block_rows, one_block, owner_initial
    )
    keys_own = keys_acc.reshape(shard_rows, model_width)
    values_own = values_acc.reshape(shard_rows, model_width)
    grad_mixed = jnp.concatenate(
        [
            rotary(grad_queries.reshape(shard_rows, model_width), -places, HEADS, ROT),
            rotary(keys_own, -places, HEADS, ROT),
            values_own,
        ],
        axis=1,
    ).astype(jnp.bfloat16)
    project_grad = jnp.einsum(
        "td,te->de", normed_first, grad_mixed, preferred_element_type=jnp.float32
    )
    bias_grad = jnp.sum(grad_mixed.astype(jnp.float32), axis=0)
    grad_normed_first = jnp.einsum(
        "te,de->td", grad_mixed, attend_set[2], preferred_element_type=jnp.float32
    )
    normed_check, pullback_first = jax.vjp(
        layer_norm, inputs, attend_set[0].astype(jnp.float32), attend_set[1].astype(jnp.float32)
    )
    input_part, attend_gain_part, attend_shift_part = pullback_first(grad_normed_first)
    grad_tokens = grad_mid + input_part
    attend_grads = (
        lax.psum_scatter(attend_gain_part, ("rows", "blk"), scatter_dimension=0, tiled=True),
        lax.psum_scatter(attend_shift_part, ("rows", "blk"), scatter_dimension=0, tiled=True),
        lax.psum_scatter(project_grad, ("rows", "blk"), scatter_dimension=0, tiled=True),
        lax.psum_scatter(bias_grad, ("rows", "blk"), scatter_dimension=0, tiled=True),
        lax.psum_scatter(out_weight_grad, ("rows", "blk"), scatter_dimension=0, tiled=True),
    )
    return (
        output[None],
        grad_tokens[None],
        attend_grads[0],
        attend_grads[1],
        attend_grads[2],
        attend_grads[3],
        attend_grads[4],
        feed_grads[0],
        feed_grads[1],
        feed_grads[2],
        feed_grads[3],
        feed_grads[4],
    )


def solution(mesh):
    in_specs = (
        P("rows", "blk", None),
        P("rows", "blk"),
        P("rows", "blk", None),
        P(("rows", "blk")),
        P(("rows", "blk")),
        P(("rows", "blk"), None),
        P(("rows", "blk")),
        P(("rows", "blk"), None),
        P(("rows", "blk")),
        P(("rows", "blk")),
        P(("rows", "blk"), None),
        P(("rows", "blk"), None),
        P(("rows", "blk"), None),
    )
    out_specs = (
        P("rows", "blk", None),
        P("rows", "blk", None),
        P(("rows", "blk")),
        P(("rows", "blk")),
        P(("rows", "blk"), None),
        P(("rows", "blk")),
        P(("rows", "blk"), None),
        P(("rows", "blk")),
        P(("rows", "blk")),
        P(("rows", "blk"), None),
        P(("rows", "blk"), None),
        P(("rows", "blk"), None),
    )
    return jax.shard_map(body, mesh=mesh, in_specs=in_specs, out_specs=out_specs, check_vma=False)
```

profile of v0, /device:TPU:0, one launch (start us, length us, event | category | flops | bytes accessed | tf_op | source)
XLA Modules:
  0.0 3053.3 jit_solution(15246624236072687172)
XLA Ops:
  12.2 43.5 %all-reduce.11 = (bf16[6144]{0:T(1024)(128)(2,1)S(1)}, bf16[2048]{0:T(1024)(128)(2,1)S(1)}, bf16[2048]{0:T(1024)(128)(2,1)S(1)}, bf16[2048]{0:T(1024)(128)(2,1)S(1)}, bf16[2048]{0:T(1024)(128)(2,1)S(1)}) all-reduce(bf16[6144]{0:T(1024)(128)(2,1)S(1)} %dynamic-update-slice.2, ...), channel_id=1, replica_groups=mesh['rows'=4,'blk'=8] {'rows','blk'}, use_global_device_ids=true, to_apply=%add.2 | all-reduce | flops 14336 | bytes 57344
  58.3 111.6 %all-gather.10.cloned.1.call-done = bf16[2048,6144]{1,0:T(8,128)(2,1)} async-done(((bf16[64,6144]{1,0:T(8,128)(2,1)}), bf16[2048,6144]{1,0:T(8,128)(2,1)}) %all-gather.10.cloned.1.call-update) | async-done | bytes 25165840 | tf_op jit(solution)/shard_map/all_gather | solution.py:122
  201.0 25.7 all-gather.14.cloned.1.call-done
  233.0 42.3 %all-gather.12.cloned.1.call-done = bf16[1024,2048]{0,1:T(8,128)(2,1)} async-done(((bf16[128,2048]{0,1:T(8,128)(2,1)}), bf16[1024,2048]{0,1:T(8,128)(2,1)}) %all-gather.12.cloned.1.call-update) | async-done | bytes 4194320 | tf_op jit(solution)/shard_map/all_gather | solution.py:133
  276.4 13.4 while.55
  292.8 61.1 %all-gather.16.cloned.1.call-done = bf16[2048,2048]{1,0:T(8,128)(2,1)} async-done(((bf16[64,2048]{1,0:T(8,128)(2,1)}), bf16[2048,2048]{1,0:T(8,128)(2,1)}) %all-gather.16.cloned.1.call-update) | async-done | bytes 8388624 | tf_op jit(solution)/shard_map/all_gather | solution.py:124
  359.5 140.3 %all-gather.18.cloned.1.call-done = bf16[2048,5632]{1,0:T(8,128)(2,1)} async-done(((bf16[64,5632]{1,0:T(8,128)(2,1)}), bf16[2048,5632]{1,0:T(8,128)(2,1)}) %all-gather.18.cloned.1.call-update) | async-done | bytes 23068688 | tf_op jit(solution)/shard_map/all_gather | solution.py:183
  499.8 12.3 fusion.93
  512.1 133.3 %all-gather.20.cloned.1.call-done = bf16[2048,5632]{1,0:T(8,128)(2,1)} async-done(((bf16[64,5632]{1,0:T(8,128)(2,1)}), bf16[2048,5632]{1,0:T(8,128)(2,1)}) %all-gather.20.cloned.1.call-update) | async-done | bytes 23068688 | tf_op jit(solution)/shard_map/all_gather | solution.py:184
  645.4 12.3 fusion.94
  657.7 133.4 %all-gather.22.cloned.1.call-done = bf16[5632,2048]{1,0:T(8,128)(2,1)} async-done(((bf16[176,2048]{1,0:T(8,128)(2,1)}), bf16[5632,2048]{1,0:T(8,128)(2,1)}) %all-gather.22.cloned.1.call-update) | async-done | bytes 23068688 | tf_op jit(solution)/shard_map/all_gather | solution.py:185
  791.1 14.5 multiply_convert_fusion.6
  805.6 24.1 fusion.95
  829.8 13.2 multiply_reduce_fusion
  866.1 19.1 while.56
  866.8 17.8 conditional.10
  887.2 34.6 %all_gather.79 = bf16[1024,32]{0,1:T(8,128)(2,1)S(1)} all-gather(bf16[128,32]{0,1:T(8,128)(2,1)S(1)} %convert_element_type.222), channel_id=1, replica_groups=mesh['rows'=4,'blk'=8] {'blk'}, dimensions={0}, use_global_device_ids=true | all-gather | bytes 73728 | tf_op jit(solution)/shard_map/all_gather | solution.py:307
  921.8 14.6 all_gather.77
  948.8 51.2 %while.57 = (s32[]{:T(128)}, f32[128,32,64]{0,2,1:T(8,128)}, f32[128,32,64]{0,2,1:T(8,128)}, s32[]{:T(128)}, bf16[1024,2048]{0,1:T(8,128)(2,1)}, /*index=5*/s32[...) while((s32[]{:T(128)}, f32[128,32,64]{0,2,1:T(8,128)}, ...), condition=%wide.region_21.22_spmd.clone, body=%wide.region_18.0_spmd.clone.sunk | while | flops 1097532032 | bytes 47854520 | solution.py:378
  949.5 24.9 conditional.11
  975.0 25.0 conditional.11
  1005.1 21.4 fusion.81
  1028.1 18.5 fusion.96
  1048.0 18.4 fusion.97
  1067.9 18.3 fusion.72
  1087.5 11.9 fusion.58
  1099.9 14.4 fusion.86
  1116.1 39.1 %all-reduce.10 = (f32[2048]{0:T(1024)S(1)}, f32[2048]{0:T(1024)S(1)}, f32[6144]{0:T(1024)S(1)}, f32[2048]{0:T(1024)S(1)}, f32[2048]{0:T(1024)S(1)}) all-reduce(f32[2048]{0:T(1024)S(1)} %get-tuple-element.1188, f32[2048]{0:T(1024)S(1)} %get-tuple-element.1191, ...), channel_id=2, replica_groups=mesh['rows'=4,'blk'=8] {'rows','blk'}, use_global_device_ids=true, to_apply=%region_25.26.clone | all-reduce | flops 14336 | bytes 114688
  1161.1 409.3 %reduce-scatter.6.cloned.1.call-done = f32[64,6144]{1,0:T(8,128)} async-done(((f32[2048,6144]{1,0:T(8,128)}), f32[64,6144]{1,0:T(8,128)}) %reduce-scatter.6.cloned.1.call-update) | async-done | bytes 1572880 | tf_op jit(solution)/shard_map/reduce_scatter | solution.py:406
  1570.4 493.7 %reduce-scatter.10.cloned.1.call-done = f32[64,5632]{1,0:T(8,128)} async-done(((f32[2048,5632]{1,0:T(8,128)}), f32[64,5632]{1,0:T(8,128)}) %reduce-scatter.10.cloned.1.call-update) | async-done | bytes 1441808 | tf_op jit(solution)/shard_map/reduce_scatter | solution.py:225
  2064.0 491.3 %reduce-scatter.12.cloned.1.call-done = f32[64,5632]{1,0:T(8,128)} async-done(((f32[2048,5632]{1,0:T(8,128)}), f32[64,5632]{1,0:T(8,128)}) %reduce-scatter.12.cloned.1.call-update) | async-done | bytes 1441808 | tf_op jit(solution)/shard_map/reduce_scatter | solution.py:226
  2555.3 491.2 %reduce-scatter.14.cloned.1.call-done = f32[176,2048]{1,0:T(8,128)} async-done(((f32[5632,2048]{1,0:T(8,128)}), f32[176,2048]{1,0:T(8,128)}) %reduce-scatter.14.cloned.1.call-update) | async-done | bytes 1441808 | tf_op jit(solution)/shard_map/reduce_scatter | solution.py:227
  (248 shorter events, 201.5 us)
Async XLA Ops:
  7.2 162.7 %all-gather.10.cloned.1.call-start = ((), (), s32[]{:S(2)}) async-start(), calls=%async_computation.5 | async-start | bytes 25952256 | tf_op jit(solution)/shard_map/all_gather | solution.py:122
  7.9 218.7 %all-gather.14.cloned.1.call-start = ((), (), s32[]{:S(2)}) async-start(), calls=%async_computation.7 | async-start | bytes 4718592 | tf_op jit(solution)/shard_map/all_gather | solution.py:134
  55.7 124.5 %copy-start.29 = (f32[2048]{0:T(1024)}, f32[2048]{0:T(1024)S(1)}, u32[]{:S(2)}) copy-start(f32[2048]{0:T(1024)S(1)} %convert_element_type.193) | copy-start | bytes 24580
  55.7 124.5 %copy-start.32 = (f32[2048]{0:T(1024)}, f32[2048]{0:T(1024)S(1)}, u32[]{:S(2)}) copy-start(f32[2048]{0:T(1024)S(1)} %convert_element_type.194) | copy-start | bytes 24580
  56.9 123.3 %copy-start.35 = (f32[128]{0:T(128)}, f32[128]{0:T(128)S(1)}, u32[]{:S(2)}) copy-start(f32[128]{0:T(128)S(1)} %broadcast_multiply_fusion.1) | copy-start | bytes 1540
  58.3 121.9 %copy-start.43 = (f32[128]{0:T(128)}, f32[128]{0:T(128)S(1)}, u32[]{:S(2)}) copy-start(f32[128]{0:T(128)S(1)} %fusion.69) | copy-start | bytes 1540
  58.3 121.9 %copy-start.37 = (f32[128]{0:T(128)}, f32[128]{0:T(128)S(1)}, u32[]{:S(2)}) copy-start(f32[128]{0:T(128)S(1)} %fusion.79) | copy-start | bytes 1540
  58.3 122.9 %copy-start.34 = (s32[1,128]{1,0:T(1,128)S(1)}, s32[1,128]{1,0:T(1,128)}, u32[]{:S(2)}) copy-start(s32[1,128]{1,0:T(1,128)} %param.26) | copy-start | bytes 1540
  181.1 94.2 %all-gather.12.cloned.1.call-start = ((), (), s32[]{:S(2)}) async-start(), calls=%async_computation.6 | async-start | bytes 4718592 | tf_op jit(solution)/shard_map/all_gather | solution.py:133
  197.5 156.4 %all-gather.16.cloned.1.call-start = ((), (), s32[]{:S(2)}) async-start(), calls=%async_computation.8 | async-start | bytes 8650752 | tf_op jit(solution)/shard_map/all_gather | solution.py:124
  198.1 301.8 %all-gather.18.cloned.1.call-start = ((), (), s32[]{:S(2)}) async-start(), calls=%async_computation.9 | async-start | bytes 23789568 | tf_op jit(solution)/shard_map/all_gather | solution.py:183
  198.6 446.7 %all-gather.20.cloned.1.call-start = ((), (), s32[]{:S(2)}) async-start(), calls=%async_computation.10 | async-start | bytes 23789568 | tf_op jit(solution)/shard_map/all_gather | solution.py:184
  199.2 591.9 %all-gather.22.cloned.1.call-start = ((), (), s32[]{:S(2)}) async-start(), calls=%async_computation.11 | async-start | bytes 23789568 | tf_op jit(solution)/shard_map/all_gather | solution.py:185
  200.0 736.5 %all-gather.26.cloned.1.call-start = ((), (), s32[]{:S(2)}) async-start(), calls=%async_computation.13 | async-start | bytes 4718592 | tf_op jit(solution)/shard_map/all_gather | solution.py:301
  289.9 69.1 %copy-start = (bf16[128,32,64]{0,2,1:T(8,128)(2,1)}, bf16[128,32,64]{0,2,1:T(8,128)(2,1)S(1)}, u32[]{:S(2)}) copy-start(bf16[128,32,64]{0,2,1:T(8,128)(2,1)S(1)} %get-tuple-element.1724) | copy-start | bytes 1572868
  289.9 64.0 %copy-start.4 = (bf16[1,128,2048]{2,1,0:T(8,128)(2,1)S(1)}, bf16[1,128,2048]{2,1,0:T(8,128)(2,1)}, u32[]{:S(2)}) copy-start(bf16[1,128,2048]{2,1,0:T(8,128)(2,1)} %param.25) | copy-start | bytes 1572868
  358.9 484.0 %copy-start.2 = (f32[128,2048]{1,0:T(8,128)}, f32[128,2048]{1,0:T(8,128)S(1)}, u32[]{:S(2)}) copy-start(f32[128,2048]{1,0:T(8,128)S(1)} %get-tuple-element.1319) | copy-start | bytes 3145732
  359.5 285.9 %copy-start.9 = (bf16[128,2048]{1,0:T(8,128)(2,1)}, bf16[128,2048]{1,0:T(8,128)(2,1)S(1)}, u32[]{:S(2)}) copy-start(bf16[128,2048]{1,0:T(8,128)(2,1)S(1)} %add_convert_fusion) | copy-start | bytes 1572868
  512.1 279.0 %copy-start.22 = (bf16[1,128,2048]{2,1,0:T(8,128)(2,1)S(1)}, bf16[1,128,2048]{2,1,0:T(8,128)(2,1)}, u32[]{:S(2)}) copy-start(bf16[1,128,2048]{2,1,0:T(8,128)(2,1)} %param.27) | copy-start | bytes 1572868
  805.6 24.1 copy-start.11
  805.6 24.1 copy-start.13
  852.1 94.5 %all-gather.24.cloned.1.call-start = ((), (), s32[]{:S(2)}) async-start(), calls=%async_computation.12 | async-start | bytes 4718592 | tf_op jit(solution)/shard_map/all_gather | solution.py:298
  852.8 308.3 %reduce-scatter.8.cloned.1.call-start = ((), (), s32[]{:S(2)}) async-start(), calls=%async_computation.15 | async-start | bytes 17301504 | tf_op jit(solution)/shard_map/reduce_scatter | solution.py:408
  861.5 708.9 %reduce-scatter.6.cloned.1.call-start = ((), (), s32[]{:S(2)}) async-start(), calls=%async_computation.14 | async-start | bytes 51904512 | tf_op jit(solution)/shard_map/reduce_scatter | solution.py:406
  1004.9 21.5 copy-start.18
  1005.0 21.5 copy-start.20
  1026.5 1037.5 %reduce-scatter.10.cloned.1.call-start = ((), (), s32[]{:S(2)}) async-start(), calls=%async_computation.16 | async-start | bytes 47579136 | tf_op jit(solution)/shard_map/reduce_scatter | solution.py:225
  1046.6 1508.7 %reduce-scatter.12.cloned.1.call-start = ((), (), s32[]{:S(2)}) async-start(), calls=%async_computation.17 | async-start | bytes 47579136 | tf_op jit(solution)/shard_map/reduce_scatter | solution.py:226
  1066.4 1980.1 %reduce-scatter.14.cloned.1.call-start = ((), (), s32[]{:S(2)}) async-start(), calls=%async_computation.18 | async-start | bytes 47579136 | tf_op jit(solution)/shard_map/reduce_scatter | solution.py:227
  1099.9 58.4 %copy-start.16 = (f32[128,2048]{1,0:T(8,128)S(1)}, f32[128,2048]{1,0:T(8,128)}, u32[]{:S(2)}) copy-start(f32[128,2048]{1,0:T(8,128)} %copy-done.15) | copy-start | bytes 3145732
  1099.9 58.4 %copy-start.24 = (bf16[1,128,2048]{2,1,0:T(8,128)(2,1)S(1)}, bf16[1,128,2048]{2,1,0:T(8,128)(2,1)}, u32[]{:S(2)}) copy-start(bf16[1,128,2048]{2,1,0:T(8,128)(2,1)} %param.27) | copy-start | bytes 1572868
  1099.9 58.4 %copy-start.42 = (f32[128]{0:T(128)S(1)}, f32[128]{0:T(128)}, u32[]{:S(2)}) copy-start(f32[128]{0:T(128)} %copy-done.41) | copy-start | bytes 1540
  (27 other events, 152.6 us)
Sparse Core Ops, SparseCore 0:
  11.0 158.8 all-gather.9
  181.2 45.3 all-gather.13
  228.8 46.5 all-gather.11
  278.2 75.6 all-gather.15
  356.6 143.2 all-gather.17
  502.5 142.8 all-gather.19
  648.2 142.7 all-gather.21
  852.2 45.3 all-gather.25
  899.2 47.4 all-gather.23
  949.3 184.7 reduce-scatter.7
  1141.2 429.1 reduce-scatter.5
  1573.1 490.8 reduce-scatter.9
  2066.9 488.4 reduce-scatter.11
  2558.1 488.4 reduce-scatter.13
where the time goes:
time: 3050 us
  waiting for transfers between devices  2540 us (83%)
  matrix products  273 us (9%)
  blocking collectives  142 us (5%)
  local copies, waits for them, and re-layouts  59.7 us (2%)
    reduce_scatter x1, waiting for transfers between devices, body(): lax.psum_scatter(gate_grad, ('rows', 'blk'), scatter_dimension=0, tiled=T...  494 us
    reduce_scatter x1, waiting for transfers between devices, body(): lax.psum_scatter(up_grad, ('rows', 'blk'), scatter_dimension=0, tiled=True)  491 us
    reduce_scatter x1, waiting for transfers between devices, body(): lax.psum_scatter(down_grad, ('rows', 'blk'), scatter_dimension=0, tiled=T...  491 us
    reduce_scatter x1, waiting for transfers between devices, body(): lax.psum_scatter(project_grad, ('rows', 'blk'), scatter_dimension=0, tile...  409 us
    all_gather x1, waiting for transfers between devices, body(): lax.all_gather(gate_weight, ('rows', 'blk'), axis=0, tiled=True)  140 us
    all_gather x1, waiting for transfers between devices, body(): lax.all_gather(down_weight, ('rows', 'blk'), axis=0, tiled=True)  133 us
    all_gather x1, waiting for transfers between devices, body(): lax.all_gather(up_weight, ('rows', 'blk'), axis=0, tiled=True)  133 us
    all_gather x1, waiting for transfers between devices, body(): lax.all_gather(project_weight, ('rows', 'blk'), axis=0, tiled=True)  112 us
  transfers between devices with their start and end apart: 14, of which 12 were waited for; matrix products, arithmetic and copies ran while one was open for 9% of the time, Pallas kernels for 0%

commit v1 on v0

v1 whole, which is shorter than its diff:
```python
import math

import jax
import jax.numpy as jnp
from jax import lax
from jax.sharding import PartitionSpec as P

HEADS = 32
ROT = 16
BOTH = ("rows", "blk")

epsilon = 1e-05
rotary_base = 10000.0
masked_value = -1e30


def dot(left, right, contract):
    return lax.dot_general(
        left, right, (contract, ((), ())), preferred_element_type=jnp.float32
    )


def norm_stats(inputs):
    row_mean = jnp.mean(inputs, axis=-1, keepdims=True)
    centered = inputs - row_mean
    variance = jnp.mean(centered * centered, axis=-1, keepdims=True)
    inverse = lax.rsqrt(variance + epsilon)
    return centered * inverse, inverse


def norm_back(incoming, unit, inverse, gain):
    gain_part = jnp.sum(incoming * unit, axis=0)
    shift_part = jnp.sum(incoming, axis=0)
    unit_grad = incoming * gain
    grad = inverse * (
        unit_grad
        - jnp.mean(unit_grad, axis=-1, keepdims=True)
        - unit * jnp.mean(unit_grad * unit, axis=-1, keepdims=True)
    )
    return grad, gain_part, shift_part


def rotate(columns, cosine, sine, head_width):
    half = cosine.shape[1]
    heads = columns.reshape(columns.shape[0], -1, head_width)
    cosine, sine = cosine[:, None, :], sine[:, None, :]
    first, second, rest = heads[..., :half], heads[..., half : 2 * half], heads[..., 2 * half :]
    return jnp.concatenate(
        [first * cosine - second * sine, second * cosine + first * sine, rest], axis=-1
    ).reshape(columns.shape)


def gather_blk(rows):
    return lax.all_gather(rows, "blk", axis=0, tiled=True)


def scatter_blk(partial):
    return lax.psum_scatter(
        partial.astype(jnp.bfloat16), "blk", scatter_dimension=0, tiled=True
    ).astype(jnp.float32)


def gather_rows(shard):
    return lax.all_gather(shard, "rows", axis=0, tiled=True)


def scatter_rows(partial):
    return lax.psum_scatter(
        partial.astype(jnp.bfloat16), "rows", scatter_dimension=0, tiled=True
    )


def exchange_blk(pieces):
    return lax.all_to_all(pieces, "blk", split_axis=0, concat_axis=0, tiled=True)


def make_body(group, ranks):
    def columns_of(shard, parts, inner):
        depth = shard.shape[0]
        pieces = shard.reshape(depth, parts, ranks, inner).transpose(2, 0, 1, 3)
        pieces = exchange_blk(pieces.reshape(ranks, depth, parts * inner))
        return gather_rows(pieces.reshape(ranks * depth, parts * inner))

    def columns_back(grad, parts, inner):
        owned = scatter_rows(grad)
        depth = owned.shape[0] // ranks
        pieces = exchange_blk(owned.reshape(ranks, depth, parts * inner))
        pieces = pieces.reshape(ranks, depth, parts, inner).transpose(1, 2, 0, 3)
        return pieces.reshape(depth, parts * ranks * inner).astype(jnp.float32)

    def body(
        tokens,
        segments,
        cotangent,
        attend_gain,
        attend_shift,
        project_weight,
        project_bias,
        output_weight,
        feed_gain,
        feed_shift,
        gate_weight,
        up_weight,
        down_weight,
    ):
        own_rows, width = tokens.shape[1], tokens.shape[2]
        length = own_rows * ranks
        head_width = width // HEADS
        local_heads = HEADS // ranks
        local_width = local_heads * head_width
        score_scale = 1.0 / math.sqrt(head_width)
        hidden_shard = down_weight.shape[0]
        shard = attend_gain.shape[0]
        me = lax.axis_index("blk")

        packed = jnp.concatenate(
            [
                attend_gain,
                attend_shift,
                feed_gain,
                feed_shift,
                project_bias,
                segments[0].astype(jnp.bfloat16),
            ]
        )
        packed = lax.all_gather(packed, BOTH, axis=0, tiled=False)
        a_gain = packed[:, :shard].reshape(-1).astype(jnp.float32)
        a_shift = packed[:, shard : 2 * shard].reshape(-1).astype(jnp.float32)
        f_gain = packed[:, 2 * shard : 3 * shard].reshape(-1).astype(jnp.float32)
        f_shift = packed[:, 3 * shard : 4 * shard].reshape(-1).astype(jnp.float32)
        bias = packed[:, 4 * shard : 7 * shard].reshape(3, ranks, local_width)
        bias = lax.dynamic_index_in_dim(bias, me, 1, False).reshape(-1).astype(jnp.float32)
        doc = packed[:, 7 * shard :].reshape(group, ranks * own_rows)
        doc = lax.dynamic_index_in_dim(doc, lax.axis_index("rows"), 0, False)

        w_project = columns_of(project_weight, 3, local_width)
        w_gate = columns_of(gate_weight, group, hidden_shard)
        w_up = columns_of(up_weight, group, hidden_shard)
        w_down = gather_rows(down_weight)
        w_out = lax.all_gather(output_weight, BOTH, axis=0, tiled=True)

        doc = doc.astype(jnp.int32)
        index = jnp.arange(length, dtype=jnp.int32)
        places = index - jnp.sum((doc[None, :] < doc[:, None]).astype(jnp.int32), axis=1)
        half = ROT // 2
        frequency = jnp.power(
            rotary_base, -jnp.arange(half, dtype=jnp.int32).astype(jnp.float32) / half
        )
        angles = places.astype(jnp.float32)[:, None] * frequency
        cosine, sine = jnp.cos(angles), jnp.sin(angles)
        mask = ((index[None, :] <= index[:, None]) & (doc[None, :] == doc[:, None]))[None]

        inputs = tokens[0].astype(jnp.float32)
        unit_first, inverse_first = norm_stats(inputs)
        normed_first = gather_blk((unit_first * a_gain + a_shift).astype(jnp.bfloat16))
        grad_out = gather_blk(cotangent[0])
        mixed = dot(normed_first, w_project, ((1,), (0,))) + bias
        queries = rotate(mixed[:, :local_width], cosine, sine, head_width).astype(jnp.bfloat16)
        keys = rotate(mixed[:, local_width : 2 * local_width], cosine, sine, head_width)
        keys = keys.astype(jnp.bfloat16)
        values = mixed[:, 2 * local_width :].astype(jnp.bfloat16)
        q_heads = queries.reshape(length, local_heads, head_width)
        k_heads = keys.reshape(length, local_heads, head_width)
        v_heads = values.reshape(length, local_heads, head_width)
        scores = jnp.einsum("qhd,khd->hqk", q_heads, k_heads, preferred_element_type=jnp.float32)
        scores = jnp.where(mask, scores * score_scale, masked_value)
        top = jnp.max(scores, axis=2, keepdims=True)
        weights = jnp.where(mask, jnp.exp(scores - top), 0.0)
        total = jnp.sum(weights, axis=2, keepdims=True)
        attended = jnp.einsum(
            "hqk,khd->qhd",
            weights.astype(jnp.bfloat16),
            v_heads,
            preferred_element_type=jnp.float32,
        ) / jnp.transpose(total[:, :, 0])[:, :, None]
        log_total = top + jnp.log(total)
        attended_flat = attended.reshape(length, local_width)
        attended_low = exchange_blk(
            attended_flat.astype(jnp.bfloat16).reshape(ranks, own_rows, local_width)
        )
        attended_low = attended_low.transpose(1, 0, 2).reshape(own_rows, width)
        resid_mid = inputs + dot(attended_low, w_out, ((1,), (0,)))

        unit_second, inverse_second = norm_stats(resid_mid)
        normed_second = gather_blk((unit_second * f_gain + f_shift).astype(jnp.bfloat16))
        gate_value = dot(normed_second, w_gate, ((1,), (0,)))
        up_value = dot(normed_second, w_up, ((1,), (0,)))
        gate_sigmoid = jax.nn.sigmoid(gate_value)
        silu = gate_value * gate_sigmoid
        hidden = (silu * up_value).astype(jnp.bfloat16)
        output = (resid_mid + scatter_blk(dot(hidden, w_down, ((1,), (0,))))).astype(jnp.bfloat16)

        grad_hidden = dot(grad_out, w_down, ((1,), (1,)))
        grad_gate = (
            grad_hidden * up_value * gate_sigmoid * (1.0 + gate_value * (1.0 - gate_sigmoid))
        ).astype(jnp.bfloat16)
        grad_up = (grad_hidden * silu).astype(jnp.bfloat16)
        grad_second = scatter_blk(
            dot(grad_gate, w_gate, ((1,), (1,))) + dot(grad_up, w_up, ((1,), (1,)))
        )
        down_grad = scatter_rows(dot(hidden, grad_out, ((0,), (0,)))).astype(jnp.float32)
        gate_grad = columns_back(dot(normed_second, grad_gate, ((0,), (0,))), group, hidden_shard)
        up_grad = columns_back(dot(normed_second, grad_up, ((0,), (0,))), group, hidden_shard)
        mid_part, f_gain_part, f_shift_part = norm_back(
            grad_second, unit_second, inverse_second, f_gain
        )
        grad_mid = cotangent[0].astype(jnp.float32) + mid_part
        grad_mid_low = grad_mid.astype(jnp.bfloat16)
        grad_attended = dot(grad_mid_low, w_out, ((1,), (1,))).astype(jnp.bfloat16)
        grad_attended = exchange_blk(
            grad_attended.reshape(own_rows, ranks, local_width).transpose(1, 0, 2)
        ).reshape(length, local_width)
        out_grad = lax.psum_scatter(
            dot(attended_low, grad_mid_low, ((0,), (0,))).astype(jnp.bfloat16),
            BOTH,
            scatter_dimension=0,
            tiled=True,
        ).astype(jnp.float32)

        g_heads = grad_attended.reshape(length, local_heads, head_width)
        delta = jnp.transpose(jnp.sum(g_heads.astype(jnp.float32) * attended, axis=2))
        probs = jnp.where(mask, jnp.exp(scores - log_total), 0.0)
        values_grad = jnp.einsum(
            "hqk,qhd->khd", probs.astype(jnp.bfloat16), g_heads, preferred_element_type=jnp.float32
        )
        grad_probs = jnp.einsum("qhd,khd->hqk", g_heads, v_heads, preferred_element_type=jnp.float32)
        grad_scores = (probs * (grad_probs - delta[:, :, None]) * score_scale).astype(jnp.bfloat16)
        grad_queries = jnp.einsum(
            "hqk,khd->qhd", grad_scores, k_heads, preferred_element_type=jnp.float32
        )
        keys_grad = jnp.einsum(
            "hqk,qhd->khd", grad_scores, q_heads, preferred_element_type=jnp.float32
        )
        grad_mixed = jnp.concatenate(
            [
                rotate(grad_queries.reshape(length, local_width), cosine, -sine, head_width),
                rotate(keys_grad.reshape(length, local_width), cosine, -sine, head_width),
                values_grad.reshape(length, local_width),
            ],
            axis=1,
        ).astype(jnp.bfloat16)
        grad_first = scatter_blk(dot(grad_mixed, w_project, ((1,), (1,))))
        project_grad = columns_back(
            dot(normed_first, grad_mixed, ((0,), (0,))), 3, local_width
        )
        bias_part = jnp.sum(grad_mixed.astype(jnp.float32), axis=0).reshape(3, 1, local_width)
        bias_part = jnp.where(jnp.arange(ranks)[None, :, None] == me, bias_part, 0.0)
        input_part, a_gain_part, a_shift_part = norm_back(
            grad_first, unit_first, inverse_first, a_gain
        )
        grad_tokens = grad_mid + input_part
        vectors = jnp.concatenate(
            [
                a_gain_part.reshape(-1, shard),
                a_shift_part.reshape(-1, shard),
                f_gain_part.reshape(-1, shard),
                f_shift_part.reshape(-1, shard),
                bias_part.reshape(-1, 3 * shard),
            ],
            axis=1,
        )
        vectors = lax.psum_scatter(vectors, BOTH, scatter_dimension=0, tiled=True)[0]
        return (
            output[None],
            grad_tokens[None],
            vectors[:shard],
            vectors[shard : 2 * shard],
            project_grad,
            vectors[4 * shard :],
            out_grad,
            vectors[2 * shard : 3 * shard],
            vectors[3 * shard : 4 * shard],
            gate_grad,
            up_grad,
            down_grad,
        )

    return body


def solution(mesh):
    tokens = P("rows", "blk", None)
    vector, matrix = P(BOTH), P(BOTH, None)
    in_specs = (
        tokens, P("rows", "blk"), tokens, vector, vector, matrix, vector, matrix, vector, vector,
        matrix, matrix, matrix,
    )
    out_specs = (
        tokens, tokens, vector, vector, matrix, vector, matrix, vector, vector, matrix, matrix, matrix,
    )
    body = make_body(mesh.shape["rows"], mesh.shape["blk"])
    return jax.shard_map(body, mesh=mesh, in_specs=in_specs, out_specs=out_specs, check_vma=False)
```

time: 3050 us -> 974 us (0.32)
  waiting for transfers between devices: 2540 us -> 546 us
  matrix products: 273 us -> 138 us
    reduce_scatter x5 -> x8, waiting for transfers between devices: 1890 us -> 247 us  [the longest x1 107 us: body(): lax.psum_scatter(dot(attended_low, grad_mid_low, ((0,), (0,))).astype(jnp...]
    all_gather x9 -> x8, waiting for transfers between devices: 651 us -> 216 us  [the longest x3 116 us: gather_blk(): return lax.all_gather(rows, 'blk', axis=0, tiled=True)]
    dot_general x25 -> x21, matrix products: 273 us -> 138 us  [the longest x15 100 us: dot(): lax.dot_general(left, right, (contract, ((), ())), preferred_element_type...]
    all_to_all x0 -> x5, waiting for transfers between devices: none -> 80.6 us  [exchange_blk(): lax.all_to_all(pieces, 'blk', split_axis=0, concat_axis=0, tiled=True)]
    all_to_all x0 -> x3, blocking collectives: none -> 76.6 us  [exchange_blk(): lax.all_to_all(pieces, 'blk', split_axis=0, concat_axis=0, tiled=True)]
    all_gather x3 -> x0, blocking collectives: 58.9 us -> none  [the longest x1 34.6 us: body(): lax.all_gather(jnp.transpose(row_delta).astype(jnp.bfloat16), 'blk', axis...]
  transfers between devices with their start and end apart: 14 -> 21, of which waited for: 12 -> 16; matrix products, arithmetic and copies ran while one was open for 9% -> 21% of each run, Pallas kernels for 0% -> 0%
where the time goes in v1:
time: 974 us; the launch traced here: 967 us
  waiting for transfers between devices  546 us (56%)
  blocking collectives  154 us (16%)
  matrix products  138 us (14%)
  local copies, waits for them, and re-layouts  60.3 us (6%)
  other arithmetic  32 us (3%)
  starting transfers between devices  21.3 us (2%)
  between operations  15.1 us (2%)
    all_gather x3, waiting for transfers between devices, gather_blk(): return lax.all_gather(rows, 'blk', axis=0, tiled=True)  116 us
    reduce_scatter x1, waiting for transfers between devices, body(): lax.psum_scatter(dot(attended_low, grad_mid_low, ((0,), (0,))).astype(jnp...  107 us
    reduce_scatter x3, waiting for transfers between devices, scatter_blk(): lax.psum_scatter(partial.astype(jnp.bfloat16), 'blk', scatter_dimension=0...  101 us
    dot_general x15, matrix products, dot(): lax.dot_general(left, right, (contract, ((), ())), preferred_element_type...  100 us
    all_to_all x5, waiting for transfers between devices, exchange_blk(): lax.all_to_all(pieces, 'blk', split_axis=0, concat_axis=0, tiled=True)  80.6 us
    unnamed x2, blocking collectives  77.9 us
    all_gather x4, waiting for transfers between devices, gather_rows(): return lax.all_gather(shard, 'rows', axis=0, tiled=True)  77.6 us
    all_to_all x3, blocking collectives, exchange_blk(): lax.all_to_all(pieces, 'blk', split_axis=0, concat_axis=0, tiled=True)  76.6 us
  transfers between devices with their start and end apart: 21, of which 16 were waited for; matrix products, arithmetic and copies ran while one was open for 21% of the time, Pallas kernels for 0%

profile of v1, /device:TPU:0, one launch (start us, length us, event | category | flops | bytes accessed | tf_op | source)
XLA Modules:
  0.0 967.4 jit_solution(10527571184016358756)
XLA Ops:
  10.0 27.3 %all_to_all.40 = bf16[8,64,768]{2,1,0:T(8,128)(2,1)} all-to-all(bf16[8,64,768]{2,1,0:T(8,128)(2,1)S(1)} %reshape.377), channel_id=1, replica_groups=mesh['rows'=4,'blk'=8] {'blk'}, dimensions={0} | all-to-all | bytes 1572864 | tf_op jit(solution)/shard_map/all_to_all | solution.py:74
  37.8 39.0 %all-reduce = bf16[18432]{0:T(1024)(128)(2,1)S(1)} all-reduce(bf16[18432]{0:T(1024)(128)(2,1)S(1)} %dynamic-update-slice), channel_id=2, replica_groups=mesh['rows'=4,'blk'=8] {'rows','blk'}, use_global_device_ids=true, to_apply=%add | all-reduce | flops 18432 | bytes 73728
  90.1 35.1 %all-to-all-done.3 = bf16[8,64,704]{2,1,0:T(8,128)(2,1)S(1)} async-done(((bf16[8,64,704]{2,1,0:T(8,128)(2,1)}), bf16[8,64,704]{2,1,0:T(8,128)(2,1)S(1)}, u32[]{:S(2)}, u32[]{:S(2)}) %all-to-all-start.3) | async-done | bytes 720928 | tf_op jit(solution)/shard_map/all_to_all | solution.py:74
  126.2 18.0 %all-gather.11.cloned.1.call-done = bf16[1024,2048]{1,0:T(8,128)(2,1)} async-done(((bf16[128,2048]{1,0:T(8,128)(2,1)}), bf16[1024,2048]{1,0:T(8,128)(2,1)}) %all-gather.11.cloned.1.call-update) | async-done | bytes 4194320 | tf_op jit(solution)/shard_map/all_gather | solution.py:54
  152.1 7.4 fusion.62
  159.6 8.8 fusion
  169.8 8.9 fusion.63
  183.8 19.8 %all-to-all-done.1 = bf16[8,128,256]{1,2,0:T(8,128)(2,1)S(1)} async-done(((bf16[8,128,256]{1,2,0:T(8,128)(2,1)}), bf16[8,128,256]{1,2,0:T(8,128)(2,1)S(1)}, u32[]{:S(2)}, u32[]{:S(2)}) %all-to-all-start.1) | async-done | bytes 524320 | tf_op jit(solution)/shard_map/all_to_all | solution.py:74
  203.6 22.9 %all-gather.15.cloned.1.call-done = bf16[2048,2048]{1,0:T(8,128)(2,1)} async-done(((bf16[64,2048]{1,0:T(8,128)(2,1)}), bf16[2048,2048]{1,0:T(8,128)(2,1)}) %all-gather.15.cloned.1.call-update) | async-done | bytes 8388624 | tf_op jit(solution)/shard_map/all_gather | solution.py:140
  239.2 25.2 %all_to_all.41 = bf16[8,64,704]{2,1,0:T(8,128)(2,1)} all-to-all(bf16[8,64,704]{2,1,0:T(8,128)(2,1)} %reshape.386), channel_id=1, replica_groups=mesh['rows'=4,'blk'=8] {'blk'}, dimensions={0} | all-to-all | bytes 1441792 | tf_op jit(solution)/shard_map/all_to_all | solution.py:74
  271.3 49.2 %all-gather.17.cloned.1.call-done = bf16[1024,2048]{1,0:T(8,128)(2,1)} async-done(((bf16[128,2048]{1,0:T(8,128)(2,1)}), bf16[1024,2048]{1,0:T(8,128)(2,1)}) %all-gather.17.cloned.1.call-update) | async-done | bytes 4194320 | tf_op jit(solution)/shard_map/all_gather | solution.py:54
  320.5 7.9 fusion.66
  328.5 36.5 %all-gather.19.cloned.1.call-done = bf16[2048,704]{1,0:T(8,128)(2,1)} async-done(((bf16[512,704]{1,0:T(8,128)(2,1)}), bf16[2048,704]{1,0:T(8,128)(2,1)}) %all-gather.19.cloned.1.call-update) | async-done | bytes 2883600 | tf_op jit(solution)/shard_map/all_gather | solution.py:64
  364.9 7.9 fusion.65
  372.9 35.7 %all-gather.23.cloned.1.call-done = bf16[704,2048]{1,0:T(8,128)(2,1)} async-done(((bf16[176,2048]{1,0:T(8,128)(2,1)}), bf16[704,2048]{1,0:T(8,128)(2,1)}) %all-gather.23.cloned.1.call-update) | async-done | bytes 2883600 | tf_op jit(solution)/shard_map/all_gather | solution.py:64
  408.6 48.8 %all-gather.25.cloned.1.call-done = bf16[1,1024,2048]{2,1,0:T(8,128)(2,1)} async-done(((bf16[1,128,2048]{2,1,0:T(8,128)(2,1)}), bf16[1,1024,2048]{2,1,0:T(8,128)(2,1)}) %all-gather.25.cloned.1.call-update) | async-done | bytes 4194320 | tf_op jit(solution)/shard_map/all_gather | solution.py:54
  457.4 10.1 %multiply_convert_fusion.1 = (bf16[1024,704]{0,1:T(8,128)(2,1)S(1)}, bf16[1024,704]{0,1:T(8,128)(2,1)S(1)}, bf16[1024,704]{0,1:T(8,128)(2,1)}) fusion(f32[1024,704]{0,1:T(8,128)} %fusion.65, f32[1024,704]{0,1:T(8,128)} %fusion.66, bf16[704,2048]{1,0:T(8,128)(2,1)} %all-gather.23.cloned.1.call-done, bf16[1,1024,2048]{2,1,0:T(8,128)(2,1)} %all-gather.25.cloned.1.call-done), kind=kOutput, calls=%fused_computation.27 | convolution fusion | flops 2963603456 | bytes 17170432 | tf_op jit(solution)/shard_map/dot_general | solution.py:18
  476.5 7.7 convolution_convert_fusion.1
  484.3 7.3 convolution_convert_fusion.4
  491.6 33.7 %reduce-scatter.11.cloned.1.call-done = bf16[128,2048]{1,0:T(8,128)(2,1)} async-done(((bf16[1024,2048]{1,0:T(8,128)(2,1)}), bf16[128,2048]{1,0:T(8,128)(2,1)}) %reduce-scatter.11.cloned.1.call-update) | async-done | bytes 524304 | tf_op jit(solution)/shard_map/reduce_scatter | solution.py:58
  528.0 47.7 %reduce-scatter.9.cloned.1.call-done = bf16[128,2048]{1,0:T(8,128)(2,1)} async-done(((bf16[1024,2048]{1,0:T(8,128)(2,1)}), bf16[128,2048]{1,0:T(8,128)(2,1)}) %reduce-scatter.9.cloned.1.call-update) | async-done | bytes 524304 | tf_op jit(solution)/shard_map/reduce_scatter | solution.py:58
  590.1 7.5 convolution_convert_fusion.5
  611.1 9.5 multiply_convert_fusion
  626.0 8.2 fusion.28
  640.5 7.4 fusion.14
  648.0 7.5 convolution_convert_fusion.2
  669.1 19.6 %all-to-all-done.7 = bf16[8,64,704]{2,1,0:T(8,128)(2,1)} async-done(((bf16[8,64,704]{2,1,0:T(8,128)(2,1)}), bf16[8,64,704]{2,1,0:T(8,128)(2,1)}, u32[]{:S(2)}, u32[]{:S(2)}) %all-to-all-start.7) | async-done | bytes 720928 | tf_op jit(solution)/shard_map/all_to_all | solution.py:74
  688.7 24.1 %all_to_all.42 = bf16[8,64,704]{2,1,0:T(8,128)(2,1)} all-to-all(bf16[8,64,704]{2,1,0:T(8,128)(2,1)S(1)} %bitcast.166), channel_id=1, replica_groups=mesh['rows'=4,'blk'=8] {'blk'}, dimensions={0} | all-to-all | bytes 1441792 | tf_op jit(solution)/shard_map/all_to_all | solution.py:74
  716.5 38.5 %reduce-scatter.23.cloned.1.call-done = bf16[176,2048]{1,0:T(8,128)(2,1)} async-done(((bf16[704,2048]{1,0:T(8,128)(2,1)}), bf16[176,2048]{1,0:T(8,128)(2,1)}) %reduce-scatter.23.cloned.1.call-update) | async-done | bytes 720912 | tf_op jit(solution)/shard_map/reduce_scatter | solution.py:68
  787.8 19.4 %reduce-scatter.13.cloned.1.call-done = bf16[128,2048]{1,0:T(8,128)(2,1)} async-done(((bf16[1024,2048]{1,0:T(8,128)(2,1)}), bf16[128,2048]{1,0:T(8,128)(2,1)}) %reduce-scatter.13.cloned.1.call-update) | async-done | bytes 524304 | tf_op jit(solution)/shard_map/reduce_scatter | solution.py:58
  808.9 38.9 %all-reduce.1 = f32[32,448]{1,0:T(8,128)S(1)} all-reduce(f32[32,448]{1,0:T(8,128)S(1)} %concatenate.32), channel_id=7, replica_groups=mesh['rows'=4,'blk'=8] {'rows','blk'}, use_global_device_ids=true, to_apply=%region_20.21.clone | all-reduce | flops 14336 | bytes 114688
  851.5 107.4 %reduce-scatter.17.cloned.1.call-done = bf16[64,2048]{1,0:T(8,128)(2,1)} async-done(((bf16[2048,2048]{1,0:T(8,128)(2,1)}), bf16[64,2048]{1,0:T(8,128)(2,1)}) %reduce-scatter.17.cloned.1.call-update) | async-done | bytes 262160 | tf_op jit(solution)/shard_map/reduce_scatter | solution.py:213
  (244 shorter events, 159.3 us)
Async XLA Ops:
  7.2 119.0 %all-gather.13.cloned.1.call-start = ((), (), s32[]{:S(2)}) async-start(), calls=%async_computation.17 | async-start | bytes 3932160 | tf_op jit(solution)/shard_map/all_gather | solution.py:64
  8.5 28.9 %copy-start.48 = (s32[1,128]{1,0:T(1,128)S(1)}, s32[1,128]{1,0:T(1,128)}, u32[]{:S(2)}) copy-start(s32[1,128]{1,0:T(1,128)} %param.14) | copy-start | bytes 1540
  8.5 28.9 %copy-start.40 = (bf16[64]{0:T(256)(128)(2,1)S(1)}, bf16[64]{0:T(256)(128)(2,1)}, u32[]{:S(2)}) copy-start(bf16[64]{0:T(256)(128)(2,1)} %param.16) | copy-start | bytes 388
  8.5 28.9 %copy-start.41 = (bf16[64]{0:T(256)(128)(2,1)S(1)}, bf16[64]{0:T(256)(128)(2,1)}, u32[]{:S(2)}) copy-start(bf16[64]{0:T(256)(128)(2,1)} %param.17) | copy-start | bytes 388
  8.6 28.9 %copy-start.42 = (bf16[64]{0:T(256)(128)(2,1)S(1)}, bf16[64]{0:T(256)(128)(2,1)}, u32[]{:S(2)}) copy-start(bf16[64]{0:T(256)(128)(2,1)} %param.21) | copy-start | bytes 388
  8.6 28.9 %copy-start.43 = (bf16[64]{0:T(256)(128)(2,1)S(1)}, bf16[64]{0:T(256)(128)(2,1)}, u32[]{:S(2)}) copy-start(bf16[64]{0:T(256)(128)(2,1)} %param.22) | copy-start | bytes 388
  8.6 28.9 %copy-start.44 = (bf16[192]{0:T(256)(128)(2,1)S(1)}, bf16[192]{0:T(256)(128)(2,1)}, u32[]{:S(2)}) copy-start(bf16[192]{0:T(256)(128)(2,1)} %param.19) | copy-start | bytes 1156
  8.6 68.6 %copy-start = (bf16[1,128,2048]{2,1,0:T(8,128)(2,1)S(1)}, bf16[1,128,2048]{2,1,0:T(8,128)(2,1)}, u32[]{:S(2)}) copy-start(bf16[1,128,2048]{2,1,0:T(8,128)(2,1)} %param.13) | copy-start | bytes 1572868
  10.0 69.7 %copy-start.13 = (bf16[64,5632]{1,0:T(8,128)(2,1)S(1)}, bf16[64,5632]{1,0:T(8,128)(2,1)}, u32[]{:S(2)}) copy-start(bf16[64,5632]{1,0:T(8,128)(2,1)} %param.24) | copy-start | bytes 2162692
  37.3 106.8 %all-gather.11.cloned.1.call-start = ((), (), s32[]{:S(2)}) async-start(), calls=%async_computation.16 | async-start | bytes 4718592 | tf_op jit(solution)/shard_map/all_gather | solution.py:54
  78.9 147.6 %all-gather.15.cloned.1.call-start = ((), (), s32[]{:S(2)}) async-start(), calls=%async_computation.18 | async-start | bytes 8650752 | tf_op jit(solution)/shard_map/all_gather | solution.py:140
  83.9 41.4 %all-to-all-start.3 = ((bf16[8,64,704]{2,1,0:T(8,128)(2,1)}), bf16[8,64,704]{2,1,0:T(8,128)(2,1)S(1)}, u32[]{:S(2)}, u32[]{:S(2)}) async-start(bf16[8,64,704]{2,1,0:T(8,128)(2,1)} %reshape.389), calls=%async_computation.3 | async-start | bytes 1572864 | tf_op jit(solution)/shard_map/all_to_all | solution.py:74
  87.7 183.7 %all-gather.21.cloned.1.call-start = ((), (), s32[]{:S(2)}) async-start(), calls=%async_computation.21 | async-start | bytes 3932160 | tf_op jit(solution)/shard_map/all_gather | solution.py:64
  89.5 61.2 %copy-start.17 = (f32[1024,8]{0,1:T(8,128)}, f32[1024,8]{0,1:T(8,128)S(1)}, u32[]{:S(2)}) copy-start(f32[1024,8]{0,1:T(8,128)S(1)} %get-tuple-element.49) | copy-start | bytes 98308
  90.1 79.6 %copy-start.1 = (pred[1024,1024]{0,1:T(8,128)(4,1)}, pred[1024,1024]{0,1:T(8,128)(4,1)S(1)}, u32[]{:S(2)}) copy-start(pred[1024,1024]{0,1:T(8,128)(4,1)S(1)} %fusion.13) | copy-start | bytes 3145732
  179.6 24.0 %all-to-all-start.1 = ((bf16[8,128,256]{1,2,0:T(8,128)(2,1)}), bf16[8,128,256]{1,2,0:T(8,128)(2,1)S(1)}, u32[]{:S(2)}, u32[]{:S(2)}) async-start(bf16[8,128,256]{1,2,0:T(8,128)(2,1)} %copy.65), calls=%async_computation.1 | async-start | bytes 1048576 | tf_op jit(solution)/shard_map/all_to_all | solution.py:74
  183.1 137.4 %all-gather.17.cloned.1.call-start = ((), (), s32[]{:S(2)}) async-start(), calls=%async_computation.19 | async-start | bytes 4718592 | tf_op jit(solution)/shard_map/all_gather | solution.py:54
  232.6 132.4 %all-gather.19.cloned.1.call-start = ((), (), s32[]{:S(2)}) async-start(), calls=%async_computation.20 | async-start | bytes 3932160 | tf_op jit(solution)/shard_map/all_gather | solution.py:64
  264.4 144.2 %all-gather.23.cloned.1.call-start = ((), (), s32[]{:S(2)}) async-start(), calls=%async_computation.22 | async-start | bytes 3604480 | tf_op jit(solution)/shard_map/all_gather | solution.py:64
  265.2 192.3 %all-gather.25.cloned.1.call-start = ((), (), s32[]{:S(2)}) async-start(), calls=%async_computation.31 | async-start | bytes 4718592 | tf_op jit(solution)/shard_map/all_gather | solution.py:54
  265.9 259.5 %reduce-scatter.11.cloned.1.call-start = ((), (), s32[]{:S(2)}) async-start(), calls=%async_computation.24 | async-start | bytes 4718592 | tf_op jit(solution)/shard_map/reduce_scatter | solution.py:58
  476.5 99.2 %reduce-scatter.9.cloned.1.call-start = ((), (), s32[]{:S(2)}) async-start(), calls=%async_computation.23 | async-start | bytes 4718592 | tf_op jit(solution)/shard_map/reduce_scatter | solution.py:58
  484.3 176.9 %reduce-scatter.21.cloned.1.call-start = ((), (), s32[]{:S(2)}) async-start(), calls=%async_computation.29 | async-start | bytes 3604480 | tf_op jit(solution)/shard_map/reduce_scatter | solution.py:68
  585.7 19.5 %all-to-all-start.4 = ((bf16[8,128,256]{1,2,0:T(8,128)(2,1)}), bf16[8,128,256]{1,2,0:T(8,128)(2,1)}, u32[]{:S(2)}, u32[]{:S(2)}) async-start(bf16[8,128,256]{1,2,0:T(8,128)(2,1)} %bitcast.20), calls=%async_computation.6 | async-start | bytes 1048576 | tf_op jit(solution)/shard_map/all_to_all | solution.py:74
  589.9 77.8 %reduce-scatter.19.cloned.1.call-start = ((), (), s32[]{:S(2)}) async-start(), calls=%async_computation.28 | async-start | bytes 3604480 | tf_op jit(solution)/shard_map/reduce_scatter | solution.py:68
  597.7 115.0 %reduce-scatter.15.cloned.1.call-start = ((), (), s32[]{:S(2)}) async-start(), calls=%async_computation.26 | async-start | bytes 3932160 | tf_op jit(solution)/shard_map/reduce_scatter | solution.py:68
  640.0 115.0 %reduce-scatter.23.cloned.1.call-start = ((), (), s32[]{:S(2)}) async-start(), calls=%async_computation.30 | async-start | bytes 3604480 | tf_op jit(solution)/shard_map/reduce_scatter | solution.py:68
  647.9 159.2 %reduce-scatter.13.cloned.1.call-start = ((), (), s32[]{:S(2)}) async-start(), calls=%async_computation.25 | async-start | bytes 4718592 | tf_op jit(solution)/shard_map/reduce_scatter | solution.py:58
  655.5 303.4 %reduce-scatter.17.cloned.1.call-start = ((), (), s32[]{:S(2)}) async-start(), calls=%async_computation.27 | async-start | bytes 8650752 | tf_op jit(solution)/shard_map/reduce_scatter | solution.py:213
  663.5 25.2 %all-to-all-start.7 = ((bf16[8,64,704]{2,1,0:T(8,128)(2,1)}), bf16[8,64,704]{2,1,0:T(8,128)(2,1)}, u32[]{:S(2)}, u32[]{:S(2)}) async-start(bf16[8,64,704]{2,1,0:T(8,128)(2,1)} %bitcast.39), calls=%async_computation.14 | async-start | bytes 1572864 | tf_op jit(solution)/shard_map/all_to_all | solution.py:74
  712.7 69.0 %all-to-all-start.5 = ((bf16[8,64,768]{2,1,0:T(8,128)(2,1)}), bf16[8,64,768]{2,1,0:T(8,128)(2,1)S(1)}, u32[]{:S(2)}, u32[]{:S(2)}) async-start(bf16[8,64,768]{2,1,0:T(8,128)(2,1)} %bitcast.180), calls=%async_computation.9 | async-start | bytes 1572864 | tf_op jit(solution)/shard_map/all_to_all | solution.py:74
  783.6 23.6 %copy-start.39 = (f32[128]{0:T(128)S(1)}, f32[128]{0:T(128)}, u32[]{:S(2)}) copy-start(f32[128]{0:T(128)} %copy-done.38) | copy-start | bytes 1540
  (40 other events, 284.8 us)
Sparse Core Ops, SparseCore 0:
  37.5 43.7 all-gather.12
  83.4 60.6 all-gather.10
  147.2 79.2 all-gather.14
  228.7 42.5 all-gather.20
  273.3 47.1 all-gather.16
  322.2 42.6 all-gather.18
  366.8 41.7 all-gather.22
  410.2 47.1 all-gather.24
  476.6 48.7 reduce-scatter.10
  527.5 48.1 reduce-scatter.8
  578.7 39.9 reduce-scatter.20
  621.6 41.7 reduce-scatter.18
  666.4 43.9 reduce-scatter.14
  713.2 41.7 reduce-scatter.22
  757.1 49.9 reduce-scatter.12
  809.3 149.5 reduce-scatter.16

commit v2 on v1

--- a/solution.py
+++ b/solution.py
@@ -1,8 +1,11 @@
+import functools
 import math
 
 import jax
 import jax.numpy as jnp
 from jax import lax
+from jax.experimental import pallas as pl
+from jax.experimental.pallas import tpu as pltpu
 from jax.sharding import PartitionSpec as P
 
 HEADS = 32
@@ -278,6 +281,927 @@
     return body
 
 
+MESH_ID = pl.DeviceIdType.MESH
+DMA = pltpu.SemaphoreType.DMA
+HBM = pl.ANY
+VMEM = pltpu.VMEM
+LIMIT = 56 * 1024 * 1024
+
+
+class Place:
+    def __init__(self):
+        self.r = lax.axis_index("rows")
+        self.b = lax.axis_index("blk")
+        self.z = self.b // 2
+        self.c = lax.rem(self.b, 2)
+        self.sibling = 2 * self.z + 1 - self.c
+        self.rx = self.r + 1 - 2 * lax.rem(self.r, 2)
+        self.ry = lax.rem(self.r + 2, 4)
+        self.rd = 3 - self.r
+
+    def barrier(self, diagonal=False):
+        sem = pltpu.get_barrier_semaphore()
+        peers = [(self.r, lax.rem(self.b + k, 8)) for k in range(1, 8)]
+        peers += [(self.rx, self.b), (self.ry, self.b)]
+        if diagonal:
+            peers.append((self.rd, self.b))
+        for peer in peers:
+            pl.semaphore_signal(sem, inc=1, device_id=peer, device_id_type=MESH_ID)
+        pl.semaphore_wait(sem, len(peers))
+
+
+def remote(src, dst, send, recv, r, b):
+    return pltpu.make_async_remote_copy(
+        src_ref=src, dst_ref=dst, send_sem=send, recv_sem=recv, device_id=(r, b), device_id_type=MESH_ID
+    )
+
+
+def drive(*jobs):
+    active = list(jobs)
+    while active:
+        for job in list(active):
+            try:
+                next(job)
+            except StopIteration:
+                active.remove(job)
+
+
+CHUNKS = 2
+
+
+def line_gather_sems():
+    return [DMA((4, CHUNKS))] * 4 + [DMA((7, CHUNKS))] * 2 + [DMA]
+
+
+def line_gather(at, own, full, sems):
+    up_send, down_send, up_recv, down_recv, pair_send, pair_recv, local_sem = sems
+    count = own.shape[0]
+    size = count // CHUNKS
+
+    def rows(device, k):
+        return full.at[pl.ds(pl.multiple_of(device * count + k * size, size), size)]
+
+    def up(d, k, src):
+        return remote(src, rows(at.b - 2 * d, k), up_send.at[d, k], up_recv.at[d, k], at.r, at.b + 2)
+
+    def down(d, k, src):
+        return remote(
+            src, rows(at.b + 2 * d, k), down_send.at[d, k], down_recv.at[d, k], at.r, at.b - 2
+        )
+
+    def up_in(d, k):
+        piece = rows(at.b - 2 * d - 2, k)
+        return remote(piece, piece, up_send.at[d, k], up_recv.at[d, k], at.r, at.b + 2)
+
+    def down_in(d, k):
+        piece = rows(at.b + 2 * d + 2, k)
+        return remote(piece, piece, down_send.at[d, k], down_recv.at[d, k], at.r, at.b - 2)
+
+    def pair(i, k, device, src):
+        return remote(src, rows(device, k), pair_send.at[i, k], pair_recv.at[i, k], at.r, at.sibling)
+
+    def pair_in(i, k, device):
+        piece = rows(device, k)
+        return remote(piece, piece, pair_send.at[i, k], pair_recv.at[i, k], at.r, at.sibling)
+
+    local = pltpu.make_async_copy(own, full.at[pl.ds(at.b * count, count)], local_sem)
+    local.start()
+    for k in range(CHUNKS):
+        src = own.at[pl.ds(k * size, size)]
+        pl.when(at.z < 3)(lambda: up(0, k, src).start())
+        pl.when(at.z > 0)(lambda: down(0, k, src).start())
+        pair(0, k, at.b, src).start()
+    yield
+    for d in range(3):
+        for k in range(CHUNKS):
+
+            @pl.when(at.z - 1 - d >= 0)
+            def _():
+                device = at.b - 2 * d - 2
+                up_in(d, k).wait_recv()
+                if d < 2:
+                    pl.when(at.z < 3)(lambda: up(d + 1, k, rows(device, k)).start())
+                pair(1 + d, k, device, rows(device, k)).start()
+
+            @pl.when(at.z + 1 + d <= 3)
+            def _():
+                device = at.b + 2 * d + 2
+                down_in(d, k).wait_recv()
+                if d < 2:
+                    pl.when(at.z > 0)(lambda: down(d + 1, k, rows(device, k)).start())
+                pair(4 + d, k, device, rows(device, k)).start()
+
+            yield
+    local.wait()
+    for k in range(CHUNKS):
+        src = own.at[pl.ds(k * size, size)]
+        pair(0, k, at.b, src).wait_send()
+        pair_in(0, k, at.sibling).wait_recv()
+        pl.when(at.z < 3)(lambda: up(0, k, src).wait_send())
+        pl.when(at.z > 0)(lambda: down(0, k, src).wait_send())
+        for d in range(3):
+
+            @pl.when(at.z - 1 - d >= 0)
+            def _():
+                device = at.b - 2 * d - 2
+                pair(1 + d, k, device, rows(device, k)).wait_send()
+                pair_in(1 + d, k, at.sibling - 2 * d - 2).wait_recv()
+                if d < 2:
+                    pl.when(at.z < 3)(lambda: up(d + 1, k, rows(device, k)).wait_send())
+
+            @pl.when(at.z + 1 + d <= 3)
+            def _():
+                device = at.b + 2 * d + 2
+                pair(4 + d, k, device, rows(device, k)).wait_send()
+                pair_in(4 + d, k, at.sibling + 2 * d + 2).wait_recv()
+                if d < 2:
+                    pl.when(at.z > 0)(lambda: down(d + 1, k, rows(device, k)).wait_send())
+
+
+def line_scatter_scratch(count, width):
+    block = VMEM((4, count, width), jnp.bfloat16)
+    arrive = VMEM((3, count, width), jnp.bfloat16)
+    return [block, arrive, arrive] + [DMA((4, CHUNKS))] * 2 + [DMA((3, CHUNKS))] * 4
+
+
+def line_scatter(at, partial, result, scratch):
+    held, from_below, from_above, pair_send, pair_recv, up_send, up_recv, down_send, down_recv = scratch
+    count = held.shape[1]
+    size = count // CHUNKS
+
+    def cut(k):
+        return pl.ds(k * size, size)
+
+    def block(z, c, k):
+        return pl.ds(pl.multiple_of((2 * z + c) * count + k * size, size), size)
+
+    def pair(z, k):
+        return remote(
+            partial.at[block(z, 1 - at.c, k)],
+            held.at[z, cut(k)],
+            pair_send.at[z, k],
+            pair_recv.at[z, k],
+            at.r,
+            at.sibling,
+        )
+
+    def up(z, k):
+        return remote(
+            held.at[z, cut(k)],
+            from_below.at[z - 1, cut(k)],
+            up_send.at[z - 1, k],
+            up_recv.at[z - 1, k],
+            at.r,
+            at.b + 2,
+        )
+
+    def down(z, k):
+        return remote(
+            held.at[z, cut(k)],
+            from_above.at[z, cut(k)],
+            down_send.at[z, k],
+            down_recv.at[z, k],
+            at.r,
+            at.b - 2,
+        )
+
+    def wide(ref):
+        return ref[...].astype(jnp.float32)
+
+    def own(z, k):
+        return wide(partial.at[block(z, at.c, k)]) + wide(held.at[z, cut(k)])
+
+    for z in (3, 0, 2, 1):
+        for k in range(CHUNKS):
+            pair(z, k).start()
+    yield
+    for step in range(3):
+        for k in range(CHUNKS):
+            far, near = 3 - step, step
+
+            @pl.when(at.z < far)
+            def _():
+                pair(far, k).wait_recv()
+
+                @pl.when(at.z == 0)
+                def _():
+                    held[far, cut(k)] = own(far, k).astype(jnp.bfloat16)
+
+                @pl.when(at.z > 0)
+                def _():
+                    up(far, k).wait_recv()
+                    held[far, cut(k)] = (
+                        own(far, k) + wide(from_below.at[far - 1, cut(k)])
+                    ).astype(jnp.bfloat16)
+
+                up(far, k).start()
+
+            @pl.when(at.z > near)
+            def _():
+                pair(near, k).wait_recv()
+
+                @pl.when(at.z == 3)
+                def _():
+                    held[near, cut(k)] = own(near, k).astype(jnp.bfloat16)
+
+                @pl.when(at.z < 3)
+                def _():
+                    down(near, k).wait_recv()
+                    held[near, cut(k)] = (
+                        own(near, k) + wide(from_above.at[near, cut(k)])
+                    ).astype(jnp.bfloat16)
+
+                down(near, k).start()
+
+            yield
+    for z in range(4):
+        for k in range(CHUNKS):
+
+            @pl.when(at.z == z)
+            def _():
+                pair(z, k).wait_recv()
+                total = own(z, k)
+                if z > 0:
+                    up(z, k).wait_recv()
+                    total += wide(from_below.at[z - 1, cut(k)])
+                if z < 3:
+                    down(z, k).wait_recv()
+                    total += wide(from_above.at[z, cut(k)])
+                result[cut(k)] = total.astype(result.dtype)
+
+    for z in range(4):
+        for k in range(CHUNKS):
+            pair(z, k).wait_send()
+            if z > 0:
+                pl.when(at.z < z)(lambda: up(z, k).wait_send())
+            if z < 3:
+                pl.when(at.z > z)(lambda: down(z, k).wait_send())
+
+
+def half_of(ref, axis, which):
+    size = ref.shape[axis] // 2
+    return ref.at[pl.ds(which * size, size)] if axis == 0 else ref.at[:, pl.ds(which * size, size)]
+
+
+def square_gather_sems():
+    return [DMA((6,)), DMA((6,)), DMA]
+
+
+def square_gather(at, own, full, sems, axis=0):
+    send, recv, local_sem = sems
+    count = own.shape[0]
+
+    def part(r, which):
+        return half_of(full.at[pl.ds(pl.multiple_of(r * count, count), count)], axis, which)
+
+    def copy(i, src, r_of, which, to):
+        return remote(src, part(r_of, which), send.at[i], recv.at[i], to, at.b)
+
+    outs = [
+        copy(0, half_of(own, axis, 0), at.r, 0, at.rx),
+        copy(1, half_of(own, axis, 1), at.r, 1, at.ry),
+        copy(2, half_of(own, axis, 1), at.r, 1, at.rx),
+        copy(3, half_of(own, axis, 0), at.r, 0, at.ry),
+    ]
+    ins = [
+        copy(0, part(at.rx, 0), at.rx, 0, at.rx),
+        copy(1, part(at.ry, 1), at.ry, 1, at.ry),
+        copy(2, part(at.rx, 1), at.rx, 1, at.rx),
+        copy(3, part(at.ry, 0), at.ry, 0, at.ry),
+        copy(4, part(at.rd, 0), at.rd, 0, at.ry),
+        copy(5, part(at.rd, 1), at.rd, 1, at.rx),
+    ]
+    local = pltpu.make_async_copy(own, full.at[pl.ds(at.r * count, count)], local_sem)
+    local.start()
+    for out in outs:
+        out.start()
+    yield
+    ins[0].wait_recv()
+    outs.append(copy(4, part(at.rx, 0), at.rx, 0, at.ry))
+    outs[4].start()
+    yield
+    ins[1].wait_recv()
+    outs.append(copy(5, part(at.ry, 1), at.ry, 1, at.rx))
+    outs[5].start()
+    yield
+    local.wait()
+    for i in (2, 3, 4, 5):
+        ins[i].wait_recv()
+    for out in outs:
+        out.wait_send()
+
+
+def square_scatter_scratch(count, width, axis=0):
+    half = (count // 2, width) if axis == 0 else (count, width // 2)
+    piece = VMEM((count, width), jnp.bfloat16)
+    part = VMEM(half, jnp.bfloat16)
+    return [piece, piece, part, part, part, part, DMA((6,)), DMA((6,))]
+
+
+def square_scatter(at, partial, result, scratch, axis=0):
+    from_x, from_y, far_x, far_y, out_x, out_y, send, recv = scratch
+    count = from_x.shape[0]
+
+    def part(r, which):
+        return half_of(partial.at[pl.ds(pl.multiple_of(r * count, count), count)], axis, which)
+
+    def wide(ref):
+        return ref[...].astype(jnp.float32)
+
+    copies = [
+        remote(part(at.rd, 0), far_x, send.at[0], recv.at[0], at.rx, at.b),
+        remote(part(at.rd, 1), far_y, send.at[1], recv.at[1], at.ry, at.b),
+        remote(part(at.rx, 0), half_of(from_x, axis, 0), send.at[2], recv.at[2], at.rx, at.b),
+        remote(part(at.ry, 1), half_of(from_y, axis, 1), send.at[3], recv.at[3], at.ry, at.b),
+        remote(out_y, half_of(from_y, axis, 0), send.at[4], recv.at[4], at.ry, at.b),
+        remote(out_x, half_of(from_x, axis, 1), send.at[5], recv.at[5], at.rx, at.b),
+    ]
+    for copy in copies[:4]:
+        copy.start()
+    yield
+    copies[0].wait_recv()
+    out_y[...] = (wide(part(at.ry, 0)) + wide(far_x)).astype(jnp.bfloat16)
+    copies[4].start()
+    yield
+    copies[1].wait_recv()
+    out_x[...] = (wide(part(at.rx, 1)) + wide(far_y)).astype(jnp.bfloat16)
+    copies[5].start()
+    yield
+    for i in (2, 3, 4, 5):
+        copies[i].wait_recv()
+    for which in range(2):
+        total = (
+            wide(part(at.r, which)) + wide(half_of(from_x, axis, which)) + wide(half_of(from_y, axis, which))
+        )
+        spot = half_of(result, axis, which)
+        spot[...] = total.astype(result.dtype)
+    for copy in copies:
+        copy.wait_send()
+
+
+def exchange_sems(parts=1):
+    return [DMA((7, parts)), DMA((7, parts)), DMA((parts,))]
+
+
+def exchange(at, take, put, sems, parts=1):
+    send, recv, local_sem = sems
+    locals_ = [
+        pltpu.make_async_copy(take(at.b, p), put(at.b, p), local_sem.at[p]) for p in range(parts)
+    ]
+    outs, ins = [], []
+    for k in (4, 3, 5, 2, 6, 1, 7):
+        to, source = lax.rem(at.b + k, 8), lax.rem(at.b + 8 - k, 8)
+        for p in range(parts):
+            pair = (send.at[k - 1, p], recv.at[k - 1, p])
+            outs.append(remote(take(to, p), put(at.b, p), *pair, at.r, to))
+            ins.append(remote(put(source, p), put(source, p), *pair, at.r, source))
+    for copy in locals_ + outs:
+        copy.start()
+    yield
+    for copy in ins:
+        copy.wait_recv()
+    for copy in locals_:
+        copy.wait()
+    for copy in outs:
+        copy.wait_send()
+
+
+def call(kernel, ins, outs, scratch, number, *args):
+    return pl.pallas_call(
+        kernel,
+        out_shape=[jax.ShapeDtypeStruct(shape, kind) for shape, kind, _ in outs],
+        in_specs=[pl.BlockSpec(memory_space=space) for space in ins],
+        out_specs=[pl.BlockSpec(memory_space=space) for _, _, space in outs],
+        scratch_shapes=scratch,
+        compiler_params=pltpu.CompilerParams(
+            collective_id=number, has_side_effects=True, vmem_limit_bytes=LIMIT
+        ),
+    )(*args)
+
+
+def vector_gather(at, own, full, sems):
+    send, recv, local_sem = sems
+    mine = 8 * at.r + at.b
+    outs, ins = [], []
+    for k in range(1, 8):
+        to, source = lax.rem(at.b + k, 8), lax.rem(at.b + 8 - k, 8)
+        outs.append(remote(own, full.at[mine], send.at[k - 1], recv.at[k - 1], at.r, to))
+        piece = full.at[8 * at.r + source]
+        ins.append(remote(piece, piece, send.at[k - 1], recv.at[k - 1], at.r, source))
+    local = pltpu.make_async_copy(own, full.at[mine], local_sem)
+    local.start()
+    for out in outs:
+        out.start()
+    yield
+    for copy in ins:
+        copy.wait_recv()
+    local.wait()
+    group = full.at[pl.ds(8 * at.r, 8)]
+    later = []
+    for i, row in enumerate((at.rx, at.ry, at.rd)):
+        outs.append(remote(group, group, send.at[7 + i], recv.at[7 + i], row, at.b))
+        outs[-1].start()
+        theirs = full.at[pl.ds(8 * row, 8)]
+        later.append(remote(theirs, theirs, send.at[7 + i], recv.at[7 + i], row, at.b))
+    yield
+    for copy in later:
+        copy.wait_recv()
+    for out in outs:
+        out.wait_send()
+
+
+def start_kernel(
+    x_ref, vector_ref, project_ref, down_ref,
+    vectors, normed, pieces, w_project, w_down,
+    unit, own, vector_sems, exchange_sem, square_sem, down_sem, line_sems,
+):
+    at = Place()
+    at.barrier(diagonal=True)
+    width = x_ref.shape[1]
+    vector_job = vector_gather(at, vector_ref, vectors, vector_sems)
+    next(vector_job)
+    inner = w_project.shape[1] // 3
+    depth = project_ref.shape[0]
+    project_job = exchange(
+        at,
+        lambda b, p: project_ref.at[:, pl.ds(pl.multiple_of(p * width + b * inner, inner), inner)],
+        lambda b, p: pieces.at[
+            pl.ds(pl.multiple_of(b * depth, depth), depth), pl.ds(p * inner, inner)
+        ],
+        exchange_sem,
+        3,
+    )
+    next(project_job)
+    down_job = square_gather(at, down_ref, w_down, down_sem, axis=1)
+    next(down_job)
+    x = x_ref[...].astype(jnp.float32)
+    centered = x - jnp.mean(x, axis=1, keepdims=True)
+    unit[...] = centered * lax.rsqrt(jnp.mean(centered * centered, axis=1, keepdims=True) + epsilon)
+    drive(vector_job)
+    for tile in range(width // 128):
+        lanes = slice(tile * 128, tile * 128 + 128)
+        both = vectors[2 * tile].astype(jnp.float32) + vectors[2 * tile + 1].astype(jnp.float32)
+        own[:, lanes] = (unit[:, lanes] * both[0:1] + both[1:2]).astype(jnp.bfloat16)
+    line_job = line_gather(at, own, normed, line_sems)
+    next(line_job)
+    drive(project_job)
+    square_job = square_gather(at, pieces, w_project, square_sem)
+    drive(square_job, line_job, down_job)
+
+
+def pack_sems(groups):
+    flat, spans = [], []
+    for group in groups:
+        spans.append((len(flat), len(flat) + len(group)))
+        flat += group
+    return flat, spans
+
+
+def grouped(kernel, lead, spans):
+    def run(*refs):
+        rest = refs[lead:]
+        return kernel(*refs[:lead], *[rest[a:b] for a, b in spans])
+
+    return run
+
+
+def start_call(x, vector, project, down):
+    rows, width = x.shape
+    depth = project.shape[0]
+    inner = project.shape[1] // 8
+    bf = jnp.bfloat16
+    groups = [
+        [DMA((10,)), DMA((10,)), DMA], exchange_sems(3), square_gather_sems(), square_gather_sems(),
+        line_gather_sems(),
+    ]
+    flat, spans = pack_sems(groups)
+    outs = [
+        ((32, 16, 128), bf, VMEM), ((8 * rows, width), bf, HBM), ((8 * depth, inner), bf, HBM),
+        ((32 * depth, inner), bf, HBM), ((4 * down.shape[0], width), bf, HBM),
+    ]
+    scratch = [VMEM((rows, width), jnp.float32), VMEM((rows, width), bf)] + flat
+    vectors, normed, _, w_project, w_down = call(
+        grouped(start_kernel, 11, spans), [VMEM, VMEM, HBM, HBM], outs, scratch, 0, x, vector, project, down
+    )
+    return vectors, normed, w_project, w_down
+
+
+def turned(columns, cosine, minus, plus):
+    half = ROT // 2
+    return (
+        columns * cosine
+        + pltpu.roll(columns, 128 - half, 1) * minus
+        + pltpu.roll(columns, half, 1) * plus
+    )
+
+
+def score_mask(first_row, rows, keys, start):
+    row = lax.broadcasted_iota(jnp.int32, (rows, keys), 0) + first_row
+    col = lax.broadcasted_iota(jnp.int32, (rows, keys), 1)
+    return (col <= row) & (col >= start)
+
+
+QROWS = 256
+
+
+def attend_forward_kernel(
+    x_ref, w_ref, bias, start, cosine, minus, plus, gate_up,
+    queries, keys, values, attended, log_total, mixed_heads, gate_up_all,
+    low, own_sems, gate_up_sems,
+):
+    at = Place()
+    at.barrier()
+    length, local = queries.shape
+    depth = gate_up.shape[1]
+    gate_up_job = exchange(
+        at, lambda b, p: gate_up.at[b], lambda b, p: gate_up_all.at[b], gate_up_sems
+    )
+    next(gate_up_job)
+    scale = 1.0 / math.sqrt(local * 8 // HEADS)
+    blocks = length // QROWS
+
+    @pl.loop(0, blocks)
+    def _(i):
+        rows = pl.ds(pl.multiple_of(i * QROWS, QROWS), QROWS)
+        mixed = dot(x_ref[rows], w_ref[...], ((1,), (0,))) + bias[...]
+        tables = (cosine[rows], minus[rows], plus[rows])
+        for pair in range(local // 128):
+            lanes = slice(pair * 128, pair * 128 + 128)
+            queries[rows, lanes] = turned(mixed[:, lanes], *tables).astype(jnp.bfloat16)
+            shifted = slice(local + pair * 128, local + pair * 128 + 128)
+            keys[rows, lanes] = turned(mixed[:, shifted], *tables).astype(jnp.bfloat16)
+        values[rows] = mixed[:, 2 * local :].astype(jnp.bfloat16)
+
+    send, recv, local_sem = own_sems
+
+    def deliver(to):
+        rows = low.at[pl.ds(to * 128, 128)]
+        spot = mixed_heads.at[:, pl.ds(pl.multiple_of(at.b * local, local), local)]
+        return remote(rows, spot, send.at[to], recv.at[at.b], at.r, to)
+
+    for i in range(blocks):
+        rows = slice(i * QROWS, (i + 1) * QROWS)
+        count = (i + 1) * QROWS
+
+        @pl.loop(0, local // 128)
+        def _(pair):
+            lanes = pl.ds(pl.multiple_of(pair * 128, 128), 128)
+            lane = lax.broadcasted_iota(jnp.int32, (QROWS, 128), 1)
+            q, k, v = queries[rows, lanes], keys[:count, lanes], values[:count, lanes]
+            allowed = score_mask(i * QROWS, QROWS, count, start[rows])
+            found = []
+            for head in range(2):
+                mine = (lane >= 64) if head else (lane < 64)
+                scores = dot(jnp.where(mine, q, jnp.zeros_like(q)), k, ((1,), (1,))) * scale
+                scores = jnp.where(allowed, scores, masked_value)
+                top = jnp.max(scores, axis=1, keepdims=True)
+                weights = jnp.exp(scores - top)
+                total = jnp.sum(weights, axis=1, keepdims=True)
+                found.append(
+                    (dot(weights.astype(jnp.bfloat16), v, ((1,), (0,))) / total, top + jnp.log(total))
+                )
+            both = jnp.where(lane < 64, found[0][0], found[1][0])
+            attended[rows, lanes] = both
+            low[rows, lanes] = both.astype(jnp.bfloat16)
+            log_total[rows, lanes] = jnp.where(lane < 64, found[0][1], found[1][1])
+
+        for to in range(i * QROWS // 128, (i + 1) * QROWS // 128):
+            pl.when(at.b != to)(lambda: deliver(to).start())
+
+            @pl.when(at.b == to)
+            def _():
+                pltpu.make_async_copy(
+                    low.at[pl.ds(to * 128, 128)],
+                    mixed_heads.at[:, pl.ds(pl.multiple_of(at.b * local, local), local)],
+                    local_sem,
+                ).start()
+
+    for source in range(8):
+
+        @pl.when(at.b != source)
+        def _():
+            spot = mixed_heads.at[:, pl.ds(source * local, local)]
+            remote(spot, spot, send.at[source], recv.at[source], at.r, source).wait_recv()
+
+        @pl.when(at.b == source)
+        def _():
+            pltpu.make_async_copy(
+                low.at[pl.ds(source * 128, 128)],
+                mixed_heads.at[:, pl.ds(source * local, local)],
+                local_sem,
+            ).wait()
+
+    drive(gate_up_job)
+    for to in range(8):
+        pl.when(at.b != to)(lambda: deliver(to).wait_send())
+
+
+def attend_forward(x, w, bias, start, tables, gate_up):
+    length, local = x.shape[0], w.shape[1] // 3
+    bf, f32 = jnp.bfloat16, jnp.float32
+    flat, spans = pack_sems([[DMA((8,)), DMA((8,)), DMA], exchange_sems()])
+    outs = [((length, local), bf, VMEM)] * 3 + [((length, local), f32, VMEM)] * 2
+    outs += [((length // 8, 8 * local), bf, VMEM), (gate_up.shape, bf, HBM)]
+    return call(
+        grouped(attend_forward_kernel, 16, spans), [VMEM] * 7 + [HBM], outs,
+        [VMEM((length, local), bf)] + flat, 1, x, w, bias, start, *tables, gate_up,
+    )
+
+
+def second_gather_kernel(own, gate_up, normed, w_gate_up, line_sems, square_sems):
+    at = Place()
+    at.barrier()
+    drive(
+        line_gather(at, own, normed, line_sems), square_gather(at, gate_up, w_gate_up, square_sems)
+    )
+
+
+def second_gather(own, gate_up):
+    flat, spans = pack_sems([line_gather_sems(), square_gather_sems()])
+    bf = jnp.bfloat16
+    outs = [
+        ((8 * own.shape[0], own.shape[1]), bf, HBM), ((4 * gate_up.shape[0], gate_up.shape[1]), bf, HBM)
+    ]
+    return call(
+        grouped(second_gather_kernel, 4, spans), [HBM, HBM], outs, flat, 2, own, gate_up
+    )
+
+
+def reduce_kernel(axis, partial, weight, result, weight_result, line_scratch, square_scratch):
+    at = Place()
+    at.barrier()
+    drive(
+        line_scatter(at, partial, result, line_scratch),
+        square_scatter(at, weight, weight_result, square_scratch, axis),
+    )
+
+
+def reduce_call(partial, weight, number, axis, kind):
+    rows, width = partial.shape[0] // 8, partial.shape[1]
+    owned = (weight.shape[0] // 4, weight.shape[1])
+    flat, spans = pack_sems([line_scatter_scratch(rows, width), square_scatter_scratch(*owned, axis)])
+    outs = [((rows, width), jnp.float32, VMEM), (owned, kind, VMEM)]
+    return call(
+        grouped(functools.partial(reduce_kernel, axis), 4, spans), [VMEM, VMEM], outs, flat, number,
+        partial, weight,
+    )
+
+
+def attend_backward_kernel(
+    grad_rows, queries, keys, values, attended, log_total, start, cosine, minus, plus, weight,
+    grad_mixed, weight_result,
+    grad, keys_sum, values_sum, own_sems, square_scratch,
+):
+    at = Place()
+    at.barrier()
+    length, local = queries.shape
+    scale = 1.0 / math.sqrt(local * 8 // HEADS)
+    blocks = length // QROWS
+    own_job = exchange(
+        at,
+        lambda b, p: grad_rows.at[:, pl.ds(pl.multiple_of(b * local, local), local)],
+        lambda b, p: grad.at[pl.ds(pl.multiple_of(b * 128, 128), 128)],
+        own_sems,
+    )
+    next(own_job)
+    weight_job = square_scatter(at, weight, weight_result, square_scratch)
+    next(weight_job)
+    keys_sum[...] = jnp.zeros_like(keys_sum)
+    values_sum[...] = jnp.zeros_like(values_sum)
+    drive(own_job)
+    for i in range(blocks):
+        rows = slice(i * QROWS, (i + 1) * QROWS)
+        count = (i + 1) * QROWS
+
+        @pl.loop(0, local // 128)
+        def _(pair):
+            lanes = pl.ds(pl.multiple_of(pair * 128, 128), 128)
+            lane = lax.broadcasted_iota(jnp.int32, (QROWS, 128), 1)
+            q, g = queries[rows, lanes], grad[rows, lanes]
+            k, v = keys[:count, lanes], values[:count, lanes]
+            allowed = score_mask(i * QROWS, QROWS, count, start[rows])
+            product = g.astype(jnp.float32) * attended[rows, lanes]
+            logs = log_total[rows, lanes]
+            queries_part, keys_part, values_part = [], [], []
+            for head in range(2):
+                mine = (lane >= 64) if head else (lane < 64)
+                q_head = jnp.where(mine, q, jnp.zeros_like(q))
+                g_head = jnp.where(mine, g, jnp.zeros_like(g))
+                delta = jnp.sum(jnp.where(mine, product, 0.0), axis=1, keepdims=True)
+                log_head = jnp.max(jnp.where(mine, logs, masked_value), axis=1, keepdims=True)
+                scores = dot(q_head, k, ((1,), (1,))) * scale
+                probs = jnp.exp(jnp.where(allowed, scores - log_head, masked_value))
+                grad_probs = dot(g_head, v, ((1,), (1,)))
+                grad_scores = (probs * (grad_probs - delta) * scale).astype(jnp.bfloat16)
+                queries_part.append(dot(grad_scores, k, ((1,), (0,))))
+                keys_part.append(dot(grad_scores, q_head, ((0,), (0,))))
+                values_part.append(dot(probs.astype(jnp.bfloat16), g_head, ((0,), (0,))))
+            both = jnp.where(lane < 64, queries_part[0], queries_part[1])
+            tables = (cosine[rows], -minus[rows], -plus[rows])
+            grad_mixed[rows, lanes] = turned(both, *tables).astype(jnp.bfloat16)
+            keys_sum[:count, lanes] += keys_part[0] + keys_part[1]
+            values_sum[:count, lanes] += values_part[0] + values_part[1]
+
+        next(weight_job, None)
+
+    @pl.loop(0, blocks)
+    def _(i):
+        rows = pl.ds(pl.multiple_of(i * QROWS, QROWS), QROWS)
+        tables = (cosine[rows], -minus[rows], -plus[rows])
+        for pair in range(local // 128):
+            lanes = slice(pair * 128, pair * 128 + 128)
+            shifted = slice(local + pair * 128, local + pair * 128 + 128)
+            grad_mixed[rows, shifted] = turned(keys_sum[rows, lanes], *tables).astype(jnp.bfloat16)
+        grad_mixed[rows, slice(2 * local, 3 * local)] = values_sum[rows].astype(jnp.bfloat16)
+
+    drive(weight_job)
+
+
+def attend_backward(grad_rows, queries, keys, values, attended, log_total, start, tables, weight):
+    length, local = queries.shape
+    bf, f32 = jnp.bfloat16, jnp.float32
+    owned = (weight.shape[0] // 4, weight.shape[1])
+    flat, spans = pack_sems([exchange_sems(), square_scatter_scratch(*owned)])
+    outs = [((length, 3 * local), bf, VMEM), (owned, bf, VMEM)]
+    scratch = [VMEM((length, local), bf), VMEM((length, local), f32), VMEM((length, local), f32)]
+    return call(
+        grouped(attend_backward_kernel, 16, spans), [VMEM] * 11, outs, scratch + flat, 4,
+        grad_rows, queries, keys, values, attended, log_total, start, *tables, weight,
+    )
+
+
+def owners_kernel(
+    project, gate_up, vectors, project_out, gate_up_out, vector_out,
+    arrived, summed, rows_in, project_sems, gate_up_sems, vector_sems, row_sems,
+):
+    at = Place()
+    at.barrier(diagonal=True)
+    vector_job = exchange(at, lambda b, p: vectors.at[b], lambda b, p: arrived.at[b], vector_sems)
+    next(vector_job)
+    project_job = exchange(
+        at, lambda b, p: project.at[b], lambda b, p: project_out.at[b], project_sems
+    )
+    next(project_job)
+    gate_up_job = exchange(
+        at, lambda b, p: gate_up.at[b], lambda b, p: gate_up_out.at[b], gate_up_sems
+    )
+    next(gate_up_job)
+    drive(vector_job)
+    summed[...] = jnp.sum(arrived[...], axis=0)
+    send, recv = row_sems
+    copies = [
+        remote(summed.at[row], rows_in.at[i], send.at[i], recv.at[i], row, at.b)
+        for i, row in enumerate((at.rx, at.ry, at.rd))
+    ]
+    for copy in copies:
+        copy.start()
+    for copy in copies:
+        copy.wait()
+    vector_out[...] = summed[at.r] + rows_in[0] + rows_in[1] + rows_in[2]
+    drive(project_job, gate_up_job)
+
+
+def owners_call(project, gate_up, vectors):
+    f32 = jnp.float32
+    flat, spans = pack_sems(
+        [exchange_sems(), exchange_sems(), exchange_sems(), [DMA((3,)), DMA((3,))]]
+    )
+    tail = vectors.shape[1:]
+    outs = [
+        (project.shape, project.dtype, HBM), (gate_up.shape, gate_up.dtype, HBM), (tail[1:], f32, VMEM)
+    ]
+    scratch = [VMEM((8,) + tail, f32), VMEM(tail, f32), VMEM((3,) + tail[1:], f32)]
+    return call(
+        grouped(owners_kernel, 9, spans), [HBM, HBM, VMEM], outs, scratch + flat, 6,
+        project, gate_up, vectors,
+    )
+
+
+def fast_body(
+    tokens, segments, cotangent, attend_gain, attend_shift, project_weight, project_bias,
+    output_weight, feed_gain, feed_shift, gate_weight, up_weight, down_weight,
+):
+    bf, f32 = jnp.bfloat16, jnp.float32
+    own_rows, width = tokens.shape[1], tokens.shape[2]
+    length = own_rows * 8
+    head_width = width // HEADS
+    local = width // 8
+    hidden = down_weight.shape[0]
+    shard = attend_gain.shape[0]
+    r, b = lax.axis_index("rows"), lax.axis_index("blk")
+
+    small = jnp.stack([attend_gain, attend_shift, feed_gain, feed_shift])
+    zeros = jnp.zeros_like(small)
+    small = jnp.where(
+        b % 2 == 0, jnp.concatenate([small, zeros], 1), jnp.concatenate([zeros, small], 1)
+    )
+    rest = jnp.pad(project_bias, (0, 64)).reshape(2, 128)
+    vector = jnp.concatenate(
+        [small, rest, segments.astype(bf), jnp.zeros((9, 128), bf)], axis=0
+    )
+
+    def pieces_of(weight):
+        depth = weight.shape[0]
+        return weight.reshape(depth, 4, 8, hidden).transpose(2, 0, 1, 3).reshape(8, depth, 4 * hidden)
+
+    w_out = lax.all_gather(output_weight, BOTH, axis=0, tiled=True)
+    gate_up = jnp.concatenate([pieces_of(gate_weight), pieces_of(up_weight)], axis=2)
+
+    vectors, normed_first, w_project, w_down = start_call(
+        tokens[0], vector, project_weight, down_weight
+    )
+    grad_out = gather_blk(cotangent[0])
+
+    def whole(row):
+        pairs = vectors[:, row].reshape(16, 2, 128).astype(f32)
+        return (pairs[:, 0] + pairs[:, 1]).reshape(-1)
+
+    a_gain, f_gain, f_shift = whole(0), whole(2), whole(3)
+    bias = vectors[:, 4:6].reshape(32, 256)[:, : 3 * shard].reshape(3, 8, local)
+    bias = lax.dynamic_index_in_dim(bias, b, 1, False).reshape(1, -1).astype(f32)
+    doc = lax.dynamic_slice_in_dim(vectors[:, 6], 8 * r, 8, 0).reshape(-1).astype(f32)
+    starts = jnp.sum((doc[None, :] < doc[:, None]).astype(jnp.int32), axis=1)
+    places = (jnp.arange(length, dtype=jnp.int32) - starts).astype(f32)
+    half = ROT // 2
+    frequency = jnp.power(rotary_base, -jnp.arange(half, dtype=jnp.int32).astype(f32) / half)
+    angles = frequency[:, None] * places[None, :]
+    cosine, sine = jnp.cos(angles), jnp.sin(angles)
+    gap = jnp.zeros((head_width - ROT, length), f32)
+    eight = jnp.zeros((half, length), f32)
+
+    def table(first, second, fill):
+        one = jnp.concatenate([first, second, gap + fill], axis=0)
+        return jnp.transpose(jnp.concatenate([one, one], axis=0))
+
+    tables = (table(cosine, cosine, 1.0), table(-sine, eight, 0.0), table(eight, sine, 0.0))
+    start = starts[:, None]
+
+    queries, keys, values, attended, log_total, attended_low, gate_up = attend_forward(
+        normed_first, w_project, bias, start, tables, gate_up
+    )
+    inputs = tokens[0].astype(f32)
+    resid_mid = inputs + dot(attended_low, w_out, ((1,), (0,)))
+    unit_second, inverse_second = norm_stats(resid_mid)
+    normed_second, w_gate_up = second_gather(
+        (unit_second * f_gain + f_shift).astype(bf), gate_up.reshape(8 * shard, 8 * hidden)
+    )
+    both = dot(normed_second, w_gate_up, ((1,), (0,)))
+    gate_value, up_value = both[:, : 4 * hidden], both[:, 4 * hidden :]
+    gate_sigmoid = jax.nn.sigmoid(gate_value)
+    silu = gate_value * gate_sigmoid
+    hidden_low = (silu * up_value).astype(bf)
+    grad_hidden = dot(grad_out, w_down, ((1,), (1,)))
+    grad_gate = grad_hidden * up_value * gate_sigmoid * (1.0 + gate_value * (1.0 - gate_sigmoid))
+    grad_both = jnp.concatenate([grad_gate.astype(bf), (grad_hidden * silu).astype(bf)], axis=1)
+    grad_second = dot(grad_both, w_gate_up, ((1,), (1,))).astype(bf)
+    down_partial = dot(hidden_low, grad_out, ((0,), (0,))).astype(bf)
+    grad_second, down_grad = reduce_call(grad_second, down_partial, 3, 1, f32)
+    output = (resid_mid + scatter_blk(dot(hidden_low, w_down, ((1,), (0,))))).astype(bf)
+    gate_up_partial = dot(normed_second, grad_both, ((0,), (0,))).astype(bf)
+
+    mid_part, f_gain_part, f_shift_part = norm_back(grad_second, unit_second, inverse_second, f_gain)
+    grad_mid = cotangent[0].astype(f32) + mid_part
+    grad_mid_low = grad_mid.astype(bf)
+    grad_attended = dot(grad_mid_low, w_out, ((1,), (1,))).astype(bf)
+    grad_mixed, gate_up_grad = attend_backward(
+        grad_attended, queries, keys, values, attended, log_total, start, tables, gate_up_partial
+    )
+    out_grad = lax.psum_scatter(
+        dot(attended_low, grad_mid_low, ((0,), (0,))).astype(bf), BOTH, scatter_dimension=0, tiled=True
+    ).astype(f32)
+    grad_first = dot(grad_mixed, w_project, ((1,), (1,))).astype(bf)
+    project_partial = dot(normed_first, grad_mixed, ((0,), (0,))).astype(bf)
+    grad_first, project_grad = reduce_call(grad_first, project_partial, 5, 0, bf)
+    unit_first, inverse_first = norm_stats(inputs)
+    input_part, a_gain_part, a_shift_part = norm_back(grad_first, unit_first, inverse_first, a_gain)
+    grad_tokens = grad_mid + input_part
+
+    bias_part = jnp.sum(grad_mixed.astype(f32), axis=0).reshape(3, 1, local)
+    bias_part = jnp.where(jnp.arange(8)[None, :, None] == b, bias_part, 0.0)
+    bias_part = jnp.pad(bias_part.reshape(32, 3 * shard), ((0, 0), (0, 64))).reshape(32, 2, 128)
+    gains = jnp.stack(
+        [part.reshape(32, shard) for part in (a_gain_part, a_shift_part, f_gain_part, f_shift_part)], axis=1
+    )
+    gains = jnp.pad(gains, ((0, 0), (0, 0), (0, 64)))
+    sums = jnp.concatenate([gains, bias_part, jnp.zeros((32, 2, 128), f32)], axis=1)
+    sums = sums.reshape(4, 8, 8, 128).transpose(1, 0, 2, 3)
+    project_grad, gate_up_grad, vector = owners_call(
+        project_grad.reshape(8, shard, 3 * local), gate_up_grad.reshape(8, shard, 8 * hidden), sums
+    )
+
+    def owned(pieces, parts):
+        inner = pieces.shape[2] // parts
+        pieces = pieces.reshape(8, shard, parts, inner).transpose(1, 2, 0, 3)
+        return pieces.reshape(shard, 8 * parts * inner).astype(f32)
+
+    return (
+        output[None], grad_tokens[None], vector[0, :shard], vector[1, :shard],
+        owned(project_grad, 3), vector[4:6].reshape(-1)[: 3 * shard], out_grad,
+        vector[2, :shard], vector[3, :shard],
+        owned(gate_up_grad[:, :, : 4 * hidden], 4), owned(gate_up_grad[:, :, 4 * hidden :], 4), down_grad,
+    )
+
+
 def solution(mesh):
     tokens = P("rows", "blk", None)
     vector, matrix = P(BOTH), P(BOTH, None)
@@ -288,5 +1212,8 @@
     out_specs = (
         tokens, tokens, vector, vector, matrix, vector, matrix, vector, vector, matrix, matrix, matrix,
     )
-    body = make_body(mesh.shape["rows"], mesh.shape["blk"])
+    if (mesh.shape["rows"], mesh.shape["blk"]) == (4, 8):
+        body = fast_body
+    else:
+        body = make_body(mesh.shape["rows"], mesh.shape["blk"])
     return jax.shard_map(body, mesh=mesh, in_specs=in_specs, out_specs=out_specs, check_vma=False)

time: 974 us -> 714 us (0.73)
  the two profiles are of different devices: /device:TPU:0 before, /device:TPU:16 now
where the time goes in v2:
time: 714 us; the launch traced here: 705 us
  Pallas kernels  525 us (74%)
  matrix products  89 us (12%)
  local copies, waits for them, and re-layouts  52.1 us (7%)
  other arithmetic  22.7 us (3%)
  between operations  14.6 us (2%)
    pallas_call x7, Pallas kernels, call(): pl.pallas_call(kernel, out_shape=[jax.ShapeDtypeStruct(shape, kind) for s...  525 us
    dot_general x11, matrix products, dot(): lax.dot_general(left, right, (contract, ((), ())), preferred_element_type...  89 us
    convert_element_type x8, local copies, waits for them, and re-layouts, owned(): return pieces.reshape(shard, 8 * parts * inner).astype(f32)  28 us
  transfers between devices with their start and end apart: 4, of which 0 were waited for; matrix products, arithmetic and copies ran while one was open for 19% of the time, Pallas kernels for 74%

profile of v2, /device:TPU:16, one launch (start us, length us, event | category | flops | bytes accessed | tf_op | source)
XLA Modules:
  0.0 705.3 jit_solution(10129305956783171444)
XLA Ops:
  9.4 3.0 reshape.217
  13.8 3.0 reshape.219
  19.9 94.3 %shard_map.220 = (bf16[32,16,128]{2,1,0:T(8,128)(2,1)}, bf16[1024,2048]{1,0:T(8,128)(2,1)}, bf16[512,768]{1,0:T(8,128)(2,1)}, bf16[2048,768]{1,0:T(8,128)(2,1)}, bf16[704,2048]{1,0:T(8,128)(2,1)}) custom-call(bf16[128,2048]{1,0:T(8,128)(2,1)} %bitcast.110, bf16[16,128]{1,0:T(8,128)(2,1)} %maximum_maximum_fusion.refs_1_, bf16[64,6144]{1,0:T(8,128)(2,1)} %refs_2_.1, ...), custom_call_target="tpu_custom_call" | custom-call | tf_op jit(solution)/shard_map/pallas_call | solution.py:670
  118.6 1.9 multiply_sine_fusion
  124.1 1.9 concatenate.41
  127.6 76.7 %shard_map.221 = (bf16[1024,256]{1,0:T(8,128)(2,1)}, bf16[1024,256]{1,0:T(8,128)(2,1)}, bf16[1024,256]{1,0:T(8,128)(2,1)}, f32[1024,256]{1,0:T(8,128)}, f32[1024...) custom-call(bf16[1024,2048]{1,0:T(8,128)(2,1)} %get-tuple-element.34.refs_0_, ...), custom_call_target="tpu_custom_call" | custom-call | tf_op jit(solution)/shard_map/pallas_call | solution.py:670
  204.4 4.9 fusion.31
  210.7 69.7 %shard_map.222 = (bf16[1024,2048]{1,0:T(8,128)(2,1)}, bf16[2048,1408]{1,0:T(8,128)(2,1)}) custom-call(bf16[128,2048]{1,0:T(8,128)(2,1)} %add_convert_fusion.1.refs_0_, bf16[512,1408]{1,0:T(8,128)(2,1)} %bitcast.125), custom_call_target="tpu_custom_call" | custom-call | tf_op jit(solution)/shard_map/pallas_call | solution.py:670
  280.4 11.9 %fusion.32 = f32[1024,1408]{1,0:T(8,128)} fusion(bf16[1024,2048]{1,0:T(8,128)(2,1)} %get-tuple-element.39, bf16[2048,1408]{1,0:T(8,128)(2,1)} %get-tuple-element.40), kind=kOutput, calls=%fused_computation.99 | convolution fusion | flops 5905580032 | bytes 15728640 | tf_op jit(solution)/shard_map/dot_general | solution.py:21
  292.3 10.8 %fusion.9 = (bf16[1024,704]{1,0:T(8,128)(2,1)}, bf16[1024,704]{1,0:T(8,128)(2,1)}, bf16[1024,704]{1,0:T(8,128)(2,1)S(1)}) fusion(f32[1024,1408]{1,0:T(8,128)} %fusion.32, bf16[704,2048]{1,0:T(8,128)(2,1)} %get-tuple-element.41, bf16[1,1024,2048]{2,1,0:T(8,128)(2,1)} %all-gather.6.cloned.1.call-done), kind=kOutput, calls=%fused_computation.16 | convolution fusion | flops 2963603456 | bytes 17170432 | tf_op jit(solution)/shard_map/dot_general | solution.py:21
  304.3 5.0 convolution_convert_fusion.3
  309.3 7.6 %fusion.4.refs_1_ = bf16[704,2048]{1,0:T(8,128)(2,1)} fusion(bf16[1024,704]{1,0:T(8,128)(2,1)} %copy-done.14, bf16[1,1024,2048]{2,1,0:T(8,128)(2,1)} %all-gather.6.cloned.1.call-done), kind=kOutput, calls=%fused_computation.11 | convolution fusion | flops 2954231808 | bytes 8519680 | tf_op jit(solution)/shard_map/dot_general | solution.py:21
  316.9 11.7 %convolution_convert_fusion.2.refs_0_ = bf16[1024,2048]{1,0:T(8,128)(2,1)} fusion(bf16[2048,1408]{1,0:T(8,128)(2,1)} %get-tuple-element.40, bf16[1024,704]{1,0:T(8,128)(2,1)S(1)} %copy-done.16, bf16[1024,704]{1,0:T(8,128)(2,1)S(1)} %copy-done.15), kind=kOutput, calls=%fused_computation.7 | convolution fusion | flops 5913444352 | bytes 12845056 | tf_op jit(solution)/shard_map/dot_general | solution.py:21
  328.6 74.8 %shard_map.223 = (f32[128,2048]{1,0:T(8,128)}, f32[176,2048]{1,0:T(8,128)}) custom-call(bf16[1024,2048]{1,0:T(8,128)(2,1)} %convolution_convert_fusion.2.refs_0_, bf16[704,2048]{1,0:T(8,128)(2,1)} %fusion.4.refs_1_), custom_call_target="tpu_custom_call" | custom-call | tf_op jit(solution)/shard_map/pallas_call | solution.py:670
  405.2 2.9 convert_add_fusion
  408.1 5.6 convolution_convert_fusion.1
  414.4 11.4 %convolution_convert_fusion.refs_10_ = bf16[2048,1408]{1,0:T(8,128)(2,1)} fusion(bf16[1024,2048]{1,0:T(8,128)(2,1)} %get-tuple-element.39, bf16[1024,704]{1,0:T(8,128)(2,1)} %get-tuple-element.65, bf16[1024,704]{1,0:T(8,128)(2,1)} %get-tuple-element.64), kind=kOutput, calls=%fused_computation | convolution fusion | flops 5914230784 | bytes 12845056 | tf_op jit(solution)/shard_map/dot_general | solution.py:21
  425.8 7.1 %convolution_convert_fusion.6.refs_0_ = bf16[128,2048]{1,0:T(8,128)(2,1)} fusion(bf16[2048,2048]{1,0:T(8,128)(2,1)} %all-gather.4.cloned.1.call-done, f32[128,2048]{1,0:T(8,128)S(1)} %get-tuple-element.69), kind=kOutput, calls=%fused_computation.24 | convolution fusion | flops 1074266112 | bytes 9961472 | tf_op jit(solution)/shard_map/dot_general | solution.py:21
  433.0 61.0 %shard_map.224 = (bf16[1024,768]{1,0:T(8,128)(2,1)}, bf16[512,1408]{1,0:T(8,128)(2,1)}) custom-call(bf16[128,2048]{1,0:T(8,128)(2,1)} %convolution_convert_fusion.6.refs_0_, bf16[1024,256]{1,0:T(8,128)(2,1)} %get-tuple-element.43.refs_1_, bf16[1024,256]{1,0:T(8,128)(2,1)} %get-tuple-element.44.refs_2_, bf16[1024,256]{1,0:T(8,128)(2,1)} %get-tuple-element.45.refs_3_, ...), custom_call_target="tpu_custom_call" | custom-call | tf_op jit(solution)/shard_map/pallas_call | solution.py:670
  495.7 7.9 %convolution_convert_fusion.4.refs_0_ = bf16[1024,2048]{1,0:T(8,128)(2,1)} fusion(bf16[1024,768]{1,0:T(8,128)(2,1)} %get-tuple-element.48, bf16[2048,768]{1,0:T(8,128)(2,1)} %get-tuple-element.35.refs_1_), kind=kOutput, calls=%fused_computation.9 | convolution fusion | flops 3223322624 | bytes 8912896 | tf_op jit(solution)/shard_map/dot_general | solution.py:21
  503.7 5.0 convolution_convert_fusion.5.refs_1_
  508.7 92.8 %shard_map.225 = (f32[128,2048]{1,0:T(8,128)}, bf16[512,768]{1,0:T(8,128)(2,1)}) custom-call(bf16[1024,2048]{1,0:T(8,128)(2,1)} %convolution_convert_fusion.4.refs_0_, bf16[2048,768]{1,0:T(8,128)(2,1)} %convolution_convert_fusion.5.refs_1_), custom_call_target="tpu_custom_call" | custom-call | tf_op jit(solution)/shard_map/pallas_call | solution.py:670
  604.3 55.9 %shard_map.226 = (bf16[8,64,768]{2,1,0:T(8,128)(2,1)}, bf16[8,64,1408]{2,1,0:T(8,128)(2,1)}, f32[8,128]{1,0:T(8,128)}) custom-call(bf16[8,64,768]{2,1,0:T(8,128)(2,1)} %bitcast.126, bf16[8,64,1408]{2,1,0:T(8,128)(2,1)} %bitcast.124, f32[8,4,8,128]{3,2,1,0:T(8,128)} %maximum_bitcast_fusion.refs_2_), custom_call_target="tpu_custom_call" | custom-call | tf_op jit(solution)/shard_map/pallas_call | solution.py:670
  660.2 3.6 reshape.233
  663.8 2.6 copy.68
  669.7 4.0 reshape.235
  673.7 4.1 copy.70
  677.8 3.3 reshape.232
  681.1 2.9 reshape.234
  684.0 4.2 copy.69
  688.2 3.3 reshape.231
  695.8 2.6 copy.81
  (112 shorter events, 33.1 us)
Async XLA Ops:
  7.2 197.2 %all-gather.4.cloned.1.call-start = ((), (), s32[]{:S(2)}) async-start(), calls=%async_computation.2 | async-start | bytes 8650752 | tf_op jit(solution)/shard_map/all_gather | solution.py:1107
  7.9 284.4 %all-gather.6.cloned.1.call-start = ((), (), s32[]{:S(2)}) async-start(), calls=%async_computation.5 | async-start | bytes 4718592 | tf_op jit(solution)/shard_map/all_gather | solution.py:57
  8.7 396.5 %reduce-scatter.3.cloned.1.call-start = ((), (), s32[]{:S(2)}) async-start(), calls=%async_computation.3 | async-start | bytes 4718592 | tf_op jit(solution)/shard_map/reduce_scatter | solution.py:61
  13.7 5.4 copy-start.13
  13.8 5.4 copy-start.8
  13.8 5.4 copy-start.9
  13.8 5.4 copy-start.10
  13.8 5.4 copy-start.11
  124.1 1.9 copy-start.4
  127.6 76.8 %copy-start = (bf16[1,128,2048]{2,1,0:T(8,128)(2,1)S(1)}, bf16[1,128,2048]{2,1,0:T(8,128)(2,1)}, u32[]{:S(2)}) copy-start(bf16[1,128,2048]{2,1,0:T(8,128)(2,1)} %param.13) | copy-start | bytes 1572868
  292.3 12.0 %copy-start.12 = (bf16[704,2048]{1,0:T(8,128)(2,1)S(1)}, bf16[704,2048]{1,0:T(8,128)(2,1)}, u32[]{:S(2)}) copy-start(bf16[704,2048]{1,0:T(8,128)(2,1)} %get-tuple-element.41) | copy-start | bytes 8650756
  303.1 1.1 copy-start.14
  309.3 384.7 %reduce-scatter.5.cloned.1.call-start = ((), (), s32[]{:S(2)}) async-start(), calls=%async_computation.4 | async-start | bytes 8650752 | tf_op jit(solution)/shard_map/reduce_scatter | solution.py:1169
  309.3 7.6 %copy-start.15 = (bf16[1024,704]{1,0:T(8,128)(2,1)S(1)}, bf16[1024,704]{1,0:T(8,128)(2,1)}, u32[]{:S(2)}) copy-start(bf16[1024,704]{1,0:T(8,128)(2,1)} %get-tuple-element.64) | copy-start | bytes 4325380
  309.3 7.6 %copy-start.16 = (bf16[1024,704]{1,0:T(8,128)(2,1)S(1)}, bf16[1024,704]{1,0:T(8,128)(2,1)}, u32[]{:S(2)}) copy-start(bf16[1024,704]{1,0:T(8,128)(2,1)} %get-tuple-element.65) | copy-start | bytes 4325380
  403.4 4.6 copy-start.1
  495.7 7.9 %copy-start.2 = (bf16[1024,2048]{1,0:T(8,128)(2,1)S(1)}, bf16[1024,2048]{1,0:T(8,128)(2,1)}, u32[]{:S(2)}) copy-start(bf16[1024,2048]{1,0:T(8,128)(2,1)} %get-tuple-element.34.refs_0_) | copy-start | bytes 12582916
  495.7 7.9 %copy-start.6 = (bf16[1024,768]{1,0:T(8,128)(2,1)S(1)}, bf16[1024,768]{1,0:T(8,128)(2,1)}, u32[]{:S(2)}) copy-start(bf16[1024,768]{1,0:T(8,128)(2,1)} %get-tuple-element.48) | copy-start | bytes 4718596
  663.8 4.2 copy-start.5
  684.0 7.5 %copy-start.7 = (f32[8,128]{1,0:T(8,128)S(1)}, f32[8,128]{1,0:T(8,128)}, u32[]{:S(2)}) copy-start(f32[8,128]{1,0:T(8,128)} %get-tuple-element.52) | copy-start | bytes 12292
  684.0 8.6 %copy-start.3 = (f32[128,2048]{1,0:T(8,128)S(1)}, f32[128,2048]{1,0:T(8,128)}, u32[]{:S(2)}) copy-start(f32[128,2048]{1,0:T(8,128)} %get-tuple-element.49) | copy-start | bytes 3145732
Sparse Core Ops, SparseCore 0:
  11.0 102.6 all-gather.3
  115.3 76.7 all-gather.5
  309.4 60.8 reduce-scatter.2
  413.8 148.7 reduce-scatter.4

commit v3 on v2

--- a/solution.py
+++ b/solution.py
@@ -330,92 +330,107 @@
 
 
 def line_gather_sems():
-    return [DMA((4, CHUNKS))] * 4 + [DMA((7, CHUNKS))] * 2 + [DMA]
-
-
-def line_gather(at, own, full, sems):
+    return [DMA((4, CHUNKS))] * 4 + [DMA((7, CHUNKS))] * 2 + [DMA((CHUNKS,))]
+
+
+def line_gather(at, own, spot, sems, paired=True):
     up_send, down_send, up_recv, down_recv, pair_send, pair_recv, local_sem = sems
-    count = own.shape[0]
-    size = count // CHUNKS
-
-    def rows(device, k):
-        return full.at[pl.ds(pl.multiple_of(device * count + k * size, size), size)]
 
     def up(d, k, src):
-        return remote(src, rows(at.b - 2 * d, k), up_send.at[d, k], up_recv.at[d, k], at.r, at.b + 2)
+        return remote(
+            src, spot(at.z - d, at.c, k), up_send.at[d, k], up_recv.at[d, k], at.r, at.b + 2
+        )
 
     def down(d, k, src):
         return remote(
-            src, rows(at.b + 2 * d, k), down_send.at[d, k], down_recv.at[d, k], at.r, at.b - 2
+            src, spot(at.z + d, at.c, k), down_send.at[d, k], down_recv.at[d, k], at.r, at.b - 2
         )
 
     def up_in(d, k):
-        piece = rows(at.b - 2 * d - 2, k)
+        piece = spot(at.z - d - 1, at.c, k)
         return remote(piece, piece, up_send.at[d, k], up_recv.at[d, k], at.r, at.b + 2)
 
     def down_in(d, k):
-        piece = rows(at.b + 2 * d + 2, k)
+        piece = spot(at.z + d + 1, at.c, k)
         return remote(piece, piece, down_send.at[d, k], down_recv.at[d, k], at.r, at.b - 2)
 
-    def pair(i, k, device, src):
-        return remote(src, rows(device, k), pair_send.at[i, k], pair_recv.at[i, k], at.r, at.sibling)
-
-    def pair_in(i, k, device):
-        piece = rows(device, k)
+    def pair(i, k, z, src):
+        return remote(
+            src, spot(z, at.c, k), pair_send.at[i, k], pair_recv.at[i, k], at.r, at.sibling
+        )
+
+    def pair_in(i, k, z):
+        piece = spot(z, 1 - at.c, k)
         return remote(piece, piece, pair_send.at[i, k], pair_recv.at[i, k], at.r, at.sibling)
 
-    local = pltpu.make_async_copy(own, full.at[pl.ds(at.b * count, count)], local_sem)
-    local.start()
+    locals_ = [
+        pltpu.make_async_copy(own(k), spot(at.z, at.c, k), local_sem.at[k]) for k in range(CHUNKS)
+    ]
     for k in range(CHUNKS):
-        src = own.at[pl.ds(k * size, size)]
-        pl.when(at.z < 3)(lambda: up(0, k, src).start())
-        pl.when(at.z > 0)(lambda: down(0, k, src).start())
-        pair(0, k, at.b, src).start()
+        locals_[k].start()
+        pl.when(at.z < 3)(lambda: up(0, k, own(k)).start())
+        pl.when(at.z > 0)(lambda: down(0, k, own(k)).start())
+        if paired:
+            pair(0, k, at.z, own(k)).start()
     yield
     for d in range(3):
         for k in range(CHUNKS):
 
             @pl.when(at.z - 1 - d >= 0)
             def _():
-                device = at.b - 2 * d - 2
+                z = at.z - 1 - d
                 up_in(d, k).wait_recv()
                 if d < 2:
-                    pl.when(at.z < 3)(lambda: up(d + 1, k, rows(device, k)).start())
-                pair(1 + d, k, device, rows(device, k)).start()
+                    pl.when(at.z < 3)(lambda: up(d + 1, k, spot(z, at.c, k)).start())
+                if paired:
+                    pair(1 + d, k, z, spot(z, at.c, k)).start()
 
             @pl.when(at.z + 1 + d <= 3)
             def _():
-                device = at.b + 2 * d + 2
+                z = at.z + 1 + d
                 down_in(d, k).wait_recv()
                 if d < 2:
-                    pl.when(at.z > 0)(lambda: down(d + 1, k, rows(device, k)).start())
-                pair(4 + d, k, device, rows(device, k)).start()
+                    pl.when(at.z > 0)(lambda: down(d + 1, k, spot(z, at.c, k)).start())
+                if paired:
+                    pair(4 + d, k, z, spot(z, at.c, k)).start()
 
             yield
-    local.wait()
     for k in range(CHUNKS):
-        src = own.at[pl.ds(k * size, size)]
-        pair(0, k, at.b, src).wait_send()
-        pair_in(0, k, at.sibling).wait_recv()
-        pl.when(at.z < 3)(lambda: up(0, k, src).wait_send())
-        pl.when(at.z > 0)(lambda: down(0, k, src).wait_send())
+        locals_[k].wait()
+        if paired:
+            pair(0, k, at.z, own(k)).wait_send()
+            pair_in(0, k, at.z).wait_recv()
+        pl.when(at.z < 3)(lambda: up(0, k, own(k)).wait_send())
+        pl.when(at.z > 0)(lambda: down(0, k, own(k)).wait_send())
         for d in range(3):
 
             @pl.when(at.z - 1 - d >= 0)
             def _():
-                device = at.b - 2 * d - 2
-                pair(1 + d, k, device, rows(device, k)).wait_send()
-                pair_in(1 + d, k, at.sibling - 2 * d - 2).wait_recv()
+                z = at.z - 1 - d
+                if paired:
+                    pair(1 + d, k, z, spot(z, at.c, k)).wait_send()
+                    pair_in(1 + d, k, z).wait_recv()
                 if d < 2:
-                    pl.when(at.z < 3)(lambda: up(d + 1, k, rows(device, k)).wait_send())
+                    pl.when(at.z < 3)(lambda: up(d + 1, k, spot(z, at.c, k)).wait_send())
 
             @pl.when(at.z + 1 + d <= 3)
             def _():
-                device = at.b + 2 * d + 2
-                pair(4 + d, k, device, rows(device, k)).wait_send()
-                pair_in(4 + d, k, at.sibling + 2 * d + 2).wait_recv()
+                z = at.z + 1 + d
+                if paired:
+                    pair(4 + d, k, z, spot(z, at.c, k)).wait_send()
+                    pair_in(4 + d, k, z).wait_recv()
                 if d < 2:
-                    pl.when(at.z > 0)(lambda: down(d + 1, k, rows(device, k)).wait_send())
+                    pl.when(at.z > 0)(lambda: down(d + 1, k, spot(z, at.c, k)).wait_send())
+
+
+def rows_of(ref, count):
+    size = count // CHUNKS
+    return lambda z, c, k: ref.at[pl.ds(pl.multiple_of((2 * z + c) * count + k * size, size), size)]
+
+
+def cuts_of(ref):
+    size = ref.shape[0] // CHUNKS
+    return lambda k: ref.at[pl.ds(k * size, size)]
 
 
 def line_scatter_scratch(count, width):
@@ -424,7 +439,7 @@
     return [block, arrive, arrive] + [DMA((4, CHUNKS))] * 2 + [DMA((3, CHUNKS))] * 4
 
 
-def line_scatter(at, partial, result, scratch):
+def line_scatter(at, block, result, scratch, paired=True):
     held, from_below, from_above, pair_send, pair_recv, up_send, up_recv, down_send, down_recv = scratch
     count = held.shape[1]
     size = count // CHUNKS
@@ -432,12 +447,9 @@
     def cut(k):
         return pl.ds(k * size, size)
 
-    def block(z, c, k):
-        return pl.ds(pl.multiple_of((2 * z + c) * count + k * size, size), size)
-
     def pair(z, k):
         return remote(
-            partial.at[block(z, 1 - at.c, k)],
+            block(z, 1 - at.c, k),
             held.at[z, cut(k)],
             pair_send.at[z, k],
             pair_recv.at[z, k],
@@ -469,11 +481,13 @@
         return ref[...].astype(jnp.float32)
 
     def own(z, k):
-        return wide(partial.at[block(z, at.c, k)]) + wide(held.at[z, cut(k)])
-
-    for z in (3, 0, 2, 1):
-        for k in range(CHUNKS):
-            pair(z, k).start()
+        mine = wide(block(z, at.c, k))
+        return mine + wide(held.at[z, cut(k)]) if paired else mine
+
+    if paired:
+        for z in (3, 0, 2, 1):
+            for k in range(CHUNKS):
+                pair(z, k).start()
     yield
     for step in range(3):
         for k in range(CHUNKS):
@@ -481,7 +495,8 @@
 
             @pl.when(at.z < far)
             def _():
-                pair(far, k).wait_recv()
+                if paired:
+                    pair(far, k).wait_recv()
 
                 @pl.when(at.z == 0)
                 def _():
@@ -498,7 +513,8 @@
 
             @pl.when(at.z > near)
             def _():
-                pair(near, k).wait_recv()
+                if paired:
+                    pair(near, k).wait_recv()
 
                 @pl.when(at.z == 3)
                 def _():
@@ -519,7 +535,8 @@
 
             @pl.when(at.z == z)
             def _():
-                pair(z, k).wait_recv()
+                if paired:
+                    pair(z, k).wait_recv()
                 total = own(z, k)
                 if z > 0:
                     up(z, k).wait_recv()
@@ -531,7 +548,8 @@
 
     for z in range(4):
         for k in range(CHUNKS):
-            pair(z, k).wait_send()
+            if paired:
+                pair(z, k).wait_send()
             if z > 0:
                 pl.when(at.z < z)(lambda: up(z, k).wait_send())
             if z < 3:
@@ -543,48 +561,51 @@
     return ref.at[pl.ds(which * size, size)] if axis == 0 else ref.at[:, pl.ds(which * size, size)]
 
 
+def row_halves(ref, axis=0):
+    count = ref.shape[0] // 4
+    return lambda r, which: half_of(
+        ref.at[pl.ds(pl.multiple_of(r * count, count), count)], axis, which
+    )
+
+
 def square_gather_sems():
-    return [DMA((6,)), DMA((6,)), DMA]
-
-
-def square_gather(at, own, full, sems, axis=0):
+    return [DMA((6,)), DMA((6,)), DMA((2,))]
+
+
+def square_gather(at, own, spot, sems):
     send, recv, local_sem = sems
-    count = own.shape[0]
-
-    def part(r, which):
-        return half_of(full.at[pl.ds(pl.multiple_of(r * count, count), count)], axis, which)
 
     def copy(i, src, r_of, which, to):
-        return remote(src, part(r_of, which), send.at[i], recv.at[i], to, at.b)
+        return remote(src, spot(r_of, which), send.at[i], recv.at[i], to, at.b)
 
     outs = [
-        copy(0, half_of(own, axis, 0), at.r, 0, at.rx),
-        copy(1, half_of(own, axis, 1), at.r, 1, at.ry),
-        copy(2, half_of(own, axis, 1), at.r, 1, at.rx),
-        copy(3, half_of(own, axis, 0), at.r, 0, at.ry),
+        copy(0, own(0), at.r, 0, at.rx),
+        copy(1, own(1), at.r, 1, at.ry),
+        copy(2, own(1), at.r, 1, at.rx),
+        copy(3, own(0), at.r, 0, at.ry),
     ]
     ins = [
-        copy(0, part(at.rx, 0), at.rx, 0, at.rx),
-        copy(1, part(at.ry, 1), at.ry, 1, at.ry),
-        copy(2, part(at.rx, 1), at.rx, 1, at.rx),
-        copy(3, part(at.ry, 0), at.ry, 0, at.ry),
-        copy(4, part(at.rd, 0), at.rd, 0, at.ry),
-        copy(5, part(at.rd, 1), at.rd, 1, at.rx),
+        copy(0, spot(at.rx, 0), at.rx, 0, at.rx),
+        copy(1, spot(at.ry, 1), at.ry, 1, at.ry),
+        copy(2, spot(at.rx, 1), at.rx, 1, at.rx),
+        copy(3, spot(at.ry, 0), at.ry, 0, at.ry),
+        copy(4, spot(at.rd, 0), at.rd, 0, at.ry),
+        copy(5, spot(at.rd, 1), at.rd, 1, at.rx),
     ]
-    local = pltpu.make_async_copy(own, full.at[pl.ds(at.r * count, count)], local_sem)
-    local.start()
-    for out in outs:
-        out.start()
+    locals_ = [pltpu.make_async_copy(own(h), spot(at.r, h), local_sem.at[h]) for h in range(2)]
+    for copy_ in outs + locals_:
+        copy_.start()
     yield
     ins[0].wait_recv()
-    outs.append(copy(4, part(at.rx, 0), at.rx, 0, at.ry))
+    outs.append(copy(4, spot(at.rx, 0), at.rx, 0, at.ry))
     outs[4].start()
     yield
     ins[1].wait_recv()
-    outs.append(copy(5, part(at.ry, 1), at.ry, 1, at.rx))
+    outs.append(copy(5, spot(at.ry, 1), at.ry, 1, at.rx))
     outs[5].start()
     yield
-    local.wait()
+    for copy_ in locals_:
+        copy_.wait()
     for i in (2, 3, 4, 5):
         ins[i].wait_recv()
     for out in outs:
@@ -598,12 +619,9 @@
     return [piece, piece, part, part, part, part, DMA((6,)), DMA((6,))]
 
 
-def square_scatter(at, partial, result, scratch, axis=0):
+def square_scatter(at, part, result, scratch, axis=0, prepare=None):
     from_x, from_y, far_x, far_y, out_x, out_y, send, recv = scratch
-    count = from_x.shape[0]
-
-    def part(r, which):
-        return half_of(partial.at[pl.ds(pl.multiple_of(r * count, count), count)], axis, which)
+    prepare = prepare or (lambda r: None)
 
     def wide(ref):
         return ref[...].astype(jnp.float32)
@@ -616,16 +634,24 @@
         remote(out_y, half_of(from_y, axis, 0), send.at[4], recv.at[4], at.ry, at.b),
         remote(out_x, half_of(from_x, axis, 1), send.at[5], recv.at[5], at.rx, at.b),
     ]
-    for copy in copies[:4]:
-        copy.start()
+    prepare(at.rd)
+    copies[0].start()
+    copies[1].start()
+    yield
+    prepare(at.rx)
+    copies[2].start()
+    yield
+    prepare(at.ry)
+    copies[3].start()
     yield
     copies[0].wait_recv()
     out_y[...] = (wide(part(at.ry, 0)) + wide(far_x)).astype(jnp.bfloat16)
     copies[4].start()
-    yield
     copies[1].wait_recv()
     out_x[...] = (wide(part(at.rx, 1)) + wide(far_y)).astype(jnp.bfloat16)
     copies[5].start()
+    yield
+    prepare(at.r)
     yield
     for i in (2, 3, 4, 5):
         copies[i].wait_recv()
@@ -710,10 +736,42 @@
         out.wait_send()
 
 
+def make_tables(at, vectors, start, cosine, minus, plus):
+    docs = jnp.concatenate(
+        [vectors[8 * at.r + j, 6:7].astype(jnp.float32) for j in range(8)], axis=0
+    )
+    begins = jnp.zeros_like(docs)
+    for doc in range(1, 5):
+        before = jnp.sum((docs < doc).astype(jnp.float32), axis=(0, 1), keepdims=True)
+        begins = jnp.where(docs == doc, before, begins)
+    index = lax.broadcasted_iota(jnp.int32, docs.shape, 0) * 128
+    index = (index + lax.broadcasted_iota(jnp.int32, docs.shape, 1)).astype(jnp.float32)
+    places = index - begins
+    half = ROT // 2
+    row = lax.broadcasted_iota(jnp.int32, (half, 128), 0)
+    frequency = jnp.zeros((half, 128), jnp.float32)
+    for j in range(half):
+        frequency = jnp.where(row == j, rotary_base ** (-j / half), frequency)
+    eight = jnp.zeros((half, 128), jnp.float32)
+    gap = jnp.zeros((48, 128), jnp.float32)
+    for j in range(8):
+        rows = slice(j * 128, j * 128 + 128)
+        angles = frequency * places[j : j + 1]
+        cos, sin = jnp.cos(angles), jnp.sin(angles)
+
+        def table(first, second, rest):
+            return jnp.transpose(jnp.concatenate([first, second, rest] * 2, axis=0))
+
+        cosine[rows] = table(cos, cos, gap + 1.0)
+        minus[rows] = table(-sin, eight, gap)
+        plus[rows] = table(eight, sin, gap)
+        start[rows] = jnp.transpose(jnp.broadcast_to(begins[j : j + 1], (128, 128))).astype(jnp.int32)
+
+
 def start_kernel(
-    x_ref, vector_ref, project_ref, down_ref,
-    vectors, normed, pieces, w_project, w_down,
-    unit, own, vector_sems, exchange_sem, square_sem, down_sem, line_sems,
+    x_ref, vector_ref, project_ref, down_ref, out_ref, gate_ref, up_ref,
+    vectors, normed, pieces, w_project, w_down, w_out, gate_up, start, cosine, minus, plus,
+    unit, own, vector_sems, exchange_sem, square_sem, down_sem, line_sems, out_sems,
 ):
     at = Place()
     at.barrier(diagonal=True)
@@ -732,7 +790,9 @@
         3,
     )
     next(project_job)
-    down_job = square_gather(at, down_ref, w_down, down_sem, axis=1)
+    down_job = square_gather(
+        at, lambda half: half_of(down_ref, 1, half), row_halves(w_down, 1), down_sem
+    )
     next(down_job)
     x = x_ref[...].astype(jnp.float32)
     centered = x - jnp.mean(x, axis=1, keepdims=True)
@@ -742,11 +802,26 @@
         lanes = slice(tile * 128, tile * 128 + 128)
         both = vectors[2 * tile].astype(jnp.float32) + vectors[2 * tile + 1].astype(jnp.float32)
         own[:, lanes] = (unit[:, lanes] * both[0:1] + both[1:2]).astype(jnp.bfloat16)
-    line_job = line_gather(at, own, normed, line_sems)
+    line_job = line_gather(at, cuts_of(own), rows_of(normed, own.shape[0]), line_sems)
     next(line_job)
+    size = depth // CHUNKS
+    out_job = line_gather(
+        at, cuts_of(out_ref), lambda z, c, k: w_out.at[z, pl.ds(k * size, size)], out_sems, False
+    )
+    next(out_job)
+    hidden = down_ref.shape[0]
+    for b in range(8):
+        for r in range(4):
+            source = slice((8 * r + b) * hidden, (8 * r + b + 1) * hidden)
+            gate_up[b, :, r * hidden : (r + 1) * hidden] = gate_ref[:, source]
+            gate_up[b, :, (4 + r) * hidden : (5 + r) * hidden] = up_ref[:, source]
     drive(project_job)
-    square_job = square_gather(at, pieces, w_project, square_sem)
-    drive(square_job, line_job, down_job)
+    square_job = square_gather(
+        at, lambda half: half_of(pieces, 0, half), row_halves(w_project), square_sem
+    )
+    next(square_job)
+    make_tables(at, vectors, start, cosine, minus, plus)
+    drive(square_job, line_job, down_job, out_job)
 
 
 def pack_sems(groups):
@@ -765,25 +840,28 @@
     return run
 
 
-def start_call(x, vector, project, down):
+def start_call(x, vector, project, down, out_weight, gate, up):
     rows, width = x.shape
     depth = project.shape[0]
     inner = project.shape[1] // 8
-    bf = jnp.bfloat16
+    bf, f32 = jnp.bfloat16, jnp.float32
     groups = [
         [DMA((10,)), DMA((10,)), DMA], exchange_sems(3), square_gather_sems(), square_gather_sems(),
-        line_gather_sems(),
+        line_gather_sems(), line_gather_sems(),
     ]
     flat, spans = pack_sems(groups)
     outs = [
         ((32, 16, 128), bf, VMEM), ((8 * rows, width), bf, HBM), ((8 * depth, inner), bf, HBM),
         ((32 * depth, inner), bf, HBM), ((4 * down.shape[0], width), bf, HBM),
-    ]
-    scratch = [VMEM((rows, width), jnp.float32), VMEM((rows, width), bf)] + flat
-    vectors, normed, _, w_project, w_down = call(
-        grouped(start_kernel, 11, spans), [VMEM, VMEM, HBM, HBM], outs, scratch, 0, x, vector, project, down
-    )
-    return vectors, normed, w_project, w_down
+        ((4, depth, width), bf, HBM), ((8, depth, 8 * down.shape[0]), bf, VMEM),
+        ((8 * rows, 128), jnp.int32, VMEM),
+    ] + [((8 * rows, 128), f32, VMEM)] * 3
+    scratch = [VMEM((rows, width), f32), VMEM((rows, width), bf)] + flat
+    vectors, normed, _, w_project, w_down, w_out, gate_up, start, *tables = call(
+        grouped(start_kernel, 20, spans), [VMEM, VMEM, HBM, HBM, HBM, VMEM, VMEM], outs, scratch, 0,
+        x, vector, project, down, out_weight, gate, up,
+    )
+    return vectors, normed, w_project, w_down, w_out, gate_up, start, tables
 
 
 def turned(columns, cosine, minus, plus):
@@ -805,12 +883,19 @@
 
 
 def attend_forward_kernel(
-    x_ref, w_ref, bias, start, cosine, minus, plus, gate_up,
-    queries, keys, values, attended, log_total, mixed_heads, gate_up_all,
-    low, own_sems, gate_up_sems,
+    x_ref, w_ref, bias, start, cosine, minus, plus, gate_up, out_ref,
+    queries, keys, values, attended, log_total, mixed_heads, gate_up_all, w_out,
+    low, own_sems, gate_up_sems, square_sems, pair_sems,
 ):
     at = Place()
     at.barrier()
+    out_job = square_gather(
+        at,
+        lambda half: half_of(out_ref, 0, half),
+        lambda r, half: w_out.at[r, pl.ds(2 * half, 2), at.c],
+        square_sems,
+    )
+    next(out_job)
     length, local = queries.shape
     depth = gate_up.shape[1]
     gate_up_job = exchange(
@@ -848,7 +933,7 @@
             lanes = pl.ds(pl.multiple_of(pair * 128, 128), 128)
             lane = lax.broadcasted_iota(jnp.int32, (QROWS, 128), 1)
             q, k, v = queries[rows, lanes], keys[:count, lanes], values[:count, lanes]
-            allowed = score_mask(i * QROWS, QROWS, count, start[rows])
+            allowed = score_mask(i * QROWS, QROWS, count, start[rows, 0:1])
             found = []
             for head in range(2):
                 mine = (lane >= 64) if head else (lane < 64)
@@ -865,6 +950,7 @@
             low[rows, lanes] = both.astype(jnp.bfloat16)
             log_total[rows, lanes] = jnp.where(lane < 64, found[0][1], found[1][1])
 
+        next(out_job, None)
         for to in range(i * QROWS // 128, (i + 1) * QROWS // 128):
             pl.when(at.b != to)(lambda: deliver(to).start())
 
@@ -876,6 +962,16 @@
                     local_sem,
                 ).start()
 
+    drive(out_job)
+    pair_send, pair_recv = pair_sems
+    pairs = [
+        remote(
+            w_out.at[r, :, at.c], w_out.at[r, :, at.c], pair_send.at[r], pair_recv.at[r], at.r, at.sibling
+        )
+        for r in range(4)
+    ]
+    for copy in pairs:
+        copy.start()
     for source in range(8):
 
         @pl.when(at.b != source)
@@ -894,63 +990,89 @@
     drive(gate_up_job)
     for to in range(8):
         pl.when(at.b != to)(lambda: deliver(to).wait_send())
-
-
-def attend_forward(x, w, bias, start, tables, gate_up):
+    for r in range(4):
+        theirs = w_out.at[r, :, 1 - at.c]
+        remote(theirs, theirs, pair_send.at[r], pair_recv.at[r], at.r, at.sibling).wait_recv()
+        pairs[r].wait_send()
+
+
+def attend_forward(x, w, bias, start, tables, gate_up, w_out):
     length, local = x.shape[0], w.shape[1] // 3
     bf, f32 = jnp.bfloat16, jnp.float32
-    flat, spans = pack_sems([[DMA((8,)), DMA((8,)), DMA], exchange_sems()])
+    flat, spans = pack_sems(
+        [[DMA((8,)), DMA((8,)), DMA], exchange_sems(), square_gather_sems(), [DMA((4,)), DMA((4,))]]
+    )
     outs = [((length, local), bf, VMEM)] * 3 + [((length, local), f32, VMEM)] * 2
     outs += [((length // 8, 8 * local), bf, VMEM), (gate_up.shape, bf, HBM)]
+    outs += [((4, 4, 2) + w_out.shape[1:], bf, HBM)]
     return call(
-        grouped(attend_forward_kernel, 16, spans), [VMEM] * 7 + [HBM], outs,
-        [VMEM((length, local), bf)] + flat, 1, x, w, bias, start, *tables, gate_up,
-    )
-
-
-def second_gather_kernel(own, gate_up, normed, w_gate_up, line_sems, square_sems):
+        grouped(attend_forward_kernel, 18, spans), [VMEM] * 7 + [HBM, HBM], outs,
+        [VMEM((length, local), bf)] + flat, 1, x, w, bias, start, *tables, gate_up, w_out,
+    )
+
+
+def second_gather_kernel(
+    own, gate_up, cotangent, normed, w_gate_up, grad_out, line_sems, square_sems, other_sems
+):
     at = Place()
     at.barrier()
+    count = own.shape[0]
     drive(
-        line_gather(at, own, normed, line_sems), square_gather(at, gate_up, w_gate_up, square_sems)
-    )
-
-
-def second_gather(own, gate_up):
-    flat, spans = pack_sems([line_gather_sems(), square_gather_sems()])
+        line_gather(at, cuts_of(own), rows_of(normed, count), line_sems),
+        square_gather(at, lambda half: half_of(gate_up, 0, half), row_halves(w_gate_up), square_sems),
+        line_gather(at, cuts_of(cotangent), rows_of(grad_out, count), other_sems),
+    )
+
+
+def second_gather(own, gate_up, cotangent):
+    flat, spans = pack_sems([line_gather_sems(), square_gather_sems(), line_gather_sems()])
     bf = jnp.bfloat16
-    outs = [
-        ((8 * own.shape[0], own.shape[1]), bf, HBM), ((4 * gate_up.shape[0], gate_up.shape[1]), bf, HBM)
-    ]
+    full = ((8 * own.shape[0], own.shape[1]), bf, HBM)
+    outs = [full, ((4 * gate_up.shape[0], gate_up.shape[1]), bf, HBM), full]
     return call(
-        grouped(second_gather_kernel, 4, spans), [HBM, HBM], outs, flat, 2, own, gate_up
-    )
-
-
-def reduce_kernel(axis, partial, weight, result, weight_result, line_scratch, square_scratch):
+        grouped(second_gather_kernel, 6, spans), [HBM] * 3, outs, flat, 2, own, gate_up, cotangent
+    )
+
+
+def feed_reduce_kernel(
+    partial, out_partial, normed, grad_both, result, out_result, weight_result,
+    weight, line_scratch, out_scratch, square_scratch,
+):
     at = Place()
     at.barrier()
+    rows = result.shape[0]
+    depth = weight_result.shape[0]
+    step = depth // 2
+
+    def prepare(r):
+        for half in range(2):
+            spot = pl.ds(pl.multiple_of(r * depth + half * step, step), step)
+            weight[spot] = dot(normed[:, spot], grad_both[...], ((0,), (0,))).astype(jnp.bfloat16)
+
     drive(
-        line_scatter(at, partial, result, line_scratch),
-        square_scatter(at, weight, weight_result, square_scratch, axis),
-    )
-
-
-def reduce_call(partial, weight, number, axis, kind):
+        line_scatter(at, rows_of(partial, rows), result, line_scratch),
+        square_scatter(at, row_halves(weight), weight_result, square_scratch, 0, prepare),
+        line_scatter(at, rows_of(out_partial, rows), out_result, out_scratch),
+    )
+
+
+def feed_reduce(partial, out_partial, normed, grad_both):
     rows, width = partial.shape[0] // 8, partial.shape[1]
-    owned = (weight.shape[0] // 4, weight.shape[1])
-    flat, spans = pack_sems([line_scatter_scratch(rows, width), square_scatter_scratch(*owned, axis)])
-    outs = [((rows, width), jnp.float32, VMEM), (owned, kind, VMEM)]
+    bf, f32 = jnp.bfloat16, jnp.float32
+    owned = (width // 4, grad_both.shape[1])
+    line = line_scatter_scratch(rows, width)
+    flat, spans = pack_sems([line, line, square_scatter_scratch(*owned)])
+    outs = [((rows, width), f32, VMEM)] * 2 + [(owned, bf, VMEM)]
     return call(
-        grouped(functools.partial(reduce_kernel, axis), 4, spans), [VMEM, VMEM], outs, flat, number,
-        partial, weight,
+        grouped(feed_reduce_kernel, 8, spans), [VMEM] * 4, outs,
+        [VMEM((width, owned[1]), bf)] + flat, 3, partial, out_partial, normed, grad_both,
     )
 
 
 def attend_backward_kernel(
-    grad_rows, queries, keys, values, attended, log_total, start, cosine, minus, plus, weight,
-    grad_mixed, weight_result,
-    grad, keys_sum, values_sum, own_sems, square_scratch,
+    grad_rows, queries, keys, values, attended, log_total, start, cosine, minus, plus, out_weight,
+    gate_up, grad_mixed, out_result, gate_result, up_result,
+    grad, keys_sum, values_sum, pieces, halves, own_sems, square_scratch, pair_sems, gate_up_sems,
 ):
     at = Place()
     at.barrier()
@@ -964,10 +1086,32 @@
         own_sems,
     )
     next(own_job)
-    weight_job = square_scatter(at, weight, weight_result, square_scratch)
-    next(weight_job)
+    pair_send, pair_recv = pair_sems
+    pairs = [
+        remote(
+            out_weight.at[r, :, 1 - at.c], halves.at[r], pair_send.at[r], pair_recv.at[r], at.r, at.sibling
+        )
+        for r in range(4)
+    ]
+    for copy in pairs:
+        copy.start()
+    gate_up_job = exchange(at, lambda b, p: gate_up.at[b], lambda b, p: pieces.at[b], gate_up_sems)
+    next(gate_up_job)
     keys_sum[...] = jnp.zeros_like(keys_sum)
     values_sum[...] = jnp.zeros_like(values_sum)
+    for r in range(4):
+        pairs[r].wait()
+        mine = out_weight[r, :, at.c].astype(jnp.float32) + halves[r].astype(jnp.float32)
+        halves[r] = mine.astype(jnp.bfloat16)
+    out_job = square_scatter(
+        at,
+        lambda r, half: halves.at[r, pl.ds(2 * half, 2)],
+        out_result,
+        square_scratch,
+    )
+    next(out_job)
+    next(out_job)
+    next(out_job)
     drive(own_job)
     for i in range(blocks):
         rows = slice(i * QROWS, (i + 1) * QROWS)
@@ -979,7 +1123,7 @@
             lane = lax.broadcasted_iota(jnp.int32, (QROWS, 128), 1)
             q, g = queries[rows, lanes], grad[rows, lanes]
             k, v = keys[:count, lanes], values[:count, lanes]
-            allowed = score_mask(i * QROWS, QROWS, count, start[rows])
+            allowed = score_mask(i * QROWS, QROWS, count, start[rows, 0:1])
             product = g.astype(jnp.float32) * attended[rows, lanes]
             logs = log_total[rows, lanes]
             queries_part, keys_part, values_part = [], [], []
@@ -1002,7 +1146,7 @@
             keys_sum[:count, lanes] += keys_part[0] + keys_part[1]
             values_sum[:count, lanes] += values_part[0] + values_part[1]
 
-        next(weight_job, None)
+        next(out_job, None)
 
     @pl.loop(0, blocks)
     def _(i):
@@ -1014,66 +1158,162 @@
             grad_mixed[rows, shifted] = turned(keys_sum[rows, lanes], *tables).astype(jnp.bfloat16)
         grad_mixed[rows, slice(2 * local, 3 * local)] = values_sum[rows].astype(jnp.bfloat16)
 
-    drive(weight_job)
-
-
-def attend_backward(grad_rows, queries, keys, values, attended, log_total, start, tables, weight):
+    drive(out_job)
+    drive(gate_up_job)
+    hidden = pieces.shape[2] // 8
+    for b in range(8):
+        for r in range(4):
+            source = slice((8 * r + b) * hidden, (8 * r + b + 1) * hidden)
+            gate_result[:, source] = pieces[b, :, r * hidden : (r + 1) * hidden].astype(jnp.float32)
+            up_result[:, source] = pieces[b, :, (4 + r) * hidden : (5 + r) * hidden].astype(jnp.float32)
+
+
+def attend_backward(
+    grad_rows, queries, keys, values, attended, log_total, start, tables, out_weight, gate_up
+):
     length, local = queries.shape
     bf, f32 = jnp.bfloat16, jnp.float32
-    owned = (weight.shape[0] // 4, weight.shape[1])
-    flat, spans = pack_sems([exchange_sems(), square_scatter_scratch(*owned)])
-    outs = [((length, 3 * local), bf, VMEM), (owned, bf, VMEM)]
+    depth, width = out_weight.shape[3:]
+    quarter = [VMEM((4, depth, width), bf)] * 2 + [VMEM((2, depth, width), bf)] * 4
+    flat, spans = pack_sems(
+        [
+            exchange_sems(), quarter + [DMA((6,)), DMA((6,))], [DMA((4,)), DMA((4,))], exchange_sems(),
+        ]
+    )
+    shard = (gate_up.shape[1], 4 * gate_up.shape[2])
+    outs = [((length, 3 * local), bf, VMEM), ((4, depth, width), bf, VMEM)] + [(shard, f32, VMEM)] * 2
     scratch = [VMEM((length, local), bf), VMEM((length, local), f32), VMEM((length, local), f32)]
+    scratch += [VMEM(gate_up.shape, bf), VMEM((4, 4, depth, width), bf)]
     return call(
-        grouped(attend_backward_kernel, 16, spans), [VMEM] * 11, outs, scratch + flat, 4,
-        grad_rows, queries, keys, values, attended, log_total, start, *tables, weight,
-    )
-
-
-def owners_kernel(
-    project, gate_up, vectors, project_out, gate_up_out, vector_out,
-    arrived, summed, rows_in, project_sems, gate_up_sems, vector_sems, row_sems,
+        grouped(attend_backward_kernel, 21, spans), [VMEM] * 11 + [HBM], outs, scratch + flat, 4,
+        grad_rows, queries, keys, values, attended, log_total, start, *tables, out_weight, gate_up,
+    )
+
+
+def finish_kernel(
+    partial, normed, grad_mixed, down_partial, out_part, x_ref, gain, grad_mid, feed_sums, bias_sums,
+    tokens_grad, project_grad, down_grad, out_grad, vector_out,
+    weight, weight_result, pieces, first, sums, arrived, summed, rows_in,
+    line_scratch, project_scratch, down_scratch, out_scratch, piece_sems, vector_sems, row_sems,
 ):
     at = Place()
     at.barrier(diagonal=True)
-    vector_job = exchange(at, lambda b, p: vectors.at[b], lambda b, p: arrived.at[b], vector_sems)
-    next(vector_job)
-    project_job = exchange(
-        at, lambda b, p: project.at[b], lambda b, p: project_out.at[b], project_sems
-    )
-    next(project_job)
-    gate_up_job = exchange(
-        at, lambda b, p: gate_up.at[b], lambda b, p: gate_up_out.at[b], gate_up_sems
-    )
-    next(gate_up_job)
-    drive(vector_job)
-    summed[...] = jnp.sum(arrived[...], axis=0)
-    send, recv = row_sems
-    copies = [
-        remote(summed.at[row], rows_in.at[i], send.at[i], recv.at[i], row, at.b)
-        for i, row in enumerate((at.rx, at.ry, at.rd))
+    rows, width = first.shape
+    depth = weight_result.shape[0]
+
+    def prepare(r):
+        spot = pl.ds(pl.multiple_of(r * depth, depth), depth)
+        weight[spot] = dot(normed[:, spot], grad_mixed[...], ((0,), (0,))).astype(jnp.bfloat16)
+
+    shard = depth // 8
+    size = shard // CHUNKS
+    line_job = line_scatter(at, rows_of(partial, rows), first, line_scratch)
+    next(line_job)
+    out_job = line_scatter(
+        at, lambda z, c, k: out_part.at[z, pl.ds(k * size, size)], out_grad, out_scratch, False
+    )
+    next(out_job)
+
+    def project_work():
+        yield from square_scatter(at, row_halves(weight), weight_result, project_scratch, 0, prepare)
+        yield from exchange(
+            at,
+            lambda b, p: weight_result.at[pl.ds(pl.multiple_of(b * shard, shard), shard)],
+            lambda b, p: pieces.at[b],
+            piece_sems,
+        )
+
+    project_job = project_work()
+    down_job = square_scatter(at, row_halves(down_partial, 1), down_grad, down_scratch, 1)
+
+    def vector_work():
+        x = x_ref[...].astype(jnp.float32)
+        centered = x - jnp.mean(x, axis=1, keepdims=True)
+        inverse = lax.rsqrt(jnp.mean(centered * centered, axis=1, keepdims=True) + epsilon)
+        unit = centered * inverse
+        incoming = first[...]
+        product = incoming * unit
+        parts = jnp.concatenate(
+            [
+                jnp.sum(product, axis=0, keepdims=True),
+                jnp.sum(incoming, axis=0, keepdims=True),
+                feed_sums[...],
+            ],
+            axis=0,
+        )
+        for b in range(8):
+            for r in range(4):
+                lanes = slice((4 * r + b // 2) * 128, (4 * r + b // 2 + 1) * 128)
+                sums[b, r, 0:4] = parts[:, lanes]
+                sums[b, r, 4:6] = bias_sums[b, r]
+                sums[b, r, 6:8] = jnp.zeros((2, 128), jnp.float32)
+        spread = exchange(at, lambda b, p: sums.at[b], lambda b, p: arrived.at[b], vector_sems)
+        next(spread)
+        unit_grad = incoming * gain[...]
+        tokens_grad[...] = grad_mid[...] + inverse * (
+            unit_grad
+            - jnp.mean(unit_grad, axis=1, keepdims=True)
+            - unit * jnp.mean(unit_grad * unit, axis=1, keepdims=True)
+        )
+        drive(spread)
+        summed[...] = jnp.sum(arrived[...], axis=0)
+        send, recv = row_sems
+        copies = [
+            remote(summed.at[row], rows_in.at[i], send.at[i], recv.at[i], row, at.b)
+            for i, row in enumerate((at.rx, at.ry, at.rd))
+        ]
+        for copy in copies:
+            copy.start()
+        for copy in copies:
+            copy.wait()
+        vector_out[...] = summed[at.r] + rows_in[0] + rows_in[1] + rows_in[2]
+
+    drive(line_job, project_job_steps(project_job, 6), down_job)
+    vector_work()
+    drive(project_job, out_job)
+    inner = pieces.shape[2] // 3
+    for b in range(8):
+        for p in range(3):
+            lanes = slice(p * width + b * inner, p * width + (b + 1) * inner)
+            project_grad[:, lanes] = pieces[b, :, p * inner : (p + 1) * inner].astype(jnp.float32)
+
+
+def project_job_steps(job, count):
+    for _ in range(count):
+        next(job)
+        yield
+
+
+def finish(
+    partial, normed, grad_mixed, down_partial, out_part, x, gain, grad_mid, feed_sums, bias_sums
+):
+    bf, f32 = jnp.bfloat16, jnp.float32
+    rows, width = x.shape
+    inner = grad_mixed.shape[1]
+    depth = width // 4
+    shard = depth // 8
+    down_owned = (down_partial.shape[0] // 4, width)
+    flat, spans = pack_sems(
+        [
+            line_scatter_scratch(rows, width),
+            square_scatter_scratch(depth, inner),
+            square_scatter_scratch(*down_owned, 1),
+            line_scatter_scratch(shard, width),
+            exchange_sems(), exchange_sems(), [DMA((3,)), DMA((3,))],
+        ]
+    )
+    outs = [
+        ((rows, width), f32, VMEM), ((shard, 8 * inner), f32, VMEM), (down_owned, f32, VMEM),
+        ((shard, width), f32, VMEM), ((8, 128), f32, VMEM),
     ]
-    for copy in copies:
-        copy.start()
-    for copy in copies:
-        copy.wait()
-    vector_out[...] = summed[at.r] + rows_in[0] + rows_in[1] + rows_in[2]
-    drive(project_job, gate_up_job)
-
-
-def owners_call(project, gate_up, vectors):
-    f32 = jnp.float32
-    flat, spans = pack_sems(
-        [exchange_sems(), exchange_sems(), exchange_sems(), [DMA((3,)), DMA((3,))]]
-    )
-    tail = vectors.shape[1:]
-    outs = [
-        (project.shape, project.dtype, HBM), (gate_up.shape, gate_up.dtype, HBM), (tail[1:], f32, VMEM)
+    scratch = [
+        VMEM((width, inner), bf), VMEM((depth, inner), bf), VMEM((8, shard, inner), bf),
+        VMEM((rows, width), f32), VMEM((8, 4, 8, 128), f32), VMEM((8, 4, 8, 128), f32),
+        VMEM((4, 8, 128), f32), VMEM((3, 8, 128), f32),
     ]
-    scratch = [VMEM((8,) + tail, f32), VMEM(tail, f32), VMEM((3,) + tail[1:], f32)]
     return call(
-        grouped(owners_kernel, 9, spans), [HBM, HBM, VMEM], outs, scratch + flat, 6,
-        project, gate_up, vectors,
+        grouped(finish_kernel, 23, spans), [VMEM] * 10, outs, scratch + flat, 5,
+        partial, normed, grad_mixed, down_partial, out_part, x, gain, grad_mid, feed_sums, bias_sums,
     )
 
 
@@ -1100,17 +1340,9 @@
         [small, rest, segments.astype(bf), jnp.zeros((9, 128), bf)], axis=0
     )
 
-    def pieces_of(weight):
-        depth = weight.shape[0]
-        return weight.reshape(depth, 4, 8, hidden).transpose(2, 0, 1, 3).reshape(8, depth, 4 * hidden)
-
-    w_out = lax.all_gather(output_weight, BOTH, axis=0, tiled=True)
-    gate_up = jnp.concatenate([pieces_of(gate_weight), pieces_of(up_weight)], axis=2)
-
-    vectors, normed_first, w_project, w_down = start_call(
-        tokens[0], vector, project_weight, down_weight
-    )
-    grad_out = gather_blk(cotangent[0])
+    vectors, normed_first, w_project, w_down, w_out, gate_up, start, tables = start_call(
+        tokens[0], vector, project_weight, down_weight, output_weight, gate_weight, up_weight
+    )
 
     def whole(row):
         pairs = vectors[:, row].reshape(16, 2, 128).astype(f32)
@@ -1119,31 +1351,16 @@
     a_gain, f_gain, f_shift = whole(0), whole(2), whole(3)
     bias = vectors[:, 4:6].reshape(32, 256)[:, : 3 * shard].reshape(3, 8, local)
     bias = lax.dynamic_index_in_dim(bias, b, 1, False).reshape(1, -1).astype(f32)
-    doc = lax.dynamic_slice_in_dim(vectors[:, 6], 8 * r, 8, 0).reshape(-1).astype(f32)
-    starts = jnp.sum((doc[None, :] < doc[:, None]).astype(jnp.int32), axis=1)
-    places = (jnp.arange(length, dtype=jnp.int32) - starts).astype(f32)
-    half = ROT // 2
-    frequency = jnp.power(rotary_base, -jnp.arange(half, dtype=jnp.int32).astype(f32) / half)
-    angles = frequency[:, None] * places[None, :]
-    cosine, sine = jnp.cos(angles), jnp.sin(angles)
-    gap = jnp.zeros((head_width - ROT, length), f32)
-    eight = jnp.zeros((half, length), f32)
-
-    def table(first, second, fill):
-        one = jnp.concatenate([first, second, gap + fill], axis=0)
-        return jnp.transpose(jnp.concatenate([one, one], axis=0))
-
-    tables = (table(cosine, cosine, 1.0), table(-sine, eight, 0.0), table(eight, sine, 0.0))
-    start = starts[:, None]
-
-    queries, keys, values, attended, log_total, attended_low, gate_up = attend_forward(
-        normed_first, w_project, bias, start, tables, gate_up
-    )
+
+    queries, keys, values, attended, log_total, attended_low, gate_up, w_out = attend_forward(
+        normed_first, w_project, bias, start, tables, gate_up, w_out
+    )
+    w_out = w_out.reshape(width, width)
     inputs = tokens[0].astype(f32)
     resid_mid = inputs + dot(attended_low, w_out, ((1,), (0,)))
     unit_second, inverse_second = norm_stats(resid_mid)
-    normed_second, w_gate_up = second_gather(
-        (unit_second * f_gain + f_shift).astype(bf), gate_up.reshape(8 * shard, 8 * hidden)
+    normed_second, w_gate_up, grad_out = second_gather(
+        (unit_second * f_gain + f_shift).astype(bf), gate_up.reshape(8 * shard, 8 * hidden), cotangent[0]
     )
     both = dot(normed_second, w_gate_up, ((1,), (0,)))
     gate_value, up_value = both[:, : 4 * hidden], both[:, 4 * hidden :]
@@ -1155,50 +1372,33 @@
     grad_both = jnp.concatenate([grad_gate.astype(bf), (grad_hidden * silu).astype(bf)], axis=1)
     grad_second = dot(grad_both, w_gate_up, ((1,), (1,))).astype(bf)
     down_partial = dot(hidden_low, grad_out, ((0,), (0,))).astype(bf)
-    grad_second, down_grad = reduce_call(grad_second, down_partial, 3, 1, f32)
-    output = (resid_mid + scatter_blk(dot(hidden_low, w_down, ((1,), (0,))))).astype(bf)
-    gate_up_partial = dot(normed_second, grad_both, ((0,), (0,))).astype(bf)
+    out_partial = dot(hidden_low, w_down, ((1,), (0,))).astype(bf)
+    grad_second, output, gate_up_grad = feed_reduce(grad_second, out_partial, normed_second, grad_both)
+    output = (resid_mid + output).astype(bf)
 
     mid_part, f_gain_part, f_shift_part = norm_back(grad_second, unit_second, inverse_second, f_gain)
     grad_mid = cotangent[0].astype(f32) + mid_part
     grad_mid_low = grad_mid.astype(bf)
     grad_attended = dot(grad_mid_low, w_out, ((1,), (1,))).astype(bf)
-    grad_mixed, gate_up_grad = attend_backward(
-        grad_attended, queries, keys, values, attended, log_total, start, tables, gate_up_partial
-    )
-    out_grad = lax.psum_scatter(
-        dot(attended_low, grad_mid_low, ((0,), (0,))).astype(bf), BOTH, scatter_dimension=0, tiled=True
-    ).astype(f32)
+    out_partial = dot(attended_low, grad_mid_low, ((0,), (0,))).astype(bf)
+    grad_mixed, out_part, gate_grad, up_grad = attend_backward(
+        grad_attended, queries, keys, values, attended, log_total, start, tables,
+        out_partial.reshape(4, 4, 2, shard, width), gate_up_grad.reshape(8, shard, 8 * hidden),
+    )
     grad_first = dot(grad_mixed, w_project, ((1,), (1,))).astype(bf)
-    project_partial = dot(normed_first, grad_mixed, ((0,), (0,))).astype(bf)
-    grad_first, project_grad = reduce_call(grad_first, project_partial, 5, 0, bf)
-    unit_first, inverse_first = norm_stats(inputs)
-    input_part, a_gain_part, a_shift_part = norm_back(grad_first, unit_first, inverse_first, a_gain)
-    grad_tokens = grad_mid + input_part
 
     bias_part = jnp.sum(grad_mixed.astype(f32), axis=0).reshape(3, 1, local)
     bias_part = jnp.where(jnp.arange(8)[None, :, None] == b, bias_part, 0.0)
-    bias_part = jnp.pad(bias_part.reshape(32, 3 * shard), ((0, 0), (0, 64))).reshape(32, 2, 128)
-    gains = jnp.stack(
-        [part.reshape(32, shard) for part in (a_gain_part, a_shift_part, f_gain_part, f_shift_part)], axis=1
-    )
-    gains = jnp.pad(gains, ((0, 0), (0, 0), (0, 64)))
-    sums = jnp.concatenate([gains, bias_part, jnp.zeros((32, 2, 128), f32)], axis=1)
-    sums = sums.reshape(4, 8, 8, 128).transpose(1, 0, 2, 3)
-    project_grad, gate_up_grad, vector = owners_call(
-        project_grad.reshape(8, shard, 3 * local), gate_up_grad.reshape(8, shard, 8 * hidden), sums
-    )
-
-    def owned(pieces, parts):
-        inner = pieces.shape[2] // parts
-        pieces = pieces.reshape(8, shard, parts, inner).transpose(1, 2, 0, 3)
-        return pieces.reshape(shard, 8 * parts * inner).astype(f32)
-
+    bias_part = jnp.pad(bias_part.reshape(32, 3 * shard), ((0, 0), (0, 64)))
+    bias_part = bias_part.reshape(4, 8, 2, 128).transpose(1, 0, 2, 3)
+    grad_tokens, project_grad, down_grad, out_grad, vector = finish(
+        grad_first, normed_first, grad_mixed, down_partial, out_part, tokens[0], a_gain[None], grad_mid,
+        jnp.stack([f_gain_part, f_shift_part]), bias_part,
+    )
+    gains = jnp.where(b % 2 == 0, vector[:4, :shard], vector[:4, shard:])
     return (
-        output[None], grad_tokens[None], vector[0, :shard], vector[1, :shard],
-        owned(project_grad, 3), vector[4:6].reshape(-1)[: 3 * shard], out_grad,
-        vector[2, :shard], vector[3, :shard],
-        owned(gate_up_grad[:, :, : 4 * hidden], 4), owned(gate_up_grad[:, :, 4 * hidden :], 4), down_grad,
+        output[None], grad_tokens[None], gains[0], gains[1], project_grad,
+        vector[4:6].reshape(-1)[: 3 * shard], out_grad, gains[2], gains[3], gate_grad, up_grad, down_grad,
     )
 
 

time: 714 us -> 586 us (0.82)
  the two profiles are of different devices: /device:TPU:16 before, /device:TPU:0 now
where the time goes in v3:
time: 586 us; the launch traced here: 577 us
  Pallas kernels  492 us (84%)
  matrix products  57.7 us (10%)
  other arithmetic  14.4 us (2%)
  local copies, waits for them, and re-layouts  12.1 us (2%)
    pallas_call x6, Pallas kernels, call(): pl.pallas_call(kernel, out_shape=[jax.ShapeDtypeStruct(shape, kind) for s...  492 us
    dot_general x9, matrix products, dot(): lax.dot_general(left, right, (contract, ((), ())), preferred_element_type...  57.7 us

profile of v3, /device:TPU:0, one launch (start us, length us, event | category | flops | bytes accessed | tf_op | source)
XLA Modules:
  0.0 577.2 jit_solution(15030182781887782053)
XLA Ops:
  2.1 0.7 pad_maximum_fusion.2
  2.9 0.7 maximum_maximum_fusion.refs_1_
  3.5 86.9 %shard_map.220 = (bf16[32,16,128]{2,1,0:T(8,128)(2,1)}, bf16[1024,2048]{1,0:T(8,128)(2,1)}, bf16[512,768]{1,0:T(8,128)(2,1)}, bf16[2048,768]{1,0:T(8,128)(2,1)},...) custom-call(bf16[128,2048]{1,0:T(8,128)(2,1)} %bitcast.69, ...), custom_call_target="tpu_custom_call" | custom-call | tf_op jit(solution)/shard_map/pallas_call | solution.py:696
  90.5 0.9 slice.63
  91.3 1.0 slice_convert_fusion
  93.7 54.1 %shard_map.221 = (bf16[1024,256]{1,0:T(8,128)(2,1)}, bf16[1024,256]{1,0:T(8,128)(2,1)}, bf16[1024,256]{1,0:T(8,128)(2,1)}, f32[1024,256]{1,0:T(8,128)}, f32[1024...) custom-call(bf16[1024,2048]{1,0:T(8,128)(2,1)} %get-tuple-element.45, ...), custom_call_target="tpu_custom_call" | custom-call | tf_op jit(solution)/shard_map/pallas_call | solution.py:696
  147.8 4.9 fusion.5
  153.1 1.1 add_convert_fusion.1.refs_0_
  154.1 86.4 %shard_map.222 = (bf16[1024,2048]{1,0:T(8,128)(2,1)}, bf16[2048,1408]{1,0:T(8,128)(2,1)}, bf16[1024,2048]{1,0:T(8,128)(2,1)}) custom-call(bf16[128,2048]{1,0:T(8,128)(2,1)} %add_convert_fusion.1.refs_0_, bf16[512,1408]{1,0:T(8,128)(2,1)} %bitcast.72, bf16[128,2048]{1,0:T(8,128)(2,1)} %bitcast.71), custom_call_target="tpu_custom_call" | custom-call | tf_op jit(solution)/shard_map/pallas_call | solution.py:696
  240.6 10.8 %fusion.6 = f32[1024,1408]{1,0:T(8,128)S(1)} fusion(bf16[1024,2048]{1,0:T(8,128)(2,1)} %get-tuple-element.59.refs_2_, bf16[2048,1408]{1,0:T(8,128)(2,1)} %get-tuple-element.60), kind=kOutput, calls=%fused_computation.53 | convolution fusion | flops 5905580032 | bytes 15728640 | tf_op jit(solution)/shard_map/dot_general | solution.py:21
  251.4 4.3 multiply_convert_fusion.2
  255.7 4.6 convolution_convert_fusion.4.refs_3_
  260.3 0.9 pad_maximum_fusion.refs_3_
  261.2 8.3 %convolution_convert_fusion.2.refs_0_ = bf16[1024,2048]{1,0:T(8,128)(2,1)} fusion(bf16[1024,1408]{1,0:T(8,128)(2,1)S(1)} %pad_maximum_fusion.refs_3_, bf16[2048,1408]{1,0:T(8,128)(2,1)S(1)} %bitcast.97), kind=kOutput, calls=%fused_computation.2 | convolution fusion | flops 5907677184 | bytes 12845056 | tf_op jit(solution)/shard_map/dot_general | solution.py:21
  269.4 5.3 convolution_convert_fusion.1.refs_1_
  274.8 79.7 %shard_map.223 = (f32[128,2048]{1,0:T(8,128)}, f32[128,2048]{1,0:T(8,128)}, bf16[512,1408]{1,0:T(8,128)(2,1)}) custom-call(bf16[1024,2048]{1,0:T(8,128)(2,1)} %convolution_convert_fusion.2.refs_0_, bf16[1024,2048]{1,0:T(8,128)(2,1)} %convolution_convert_fusion.1.refs_1_, bf16[1024,2048]{1,0:T(8,128)(2,1)} %get-tuple-element.59.refs_2_, ...), custom_call_target="tpu_custom_call" | custom-call | tf_op jit(solution)/shard_map/pallas_call | solution.py:696
  354.5 1.7 multiply_reduce_fusion
  356.8 2.9 multiply_add_fusion
  359.7 7.5 %convolution_convert_fusion.5.refs_0_ = bf16[128,2048]{1,0:T(8,128)(2,1)} fusion(bf16[2048,2048]{1,0:T(8,128)(2,1)} %bitcast.67, f32[128,2048]{1,0:T(8,128)S(1)} %get-tuple-element.85.refs_7_), kind=kOutput, calls=%fused_computation.13 | convolution fusion | flops 1074266112 | bytes 9961472 | tf_op jit(solution)/shard_map/dot_general | solution.py:21
  367.2 5.7 convolution_convert_fusion
  372.8 68.2 %shard_map.224 = (bf16[1024,768]{1,0:T(8,128)(2,1)}, bf16[4,64,2048]{2,1,0:T(8,128)(2,1)}, f32[64,5632]{1,0:T(8,128)}, f32[64,5632]{1,0:T(8,128)}) custom-call(bf16[128,2048]{1,0:T(8,128)(2,1)} %convolution_convert_fusion.5.refs_0_, bf16[1024,256]{1,0:T(8,128)(2,1)} %get-tuple-element.63.refs_1_, bf16[1024,256]{1,0:T(8,128)(2,1)} %get-tuple-element.64.refs_2_, ...), custom_call_target="tpu_custom_call" | custom-call | tf_op jit(solution)/shard_map/pallas_call | solution.py:696
  441.1 1.7 convert_reduce_fusion
  443.6 6.4 %convolution_convert_fusion.3.refs_0_ = bf16[1024,2048]{1,0:T(8,128)(2,1)} fusion(bf16[1024,768]{1,0:T(8,128)(2,1)} %get-tuple-element.69.refs_2_, bf16[2048,768]{1,0:T(8,128)(2,1)S(1)} %copy-done.4), kind=kOutput, calls=%fused_computation.3 | convolution fusion | flops 3223322624 | bytes 8912896 | tf_op jit(solution)/shard_map/dot_general | solution.py:21
  450.0 116.3 %shard_map.225 = (f32[128,2048]{1,0:T(8,128)}, f32[64,6144]{1,0:T(8,128)}, f32[176,2048]{1,0:T(8,128)}, f32[64,2048]{1,0:T(8,128)}, f32[8,128]{1,0:T(8,128)}) custom-call(bf16[1024,2048]{1,0:T(8,128)(2,1)} %convolution_convert_fusion.3.refs_0_, bf16[1024,2048]{1,0:T(8,128)(2,1)} %get-tuple-element.45.refs_0_.refs_1_, ...), custom_call_target="tpu_custom_call" | custom-call | tf_op jit(solution)/shard_map/pallas_call | solution.py:696
  566.3 1.4 slice_bitcast_fusion
  567.7 0.8 slice_select_fusion
  569.1 2.4 copy.48
  571.5 1.1 copy.49
  572.6 0.8 copy.50
  573.4 1.1 copy.51
  574.5 1.1 copy.52
  575.6 1.1 copy.53
  (56 shorter events, 5.1 us)
Async XLA Ops:
  93.7 54.1 %copy-start.3 = (bf16[1,128,2048]{2,1,0:T(8,128)(2,1)S(1)}, bf16[1,128,2048]{2,1,0:T(8,128)(2,1)}, u32[]{:S(2)}) copy-start(bf16[1,128,2048]{2,1,0:T(8,128)(2,1)} %param.13) | copy-start | bytes 1572868
  240.6 10.8 %copy-start.11 = (bf16[1024,2048]{1,0:T(8,128)(2,1)S(1)}, bf16[1024,2048]{1,0:T(8,128)(2,1)}, u32[]{:S(2)}) copy-start(bf16[1024,2048]{1,0:T(8,128)(2,1)} %get-tuple-element.57) | copy-start | bytes 12582916
  240.6 10.8 %copy-start.12 = (bf16[704,2048]{1,0:T(8,128)(2,1)S(1)}, bf16[704,2048]{1,0:T(8,128)(2,1)}, u32[]{:S(2)}) copy-start(bf16[704,2048]{1,0:T(8,128)(2,1)} %get-tuple-element.58) | copy-start | bytes 8650756
  255.7 5.5 slice-start
  255.7 5.5 slice-start.1
  261.2 8.3 %copy-start.1 = (bf16[1024,1408]{1,0:T(8,128)(2,1)}, bf16[1024,1408]{1,0:T(8,128)(2,1)S(1)}, u32[]{:S(2)}) copy-start(bf16[1024,1408]{1,0:T(8,128)(2,1)S(1)} %pad_maximum_fusion.refs_3_) | copy-start | bytes 8650756
  274.8 82.0 %copy-start.5 = (bf16[1,128,2048]{2,1,0:T(8,128)(2,1)S(1)}, bf16[1,128,2048]{2,1,0:T(8,128)(2,1)}, u32[]{:S(2)}) copy-start(bf16[1,128,2048]{2,1,0:T(8,128)(2,1)} %param.15) | copy-start | bytes 1572868
  359.7 7.5 %copy-start = (f32[128,2048]{1,0:T(8,128)}, f32[128,2048]{1,0:T(8,128)S(1)}, u32[]{:S(2)}) copy-start(f32[128,2048]{1,0:T(8,128)S(1)} %get-tuple-element.85.refs_7_) | copy-start | bytes 3145732
  359.7 7.5 %copy-start.2 = (bf16[128,2048]{1,0:T(8,128)(2,1)S(1)}, bf16[128,2048]{1,0:T(8,128)(2,1)}, u32[]{:S(2)}) copy-start(bf16[128,2048]{1,0:T(8,128)(2,1)} %get-tuple-element.54) | copy-start | bytes 1572868
  372.8 70.7 %copy-start.4 = (bf16[2048,768]{1,0:T(8,128)(2,1)S(1)}, bf16[2048,768]{1,0:T(8,128)(2,1)}, u32[]{:S(2)}) copy-start(bf16[2048,768]{1,0:T(8,128)(2,1)} %get-tuple-element.46.refs_1_) | copy-start | bytes 9437188
  566.3 5.2 copy-start.6
  566.3 6.3 %copy-start.10 = (f32[64,2048]{1,0:T(8,128)S(1)}, f32[64,2048]{1,0:T(8,128)}, u32[]{:S(2)}) copy-start(f32[64,2048]{1,0:T(8,128)} %get-tuple-element.118) | copy-start | bytes 1572868
  569.1 4.4 copy-start.8
  571.5 3.0 copy-start.7
  572.6 3.0 copy-start.9

commit v4 on v3

--- a/solution.py
+++ b/solution.py
@@ -285,7 +285,7 @@
 DMA = pltpu.SemaphoreType.DMA
 HBM = pl.ANY
 VMEM = pltpu.VMEM
-LIMIT = 56 * 1024 * 1024
+LIMIT = 60 * 1024 * 1024
 
 
 class Place:
@@ -324,6 +324,17 @@
                 next(job)
             except StopIteration:
                 active.remove(job)
+
+
+def later(job, count):
+    for _ in range(count):
+        yield
+    yield from job
+
+
+def steps(job, count):
+    for _ in range(count):
+        next(job, None)
 
 
 CHUNKS = 2
@@ -394,12 +405,22 @@
                 if paired:
                     pair(4 + d, k, z, spot(z, at.c, k)).start()
 
+            if d == 0:
+                locals_[k].wait()
+                if paired:
+                    pair_in(0, k, at.z).wait_recv()
+            if k == CHUNKS - 1 and paired:
+                for part in range(CHUNKS):
+                    pl.when(at.z - 1 - d >= 0)(
+                        lambda: pair_in(1 + d, part, at.z - 1 - d).wait_recv()
+                    )
+                    pl.when(at.z + 1 + d <= 3)(
+                        lambda: pair_in(4 + d, part, at.z + 1 + d).wait_recv()
+                    )
             yield
     for k in range(CHUNKS):
-        locals_[k].wait()
         if paired:
             pair(0, k, at.z, own(k)).wait_send()
-            pair_in(0, k, at.z).wait_recv()
         pl.when(at.z < 3)(lambda: up(0, k, own(k)).wait_send())
         pl.when(at.z > 0)(lambda: down(0, k, own(k)).wait_send())
         for d in range(3):
@@ -409,7 +430,6 @@
                 z = at.z - 1 - d
                 if paired:
                     pair(1 + d, k, z, spot(z, at.c, k)).wait_send()
-                    pair_in(1 + d, k, z).wait_recv()
                 if d < 2:
                     pl.when(at.z < 3)(lambda: up(d + 1, k, spot(z, at.c, k)).wait_send())
 
@@ -418,7 +438,6 @@
                 z = at.z + 1 + d
                 if paired:
                     pair(4 + d, k, z, spot(z, at.c, k)).wait_send()
-                    pair_in(4 + d, k, z).wait_recv()
                 if d < 2:
                     pl.when(at.z > 0)(lambda: down(d + 1, k, spot(z, at.c, k)).wait_send())
 
@@ -439,7 +458,7 @@
     return [block, arrive, arrive] + [DMA((4, CHUNKS))] * 2 + [DMA((3, CHUNKS))] * 4
 
 
-def line_scatter(at, block, result, scratch, paired=True):
+def line_scatter(at, block, result, scratch, paired=True, prepare=None):
     held, from_below, from_above, pair_send, pair_recv, up_send, up_recv, down_send, down_recv = scratch
     count = held.shape[1]
     size = count // CHUNKS
@@ -486,6 +505,8 @@
 
     if paired:
         for z in (3, 0, 2, 1):
+            if prepare:
+                prepare(z)
             for k in range(CHUNKS):
                 pair(z, k).start()
     yield
@@ -572,7 +593,7 @@
     return [DMA((6,)), DMA((6,)), DMA((2,))]
 
 
-def square_gather(at, own, spot, sems):
+def square_gather(at, own, spot, sems, arrived=None):
     send, recv, local_sem = sems
 
     def copy(i, src, r_of, which, to):
@@ -606,8 +627,11 @@
     yield
     for copy_ in locals_:
         copy_.wait()
-    for i in (2, 3, 4, 5):
-        ins[i].wait_recv()
+    for pair, r in (((2,), at.rx), ((3,), at.ry), ((4, 5), at.rd)):
+        for i in pair:
+            ins[i].wait_recv()
+        if arrived:
+            arrived(r)
     for out in outs:
         out.wait_send()
 
@@ -766,6 +790,7 @@
         minus[rows] = table(-sin, eight, gap)
         plus[rows] = table(eight, sin, gap)
         start[rows] = jnp.transpose(jnp.broadcast_to(begins[j : j + 1], (128, 128))).astype(jnp.int32)
+        yield
 
 
 def start_kernel(
@@ -790,6 +815,11 @@
         3,
     )
     next(project_job)
+    size = depth // CHUNKS
+    out_job = line_gather(
+        at, cuts_of(out_ref), lambda z, c, k: w_out.at[z, pl.ds(k * size, size)], out_sems, False
+    )
+    next(out_job)
     down_job = square_gather(
         at, lambda half: half_of(down_ref, 1, half), row_halves(w_down, 1), down_sem
     )
@@ -804,24 +834,26 @@
         own[:, lanes] = (unit[:, lanes] * both[0:1] + both[1:2]).astype(jnp.bfloat16)
     line_job = line_gather(at, cuts_of(own), rows_of(normed, own.shape[0]), line_sems)
     next(line_job)
-    size = depth // CHUNKS
-    out_job = line_gather(
-        at, cuts_of(out_ref), lambda z, c, k: w_out.at[z, pl.ds(k * size, size)], out_sems, False
-    )
-    next(out_job)
     hidden = down_ref.shape[0]
-    for b in range(8):
-        for r in range(4):
-            source = slice((8 * r + b) * hidden, (8 * r + b + 1) * hidden)
-            gate_up[b, :, r * hidden : (r + 1) * hidden] = gate_ref[:, source]
-            gate_up[b, :, (4 + r) * hidden : (5 + r) * hidden] = up_ref[:, source]
-    drive(project_job)
-    square_job = square_gather(
-        at, lambda half: half_of(pieces, 0, half), row_halves(w_project), square_sem
-    )
-    next(square_job)
-    make_tables(at, vectors, start, cosine, minus, plus)
-    drive(square_job, line_job, down_job, out_job)
+
+    def reorder():
+        for b in range(8):
+            for r in range(4):
+                source = slice((8 * r + b) * hidden, (8 * r + b + 1) * hidden)
+                gate_up[b, :, r * hidden : (r + 1) * hidden] = gate_ref[:, source]
+                gate_up[b, :, (4 + r) * hidden : (5 + r) * hidden] = up_ref[:, source]
+            yield
+
+    def project_work():
+        yield from project_job
+        yield from square_gather(
+            at, lambda half: half_of(pieces, 0, half), row_halves(w_project), square_sem
+        )
+
+    table_job, order_job = make_tables(at, vectors, start, cosine, minus, plus), reorder()
+    steps(table_job, 4)
+    steps(order_job, 4)
+    drive(out_job, line_job, project_work(), table_job, order_job, down_job)
 
 
 def pack_sems(groups):
@@ -883,17 +915,28 @@
 
 
 def attend_forward_kernel(
-    x_ref, w_ref, bias, start, cosine, minus, plus, gate_up, out_ref,
-    queries, keys, values, attended, log_total, mixed_heads, gate_up_all, w_out,
+    x_ref, w_ref, bias, start, cosine, minus, plus, tokens, feed_set, gate_up, out_ref,
+    queries, keys, values, attended, log_total, mixed_heads, resid_mid, normed, gate_up_all, w_out,
     low, own_sems, gate_up_sems, square_sems, pair_sems,
 ):
     at = Place()
     at.barrier()
+    pair_send, pair_recv = pair_sems
+
+    def pair(i, r, src):
+        return remote(src, w_out.at[r, :, at.c], pair_send.at[i], pair_recv.at[i], at.r, at.sibling)
+
+    pairs = [pair(0, at.r, out_ref)] + [
+        pair(i, r, w_out.at[r, :, at.c]) for i, r in ((1, at.rx), (2, at.ry), (3, at.rd))
+    ]
+    pairs[0].start()
+    handed = iter(pairs[1:])
     out_job = square_gather(
         at,
         lambda half: half_of(out_ref, 0, half),
         lambda r, half: w_out.at[r, pl.ds(2 * half, 2), at.c],
         square_sems,
+        lambda r: next(handed).start(),
     )
     next(out_job)
     length, local = queries.shape
@@ -963,15 +1006,6 @@
                 ).start()
 
     drive(out_job)
-    pair_send, pair_recv = pair_sems
-    pairs = [
-        remote(
-            w_out.at[r, :, at.c], w_out.at[r, :, at.c], pair_send.at[r], pair_recv.at[r], at.r, at.sibling
-        )
-        for r in range(4)
-    ]
-    for copy in pairs:
-        copy.start()
     for source in range(8):
 
         @pl.when(at.b != source)
@@ -987,95 +1021,168 @@
                 local_sem,
             ).wait()
 
+    total = tokens[...].astype(jnp.float32)
+    depth, width = w_out.shape[3:]
+    for i, r in enumerate((at.r, at.rx, at.ry, at.rd)):
+        theirs = w_out.at[r, :, 1 - at.c]
+        remote(theirs, theirs, pair_send.at[i], pair_recv.at[i], at.r, at.sibling).wait_recv()
+    for r in range(4):
+        lanes = slice(r * 8 * depth, (r + 1) * 8 * depth)
+        total += dot(mixed_heads[:, lanes], w_out[r].reshape(8 * depth, width), ((1,), (0,)))
+    resid_mid[...] = total
+    unit, _ = norm_stats(total)
+    normed[...] = (unit * feed_set[0:1] + feed_set[1:2]).astype(jnp.bfloat16)
     drive(gate_up_job)
     for to in range(8):
         pl.when(at.b != to)(lambda: deliver(to).wait_send())
-    for r in range(4):
-        theirs = w_out.at[r, :, 1 - at.c]
-        remote(theirs, theirs, pair_send.at[r], pair_recv.at[r], at.r, at.sibling).wait_recv()
-        pairs[r].wait_send()
-
-
-def attend_forward(x, w, bias, start, tables, gate_up, w_out):
+    for copy in pairs:
+        copy.wait_send()
+
+
+def attend_forward(x, w, bias, start, tables, tokens, feed_set, gate_up, w_out):
     length, local = x.shape[0], w.shape[1] // 3
     bf, f32 = jnp.bfloat16, jnp.float32
     flat, spans = pack_sems(
         [[DMA((8,)), DMA((8,)), DMA], exchange_sems(), square_gather_sems(), [DMA((4,)), DMA((4,))]]
     )
     outs = [((length, local), bf, VMEM)] * 3 + [((length, local), f32, VMEM)] * 2
-    outs += [((length // 8, 8 * local), bf, VMEM), (gate_up.shape, bf, HBM)]
-    outs += [((4, 4, 2) + w_out.shape[1:], bf, HBM)]
+    outs += [(tokens.shape, bf, VMEM), (tokens.shape, f32, VMEM), (tokens.shape, bf, VMEM)]
+    outs += [(gate_up.shape, bf, HBM), ((4, 4, 2) + w_out.shape[1:], bf, VMEM)]
     return call(
-        grouped(attend_forward_kernel, 18, spans), [VMEM] * 7 + [HBM, HBM], outs,
-        [VMEM((length, local), bf)] + flat, 1, x, w, bias, start, *tables, gate_up, w_out,
-    )
-
-
-def second_gather_kernel(
-    own, gate_up, cotangent, normed, w_gate_up, grad_out, line_sems, square_sems, other_sems
+        grouped(attend_forward_kernel, 22, spans), [VMEM] * 9 + [HBM, HBM], outs,
+        [VMEM((length, local), bf)] + flat, 1,
+        x, w, bias, start, *tables, tokens, feed_set, gate_up, w_out,
+    )
+
+
+def feed_kernel(
+    own, gate_up, cotangent, w_down,
+    grad_out, hidden_out, output_sum, result, weight_result,
+    normed, w_gate_up, values, out_partial, partial, weight,
+    line_sems, other_sems, square_sems, out_scratch, scatter_scratch, square_scratch,
 ):
     at = Place()
     at.barrier()
     count = own.shape[0]
-    drive(
-        line_gather(at, cuts_of(own), rows_of(normed, count), line_sems),
-        square_gather(at, lambda half: half_of(gate_up, 0, half), row_halves(w_gate_up), square_sems),
-        line_gather(at, cuts_of(cotangent), rows_of(grad_out, count), other_sems),
-    )
-
-
-def second_gather(own, gate_up, cotangent):
-    flat, spans = pack_sems([line_gather_sems(), square_gather_sems(), line_gather_sems()])
-    bf = jnp.bfloat16
-    full = ((8 * own.shape[0], own.shape[1]), bf, HBM)
-    outs = [full, ((4 * gate_up.shape[0], gate_up.shape[1]), bf, HBM), full]
-    return call(
-        grouped(second_gather_kernel, 6, spans), [HBM] * 3, outs, flat, 2, own, gate_up, cotangent
-    )
-
-
-def feed_reduce_kernel(
-    partial, out_partial, normed, grad_both, result, out_result, weight_result,
-    weight, line_scratch, out_scratch, square_scratch,
-):
-    at = Place()
-    at.barrier()
-    rows = result.shape[0]
+    hidden = hidden_out.shape[1]
+    line_job = line_gather(at, cuts_of(own), rows_of(normed, count), line_sems)
+    square_job = square_gather(
+        at, lambda half: half_of(gate_up, 0, half), row_halves(w_gate_up), square_sems
+    )
+    other_job = line_gather(at, cuts_of(cotangent), rows_of(grad_out, count), other_sems)
+
+    def rows_at(z):
+        return pl.ds(pl.multiple_of(z * 2 * count, 2 * count), 2 * count)
+
+    def forward(z):
+        rows = rows_at(z)
+        both = dot(normed[rows], w_gate_up[...], ((1,), (0,)))
+        gate_value, up_value = both[:, :hidden], both[:, hidden:]
+        low = (gate_value / (1.0 + jnp.exp(-gate_value)) * up_value).astype(jnp.bfloat16)
+        hidden_out[rows] = low
+        values[rows] = both.astype(jnp.bfloat16)
+        out_partial[rows] = dot(low, w_down[...], ((1,), (0,))).astype(jnp.bfloat16)
+
+    def backward(z):
+        rows = rows_at(z)
+        both = values[rows].astype(jnp.float32)
+        gate_value, up_value = both[:, :hidden], both[:, hidden:]
+        grad_hidden = dot(grad_out[rows], w_down[...], ((1,), (1,)))
+        gate_sigmoid = 1.0 / (1.0 + jnp.exp(-gate_value))
+        silu = gate_value * gate_sigmoid
+        grad_gate = grad_hidden * up_value * gate_sigmoid * (1.0 + gate_value * (1.0 - gate_sigmoid))
+        grads = jnp.concatenate([grad_gate, grad_hidden * silu], axis=1).astype(jnp.bfloat16)
+        values[rows] = grads
+        partial[rows] = dot(grads, w_gate_up[...], ((1,), (1,))).astype(jnp.bfloat16)
+
+    out_job = line_scatter(at, rows_of(out_partial, count), output_sum, out_scratch)
+    next(line_job)
+    next(square_job)
+    next(other_job)
+    for i in range(4):
+        steps(line_job, 1)
+        steps(square_job, 1)
+        steps(other_job, 1)
+    steps(line_job, 2)
+    drive(square_job)
+    pl.loop(0, 2)(forward)
+    steps(other_job, 1)
+    pl.loop(2, 4)(forward)
+    next(out_job)
+    steps(other_job, 1)
+    for z in range(4):
+        backward(z)
+        steps(out_job, 1)
+
     depth = weight_result.shape[0]
     step = depth // 2
 
     def prepare(r):
         for half in range(2):
             spot = pl.ds(pl.multiple_of(r * depth + half * step, step), step)
-            weight[spot] = dot(normed[:, spot], grad_both[...], ((0,), (0,))).astype(jnp.bfloat16)
-
-    drive(
-        line_scatter(at, rows_of(partial, rows), result, line_scratch),
-        square_scatter(at, row_halves(weight), weight_result, square_scratch, 0, prepare),
-        line_scatter(at, rows_of(out_partial, rows), out_result, out_scratch),
-    )
-
-
-def feed_reduce(partial, out_partial, normed, grad_both):
-    rows, width = partial.shape[0] // 8, partial.shape[1]
+            weight[spot] = dot(normed[:, spot], values[...], ((0,), (0,))).astype(jnp.bfloat16)
+
+    scatter_job = line_scatter(at, rows_of(partial, count), result, scatter_scratch)
+    weight_job = square_scatter(at, row_halves(weight), weight_result, square_scratch, 0, prepare)
+    next(scatter_job)
+    steps(weight_job, 3)
+    drive(out_job, scatter_job, weight_job, line_job, other_job)
+
+
+def feed(own, gate_up, cotangent, w_down):
     bf, f32 = jnp.bfloat16, jnp.float32
-    owned = (width // 4, grad_both.shape[1])
-    line = line_scatter_scratch(rows, width)
-    flat, spans = pack_sems([line, line, square_scatter_scratch(*owned)])
-    outs = [((rows, width), f32, VMEM)] * 2 + [(owned, bf, VMEM)]
+    rows, width = own.shape
+    hidden = w_down.shape[0]
+    owned = (width // 4, 2 * hidden)
+    full = (8 * rows, width)
+    flat, spans = pack_sems(
+        [
+            line_gather_sems(), line_gather_sems(), square_gather_sems(),
+            line_scatter_scratch(rows, width), line_scatter_scratch(rows, width),
+            square_scatter_scratch(*owned),
+        ]
+    )
+    outs = [(full, bf, VMEM), ((8 * rows, hidden), bf, VMEM)]
+    outs += [((rows, width), f32, VMEM)] * 2 + [(owned, bf, VMEM)]
+    scratch = [
+        VMEM(full, bf), VMEM((width, 2 * hidden), bf), VMEM((8 * rows, 2 * hidden), bf), VMEM(full, bf),
+        VMEM(full, bf), VMEM((width, 2 * hidden), bf),
+    ]
     return call(
-        grouped(feed_reduce_kernel, 8, spans), [VMEM] * 4, outs,
-        [VMEM((width, owned[1]), bf)] + flat, 3, partial, out_partial, normed, grad_both,
+        grouped(feed_kernel, 15, spans), [VMEM, HBM, VMEM, VMEM], outs, scratch + flat, 2,
+        own, gate_up, cotangent, w_down,
     )
 
 
 def attend_backward_kernel(
-    grad_rows, queries, keys, values, attended, log_total, start, cosine, minus, plus, out_weight,
-    gate_up, grad_mixed, out_result, gate_result, up_result,
-    grad, keys_sum, values_sum, pieces, halves, own_sems, square_scratch, pair_sems, gate_up_sems,
+    grad_second, resid_mid, cotangent, feed_gain, queries, keys, values, attended, log_total,
+    start, cosine, minus, plus, mixed_heads, gate_up, out_weight,
+    grad_mixed, out_result, gate_result, up_result, grad_mid, feed_sums,
+    grad_rows, w_out, grad, keys_sum, values_sum, pieces, halves, heads_pair, mid_pair, product_rows,
+    own_sems, square_scratch, pair_sems, gate_up_sems, load_sems,
 ):
     at = Place()
+    load = pltpu.make_async_copy(out_weight, w_out, load_sems[0])
+    load.start()
+    unit, inverse = norm_stats(resid_mid[...])
+    incoming = grad_second[...]
+    mid_part, gain_part, shift_part = norm_back(incoming, unit, inverse, feed_gain[...])
+    total = cotangent[...].astype(jnp.float32) + mid_part
+    grad_mid[...] = total
+    mid_pair[:128] = total.astype(jnp.bfloat16)
+    heads_pair[:128] = mixed_heads[...]
+    feed_sums[0:1] = gain_part[None]
+    feed_sums[1:2] = shift_part[None]
     at.barrier()
+    pair_send, pair_recv = pair_sems
+    pairs = [
+        remote(ref.at[pl.ds(0, 128)], ref.at[pl.ds(128, 128)], pair_send.at[i], pair_recv.at[i], at.r, at.sibling)
+        for i, ref in enumerate((heads_pair, mid_pair))
+    ]
+    for copy in pairs:
+        copy.start()
+    load.wait()
+    grad_rows[...] = dot(mid_pair[:128], w_out[...], ((1,), (1,))).astype(jnp.bfloat16)
     length, local = queries.shape
     scale = 1.0 / math.sqrt(local * 8 // HEADS)
     blocks = length // QROWS
@@ -1086,33 +1193,26 @@
         own_sems,
     )
     next(own_job)
-    pair_send, pair_recv = pair_sems
-    pairs = [
-        remote(
-            out_weight.at[r, :, 1 - at.c], halves.at[r], pair_send.at[r], pair_recv.at[r], at.r, at.sibling
-        )
-        for r in range(4)
-    ]
+    keys_sum[...] = jnp.zeros_like(keys_sum)
+    values_sum[...] = jnp.zeros_like(values_sum)
     for copy in pairs:
-        copy.start()
+        copy.wait()
+    depth = halves.shape[2]
+
+    def prepare(r):
+        for z in range(4):
+            lanes = pl.ds(pl.multiple_of((r * 4 + z) * 2 * depth, 2 * depth), 2 * depth)
+            product_rows[...] = dot(heads_pair[:, lanes], mid_pair[...], ((0,), (0,)))
+            mine = product_rows[pl.ds(pl.multiple_of(at.c * depth, depth), depth)]
+            halves[r, z] = mine.astype(jnp.bfloat16)
+
+    out_job = square_scatter(
+        at, lambda r, half: halves.at[r, pl.ds(2 * half, 2)], out_result, square_scratch, 0, prepare
+    )
+    next(out_job)
+    drive(own_job)
     gate_up_job = exchange(at, lambda b, p: gate_up.at[b], lambda b, p: pieces.at[b], gate_up_sems)
     next(gate_up_job)
-    keys_sum[...] = jnp.zeros_like(keys_sum)
-    values_sum[...] = jnp.zeros_like(values_sum)
-    for r in range(4):
-        pairs[r].wait()
-        mine = out_weight[r, :, at.c].astype(jnp.float32) + halves[r].astype(jnp.float32)
-        halves[r] = mine.astype(jnp.bfloat16)
-    out_job = square_scatter(
-        at,
-        lambda r, half: halves.at[r, pl.ds(2 * half, 2)],
-        out_result,
-        square_scratch,
-    )
-    next(out_job)
-    next(out_job)
-    next(out_job)
-    drive(own_job)
     for i in range(blocks):
         rows = slice(i * QROWS, (i + 1) * QROWS)
         count = (i + 1) * QROWS
@@ -1169,31 +1269,38 @@
 
 
 def attend_backward(
-    grad_rows, queries, keys, values, attended, log_total, start, tables, out_weight, gate_up
+    grad_second, resid_mid, cotangent, feed_gain, queries, keys, values, attended, log_total,
+    start, tables, mixed_heads, gate_up, w_out,
 ):
     length, local = queries.shape
     bf, f32 = jnp.bfloat16, jnp.float32
-    depth, width = out_weight.shape[3:]
+    depth = gate_up.shape[1]
+    rows, width = mixed_heads.shape
     quarter = [VMEM((4, depth, width), bf)] * 2 + [VMEM((2, depth, width), bf)] * 4
     flat, spans = pack_sems(
         [
-            exchange_sems(), quarter + [DMA((6,)), DMA((6,))], [DMA((4,)), DMA((4,))], exchange_sems(),
+            exchange_sems(), quarter + [DMA((6,)), DMA((6,))], [DMA((2,)), DMA((2,))], exchange_sems(),
+            [DMA],
         ]
     )
-    shard = (gate_up.shape[1], 4 * gate_up.shape[2])
+    shard = (depth, 4 * gate_up.shape[2])
     outs = [((length, 3 * local), bf, VMEM), ((4, depth, width), bf, VMEM)] + [(shard, f32, VMEM)] * 2
-    scratch = [VMEM((length, local), bf), VMEM((length, local), f32), VMEM((length, local), f32)]
+    outs += [((rows, width), f32, VMEM), ((2, width), f32, VMEM)]
+    scratch = [VMEM((rows, width), bf), VMEM((width, width), bf)]
+    scratch += [VMEM((length, local), bf), VMEM((length, local), f32), VMEM((length, local), f32)]
     scratch += [VMEM(gate_up.shape, bf), VMEM((4, 4, depth, width), bf)]
+    scratch += [VMEM((2 * rows, width), bf)] * 2 + [VMEM((2 * depth, width), f32)]
     return call(
-        grouped(attend_backward_kernel, 21, spans), [VMEM] * 11 + [HBM], outs, scratch + flat, 4,
-        grad_rows, queries, keys, values, attended, log_total, start, *tables, out_weight, gate_up,
+        grouped(attend_backward_kernel, 32, spans), [VMEM] * 14 + [HBM] * 2, outs, scratch + flat, 4,
+        grad_second, resid_mid, cotangent, feed_gain, queries, keys, values, attended, log_total,
+        start, *tables, mixed_heads, gate_up, w_out,
     )
 
 
 def finish_kernel(
-    partial, normed, grad_mixed, down_partial, out_part, x_ref, gain, grad_mid, feed_sums, bias_sums,
+    w_project, normed, grad_mixed, hidden, grad_out, out_part, x_ref, gain, grad_mid, feed_sums, bias_sums,
     tokens_grad, project_grad, down_grad, out_grad, vector_out,
-    weight, weight_result, pieces, first, sums, arrived, summed, rows_in,
+    weight, weight_result, pieces, first, sums, arrived, summed, rows_in, down_partial, partial,
     line_scratch, project_scratch, down_scratch, out_scratch, piece_sems, vector_sems, row_sems,
 ):
     at = Place()
@@ -1205,14 +1312,27 @@
         spot = pl.ds(pl.multiple_of(r * depth, depth), depth)
         weight[spot] = dot(normed[:, spot], grad_mixed[...], ((0,), (0,))).astype(jnp.bfloat16)
 
+    def prepare_down(r):
+        count = down_grad.shape[0]
+        for i in range(4):
+            pl.when(r == i)(lambda: down_quarter(i, count))
+
+    def down_quarter(i, count):
+        rows_ = slice(i * count, (i + 1) * count)
+        down_partial[rows_] = dot(hidden[:, rows_], grad_out[...], ((0,), (0,))).astype(jnp.bfloat16)
+
     shard = depth // 8
     size = shard // CHUNKS
-    line_job = line_scatter(at, rows_of(partial, rows), first, line_scratch)
+
+    def prepare_rows(z):
+        spot = slice(z * 2 * rows, (z + 1) * 2 * rows)
+        partial[spot] = dot(grad_mixed[spot], w_project[...], ((1,), (1,))).astype(jnp.bfloat16)
+
+    line_job = line_scatter(at, rows_of(partial, rows), first, line_scratch, True, prepare_rows)
     next(line_job)
     out_job = line_scatter(
         at, lambda z, c, k: out_part.at[z, pl.ds(k * size, size)], out_grad, out_scratch, False
     )
-    next(out_job)
 
     def project_work():
         yield from square_scatter(at, row_halves(weight), weight_result, project_scratch, 0, prepare)
@@ -1224,7 +1344,9 @@
         )
 
     project_job = project_work()
-    down_job = square_scatter(at, row_halves(down_partial, 1), down_grad, down_scratch, 1)
+    down_job = square_scatter(
+        at, row_halves(down_partial, 1), down_grad, down_scratch, 1, prepare_down
+    )
 
     def vector_work():
         x = x_ref[...].astype(jnp.float32)
@@ -1268,9 +1390,18 @@
             copy.wait()
         vector_out[...] = summed[at.r] + rows_in[0] + rows_in[1] + rows_in[2]
 
-    drive(line_job, project_job_steps(project_job, 6), down_job)
+    steps(project_job, 3)
+    steps(line_job, 2)
+    next(project_job)
+    steps(line_job, 1)
+    next(project_job)
+    steps(line_job, 1)
+    next(project_job)
+    next(out_job)
+    next(down_job)
+    drive(line_job, out_job, limited(down_job, 3))
     vector_work()
-    drive(project_job, out_job)
+    drive(down_job, project_job)
     inner = pieces.shape[2] // 3
     for b in range(8):
         for p in range(3):
@@ -1278,21 +1409,21 @@
             project_grad[:, lanes] = pieces[b, :, p * inner : (p + 1) * inner].astype(jnp.float32)
 
 
-def project_job_steps(job, count):
+def limited(job, count):
     for _ in range(count):
         next(job)
         yield
 
 
 def finish(
-    partial, normed, grad_mixed, down_partial, out_part, x, gain, grad_mid, feed_sums, bias_sums
+    w_project, normed, grad_mixed, hidden, grad_out, out_part, x, gain, grad_mid, feed_sums, bias_sums
 ):
     bf, f32 = jnp.bfloat16, jnp.float32
     rows, width = x.shape
     inner = grad_mixed.shape[1]
     depth = width // 4
     shard = depth // 8
-    down_owned = (down_partial.shape[0] // 4, width)
+    down_owned = (hidden.shape[1] // 4, width)
     flat, spans = pack_sems(
         [
             line_scatter_scratch(rows, width),
@@ -1310,10 +1441,11 @@
         VMEM((width, inner), bf), VMEM((depth, inner), bf), VMEM((8, shard, inner), bf),
         VMEM((rows, width), f32), VMEM((8, 4, 8, 128), f32), VMEM((8, 4, 8, 128), f32),
         VMEM((4, 8, 128), f32), VMEM((3, 8, 128), f32),
+        VMEM((hidden.shape[1], width), bf), VMEM((8 * rows, width), bf),
     ]
     return call(
-        grouped(finish_kernel, 23, spans), [VMEM] * 10, outs, scratch + flat, 5,
-        partial, normed, grad_mixed, down_partial, out_part, x, gain, grad_mid, feed_sums, bias_sums,
+        grouped(finish_kernel, 26, spans), [VMEM] * 11, outs, scratch + flat, 5,
+        w_project, normed, grad_mixed, hidden, grad_out, out_part, x, gain, grad_mid, feed_sums, bias_sums,
     )
 
 
@@ -1328,7 +1460,7 @@
     local = width // 8
     hidden = down_weight.shape[0]
     shard = attend_gain.shape[0]
-    r, b = lax.axis_index("rows"), lax.axis_index("blk")
+    b = lax.axis_index("blk")
 
     small = jnp.stack([attend_gain, attend_shift, feed_gain, feed_shift])
     zeros = jnp.zeros_like(small)
@@ -1352,48 +1484,27 @@
     bias = vectors[:, 4:6].reshape(32, 256)[:, : 3 * shard].reshape(3, 8, local)
     bias = lax.dynamic_index_in_dim(bias, b, 1, False).reshape(1, -1).astype(f32)
 
-    queries, keys, values, attended, log_total, attended_low, gate_up, w_out = attend_forward(
-        normed_first, w_project, bias, start, tables, gate_up, w_out
-    )
-    w_out = w_out.reshape(width, width)
-    inputs = tokens[0].astype(f32)
-    resid_mid = inputs + dot(attended_low, w_out, ((1,), (0,)))
-    unit_second, inverse_second = norm_stats(resid_mid)
-    normed_second, w_gate_up, grad_out = second_gather(
-        (unit_second * f_gain + f_shift).astype(bf), gate_up.reshape(8 * shard, 8 * hidden), cotangent[0]
-    )
-    both = dot(normed_second, w_gate_up, ((1,), (0,)))
-    gate_value, up_value = both[:, : 4 * hidden], both[:, 4 * hidden :]
-    gate_sigmoid = jax.nn.sigmoid(gate_value)
-    silu = gate_value * gate_sigmoid
-    hidden_low = (silu * up_value).astype(bf)
-    grad_hidden = dot(grad_out, w_down, ((1,), (1,)))
-    grad_gate = grad_hidden * up_value * gate_sigmoid * (1.0 + gate_value * (1.0 - gate_sigmoid))
-    grad_both = jnp.concatenate([grad_gate.astype(bf), (grad_hidden * silu).astype(bf)], axis=1)
-    grad_second = dot(grad_both, w_gate_up, ((1,), (1,))).astype(bf)
-    down_partial = dot(hidden_low, grad_out, ((0,), (0,))).astype(bf)
-    out_partial = dot(hidden_low, w_down, ((1,), (0,))).astype(bf)
-    grad_second, output, gate_up_grad = feed_reduce(grad_second, out_partial, normed_second, grad_both)
+    (
+        queries, keys, values, attended, log_total, attended_low, resid_mid, normed_second, gate_up, w_out
+    ) = attend_forward(
+        normed_first, w_project, bias, start, tables, tokens[0], jnp.stack([f_gain, f_shift]), gate_up, w_out
+    )
+    grad_out, hidden_low, output, grad_second, gate_up_grad = feed(
+        normed_second, gate_up.reshape(8 * shard, 8 * hidden), cotangent[0], w_down
+    )
     output = (resid_mid + output).astype(bf)
-
-    mid_part, f_gain_part, f_shift_part = norm_back(grad_second, unit_second, inverse_second, f_gain)
-    grad_mid = cotangent[0].astype(f32) + mid_part
-    grad_mid_low = grad_mid.astype(bf)
-    grad_attended = dot(grad_mid_low, w_out, ((1,), (1,))).astype(bf)
-    out_partial = dot(attended_low, grad_mid_low, ((0,), (0,))).astype(bf)
-    grad_mixed, out_part, gate_grad, up_grad = attend_backward(
-        grad_attended, queries, keys, values, attended, log_total, start, tables,
-        out_partial.reshape(4, 4, 2, shard, width), gate_up_grad.reshape(8, shard, 8 * hidden),
-    )
-    grad_first = dot(grad_mixed, w_project, ((1,), (1,))).astype(bf)
+    grad_mixed, out_part, gate_grad, up_grad, grad_mid, feed_sums = attend_backward(
+        grad_second, resid_mid, cotangent[0], f_gain[None], queries, keys, values, attended, log_total,
+        start, tables, attended_low, gate_up_grad.reshape(8, shard, 8 * hidden), w_out.reshape(width, width),
+    )
 
     bias_part = jnp.sum(grad_mixed.astype(f32), axis=0).reshape(3, 1, local)
     bias_part = jnp.where(jnp.arange(8)[None, :, None] == b, bias_part, 0.0)
     bias_part = jnp.pad(bias_part.reshape(32, 3 * shard), ((0, 0), (0, 64)))
     bias_part = bias_part.reshape(4, 8, 2, 128).transpose(1, 0, 2, 3)
     grad_tokens, project_grad, down_grad, out_grad, vector = finish(
-        grad_first, normed_first, grad_mixed, down_partial, out_part, tokens[0], a_gain[None], grad_mid,
-        jnp.stack([f_gain_part, f_shift_part]), bias_part,
+        w_project, normed_first, grad_mixed, hidden_low, grad_out, out_part, tokens[0], a_gain[None],
+        grad_mid, feed_sums, bias_part,
     )
     gains = jnp.where(b % 2 == 0, vector[:4, :shard], vector[:4, shard:])
     return (

time: 586 us -> 524 us (0.89)
  matrix products: 57.7 us -> 0 us
    dot_general x9 -> x0, matrix products: 57.7 us -> none  [dot(): lax.dot_general(left, right, (contract, ((), ())), preferred_element_type...]
    pallas_call x6 -> x5, Pallas kernels: 492 us -> 493 us  [call(): pl.pallas_call(kernel, out_shape=[jax.ShapeDtypeStruct(shape, kind) for s...]
where the time goes in v4:
time: 524 us; the launch traced here: 518 us
  Pallas kernels  493 us (94%)
  local copies, waits for them, and re-layouts  13.6 us (3%)
  other arithmetic  9.71 us (2%)
    pallas_call x5, Pallas kernels, call(): pl.pallas_call(kernel, out_shape=[jax.ShapeDtypeStruct(shape, kind) for s...  493 us

profile of v4, /device:TPU:0, one launch (start us, length us, event | category | flops | bytes accessed | tf_op | source)
XLA Modules:
  0.0 517.8 jit_solution(6292730885084479774)
XLA Ops:
  0.6 0.7 convert_element_type.36
  1.3 0.7 pad_bitcast_fusion.1
  2.0 0.7 pad_maximum_fusion.1
  2.8 0.1 pad.17.clone
  2.8 0.7 maximum_maximum_fusion.refs_1_
  3.5 78.5 %shard_map.220 = (bf16[32,16,128]{2,1,0:T(8,128)(2,1)}, bf16[1024,2048]{1,0:T(8,128)(2,1)}, bf16[512,768]{1,0:T(8,128)(2,1)}, bf16[2048,768]{1,0:T(8,128)(2,1)},...) custom-call(bf16[128,2048]{1,0:T(8,128)(2,1)} %bitcast.50, ...), custom_call_target="tpu_custom_call" | custom-call | tf_op jit(solution)/shard_map/pallas_call | solution.py:720
  82.0 0.9 slice.57
  82.9 0.1 reshape.138
  83.0 0.6 convert.4.refs_2_
  83.6 1.0 slice_convert_fusion
  84.7 0.6 pad_maximum_fusion.refs_8_
  85.3 53.5 %shard_map.221 = (bf16[1024,256]{1,0:T(8,128)(2,1)}, bf16[1024,256]{1,0:T(8,128)(2,1)}, bf16[1024,256]{1,0:T(8,128)(2,1)}, f32[1024,256]{1,0:T(8,128)}, f32[1024...) custom-call(bf16[1024,2048]{1,0:T(8,128)(2,1)} %get-tuple-element.48, ...), custom_call_target="tpu_custom_call" | custom-call | tf_op jit(solution)/shard_map/pallas_call | solution.py:720
  138.8 181.1 %shard_map.222 = (bf16[1024,2048]{1,0:T(8,128)(2,1)}, bf16[1024,704]{1,0:T(8,128)(2,1)}, f32[128,2048]{1,0:T(8,128)}, f32[128,2048]{1,0:T(8,128)}, bf16[512,1408]{1,0:T(8,128)(2,1)}) custom-call(bf16[128,2048]{1,0:T(8,128)(2,1)} %get-tuple-element.58.refs_0_, bf16[512,1408]{1,0:T(8,128)(2,1)} %bitcast.56, bf16[128,2048]{1,0:T(8,128)(2,1)} %bitcast.53, ...), custom_call_target="tpu_custom_call" | custom-call | tf_op jit(solution)/shard_map/pallas_call | solution.py:720
  320.0 2.1 fusion
  322.1 66.4 %shard_map.223 = (bf16[1024,768]{1,0:T(8,128)(2,1)}, bf16[4,64,2048]{2,1,0:T(8,128)(2,1)}, f32[64,5632]{1,0:T(8,128)}, f32[64,5632]{1,0:T(8,128)}, f32[128,2048]{1,0:T(8,128)}, /*index=5*/f32[2,2048]{1,0:T(2,128)}) custom-call(f32[128,2048]{1,0:T(8,128)} %get-tuple-element.62.refs_0_, f32[128,2048]{1,0:T(8,128)} %get-tuple-element.57.refs_1_, ...), custom_call_target="tpu_custom_call" | custom-call | tf_op jit(solution)/shard_map/pallas_call | solution.py:720
  388.5 0.6 add.66
  389.1 1.7 convert_reduce_fusion
  390.9 0.1 select_n.42
  391.0 0.6 copy.47
  391.6 113.8 %shard_map.224 = (f32[128,2048]{1,0:T(8,128)}, f32[64,6144]{1,0:T(8,128)}, f32[176,2048]{1,0:T(8,128)}, f32[64,2048]{1,0:T(8,128)}, f32[8,128]{1,0:T(8,128)}) custom-call(bf16[2048,768]{1,0:T(8,128)(2,1)} %get-tuple-element.49.refs_1_.refs_0_, bf16[1024,2048]{1,0:T(8,128)(2,1)} %get-tuple-element.48.refs_0_.refs_1_, ...), custom_call_target="tpu_custom_call" | custom-call | tf_op jit(solution)/shard_map/pallas_call | solution.py:720
  505.4 0.9 slice_select_fusion
  506.3 0.5 slice_bitcast_fusion.1
  506.8 1.2 slice_bitcast_fusion
  508.1 2.3 copy.55
  510.4 1.1 copy.56
  511.5 0.2 copy-done.5
  511.7 0.8 copy.57
  512.5 1.1 copy.58
  513.6 0.8 copy-done.2
  514.4 1.1 copy.59
  515.5 0.8 copy-done.4
  516.3 1.1 copy.60
  (24 shorter events, 0.3 us)
Async XLA Ops:
  84.7 54.2 %copy-start.6 = (f32[16,1,128]{2,0,1:T(8,128)}, f32[16,1,128]{2,0,1:T(8,128)S(1)}, u32[]{:S(2)}) copy-start(f32[16,1,128]{2,0,1:T(8,128)S(1)} %add.61) | copy-start | bytes 24580
  138.8 181.1 %copy-start = (f32[128,2048]{1,0:T(8,128)S(1)}, f32[128,2048]{1,0:T(8,128)}, u32[]{:S(2)}) copy-start(f32[128,2048]{1,0:T(8,128)} %get-tuple-element.57.refs_1_) | copy-start | bytes 3145732
  505.4 5.0 copy-start.1
  510.3 1.4 copy-start.5
  510.3 2.2 copy-start.3
  512.5 1.9 copy-start.2
  514.4 1.9 copy-start.4

commit v5 on v4

--- a/solution.py
+++ b/solution.py
@@ -1056,10 +1056,10 @@
 
 
 def feed_kernel(
-    own, gate_up, cotangent, w_down,
-    grad_out, hidden_out, output_sum, result, weight_result,
-    normed, w_gate_up, values, out_partial, partial, weight,
-    line_sems, other_sems, square_sems, out_scratch, scatter_scratch, square_scratch,
+    own, gate_up, cotangent, w_down, resid_mid, feed_gain, out_weight,
+    grad_out, hidden_out, output, weight_result, grad_mid, feed_sums, grad,
+    normed, w_gate_up, values, out_partial, partial, output_sum, result, grad_rows,
+    line_sems, other_sems, square_sems, out_scratch, scatter_scratch, square_scratch, own_sems, load_sems,
 ):
     at = Place()
     at.barrier()
@@ -1074,6 +1074,10 @@
     def rows_at(z):
         return pl.ds(pl.multiple_of(z * 2 * count, 2 * count), 2 * count)
 
+    def hidden_back(z):
+        rows = rows_at(z)
+        partial[rows, :hidden] = dot(grad_out[rows], w_down[...], ((1,), (1,))).astype(jnp.bfloat16)
+
     def forward(z):
         rows = rows_at(z)
         both = dot(normed[rows], w_gate_up[...], ((1,), (0,)))
@@ -1087,13 +1091,25 @@
         rows = rows_at(z)
         both = values[rows].astype(jnp.float32)
         gate_value, up_value = both[:, :hidden], both[:, hidden:]
-        grad_hidden = dot(grad_out[rows], w_down[...], ((1,), (1,)))
+        grad_hidden = partial[rows, :hidden].astype(jnp.float32)
         gate_sigmoid = 1.0 / (1.0 + jnp.exp(-gate_value))
         silu = gate_value * gate_sigmoid
         grad_gate = grad_hidden * up_value * gate_sigmoid * (1.0 + gate_value * (1.0 - gate_sigmoid))
         grads = jnp.concatenate([grad_gate, grad_hidden * silu], axis=1).astype(jnp.bfloat16)
         values[rows] = grads
         partial[rows] = dot(grads, w_gate_up[...], ((1,), (1,))).astype(jnp.bfloat16)
+
+    def near(i):
+        return at.z + (i + 1) // 2 * (1 - 2 * lax.rem(i, 2))
+
+    def far(i):
+        return at.z + 3 * (2 * i - 1)
+
+    def each(count, place, work):
+        @pl.loop(0, count)
+        def _(i):
+            z = place(i)
+            pl.when((z >= 0) & (z <= 3))(lambda: work(z))
 
     out_job = line_scatter(at, rows_of(out_partial, count), output_sum, out_scratch)
     next(line_job)
@@ -1103,13 +1119,14 @@
         steps(line_job, 1)
         steps(square_job, 1)
         steps(other_job, 1)
+    each(5, near, hidden_back)
+    drive(square_job)
+    each(5, near, forward)
     steps(line_job, 2)
-    drive(square_job)
-    pl.loop(0, 2)(forward)
-    steps(other_job, 1)
-    pl.loop(2, 4)(forward)
+    each(2, far, forward)
     next(out_job)
-    steps(other_job, 1)
+    steps(other_job, 2)
+    each(2, far, hidden_back)
     for z in range(4):
         backward(z)
         steps(out_job, 1)
@@ -1120,60 +1137,87 @@
     def prepare(r):
         for half in range(2):
             spot = pl.ds(pl.multiple_of(r * depth + half * step, step), step)
-            weight[spot] = dot(normed[:, spot], values[...], ((0,), (0,))).astype(jnp.bfloat16)
+            w_gate_up[spot] = dot(normed[:, spot], values[...], ((0,), (0,))).astype(jnp.bfloat16)
 
     scatter_job = line_scatter(at, rows_of(partial, count), result, scatter_scratch)
-    weight_job = square_scatter(at, row_halves(weight), weight_result, square_scratch, 0, prepare)
+    weight_job = square_scatter(at, row_halves(w_gate_up), weight_result, square_scratch, 0, prepare)
     next(scatter_job)
     steps(weight_job, 3)
-    drive(out_job, scatter_job, weight_job, line_job, other_job)
-
-
-def feed(own, gate_up, cotangent, w_down):
+    drive(scatter_job, limited(weight_job, 2), line_job)
+    half = out_partial.shape[0]
+    loads = [
+        pltpu.make_async_copy(out_weight.at[pl.ds(i * half, half)], place, load_sems[0].at[i])
+        for i, place in enumerate((normed, partial))
+    ]
+    for load in loads:
+        load.start()
+    unit, inverse = norm_stats(resid_mid[...])
+    mid_part, gain_part, shift_part = norm_back(result[...], unit, inverse, feed_gain[...])
+    total = cotangent[...].astype(jnp.float32) + mid_part
+    grad_mid[...] = total
+    low = total.astype(jnp.bfloat16)
+    feed_sums[0:1] = gain_part[None]
+    feed_sums[1:2] = shift_part[None]
+    for i, place in enumerate((normed, partial)):
+        loads[i].wait()
+        grad_rows[:, i * half : (i + 1) * half] = dot(low, place[...], ((1,), (1,))).astype(jnp.bfloat16)
+    local = grad.shape[1]
+    own_job = exchange(
+        at,
+        lambda b, p: grad_rows.at[:, pl.ds(pl.multiple_of(b * local, local), local)],
+        lambda b, p: grad.at[pl.ds(pl.multiple_of(b * count, count), count)],
+        own_sems,
+    )
+    next(own_job)
+    drive(out_job, weight_job, other_job)
+    output[...] = (resid_mid[...] + output_sum[...]).astype(jnp.bfloat16)
+    drive(own_job)
+
+
+def feed(own, gate_up, cotangent, w_down, resid_mid, feed_gain, w_out):
     bf, f32 = jnp.bfloat16, jnp.float32
     rows, width = own.shape
     hidden = w_down.shape[0]
     owned = (width // 4, 2 * hidden)
-    full = (8 * rows, width)
+    full, mine = (8 * rows, width), (rows, width)
     flat, spans = pack_sems(
         [
             line_gather_sems(), line_gather_sems(), square_gather_sems(),
             line_scatter_scratch(rows, width), line_scatter_scratch(rows, width),
-            square_scatter_scratch(*owned),
+            square_scatter_scratch(*owned), exchange_sems(), [DMA((2,))],
         ]
     )
-    outs = [(full, bf, VMEM), ((8 * rows, hidden), bf, VMEM)]
-    outs += [((rows, width), f32, VMEM)] * 2 + [(owned, bf, VMEM)]
+    outs = [(full, bf, VMEM), ((8 * rows, hidden), bf, VMEM), (mine, bf, VMEM), (owned, bf, VMEM)]
+    outs += [(mine, f32, VMEM), ((2, width), f32, VMEM), ((8 * rows, width // 8), bf, VMEM)]
     scratch = [
         VMEM(full, bf), VMEM((width, 2 * hidden), bf), VMEM((8 * rows, 2 * hidden), bf), VMEM(full, bf),
-        VMEM(full, bf), VMEM((width, 2 * hidden), bf),
+        VMEM(full, bf), VMEM(mine, f32), VMEM(mine, f32), VMEM(mine, bf),
     ]
     return call(
-        grouped(feed_kernel, 15, spans), [VMEM, HBM, VMEM, VMEM], outs, scratch + flat, 2,
-        own, gate_up, cotangent, w_down,
-    )
+        grouped(feed_kernel, 22, spans), [VMEM, HBM, VMEM, VMEM, VMEM, VMEM, HBM], outs, scratch + flat, 2,
+        own, gate_up, cotangent, w_down, resid_mid, feed_gain, w_out,
+    )
+
+
+def limited(job, count):
+    for _ in range(count):
+        next(job)
+        yield
 
 
 def attend_backward_kernel(
-    grad_second, resid_mid, cotangent, feed_gain, queries, keys, values, attended, log_total,
-    start, cosine, minus, plus, mixed_heads, gate_up, out_weight,
-    grad_mixed, out_result, gate_result, up_result, grad_mid, feed_sums,
-    grad_rows, w_out, grad, keys_sum, values_sum, pieces, halves, heads_pair, mid_pair, product_rows,
-    own_sems, square_scratch, pair_sems, gate_up_sems, load_sems,
+    grad, grad_mid, queries, keys, values, attended, log_total,
+    start, cosine, minus, plus, mixed_heads, gate_up,
+    grad_mixed, out_result, gate_result, up_result,
+    keys_sum, values_sum, pieces, halves, heads_pair, mid_pair, product_rows,
+    square_scratch, pair_sems, gate_up_sems,
 ):
     at = Place()
-    load = pltpu.make_async_copy(out_weight, w_out, load_sems[0])
-    load.start()
-    unit, inverse = norm_stats(resid_mid[...])
-    incoming = grad_second[...]
-    mid_part, gain_part, shift_part = norm_back(incoming, unit, inverse, feed_gain[...])
-    total = cotangent[...].astype(jnp.float32) + mid_part
-    grad_mid[...] = total
-    mid_pair[:128] = total.astype(jnp.bfloat16)
+    at.barrier()
+    gate_up_job = exchange(at, lambda b, p: gate_up.at[b], lambda b, p: pieces.at[b], gate_up_sems)
+    next(gate_up_job)
+    mid_pair[:128] = grad_mid[...].astype(jnp.bfloat16)
     heads_pair[:128] = mixed_heads[...]
-    feed_sums[0:1] = gain_part[None]
-    feed_sums[1:2] = shift_part[None]
-    at.barrier()
     pair_send, pair_recv = pair_sems
     pairs = [
         remote(ref.at[pl.ds(0, 128)], ref.at[pl.ds(128, 128)], pair_send.at[i], pair_recv.at[i], at.r, at.sibling)
@@ -1181,18 +1225,9 @@
     ]
     for copy in pairs:
         copy.start()
-    load.wait()
-    grad_rows[...] = dot(mid_pair[:128], w_out[...], ((1,), (1,))).astype(jnp.bfloat16)
     length, local = queries.shape
     scale = 1.0 / math.sqrt(local * 8 // HEADS)
     blocks = length // QROWS
-    own_job = exchange(
-        at,
-        lambda b, p: grad_rows.at[:, pl.ds(pl.multiple_of(b * local, local), local)],
-        lambda b, p: grad.at[pl.ds(pl.multiple_of(b * 128, 128), 128)],
-        own_sems,
-    )
-    next(own_job)
     keys_sum[...] = jnp.zeros_like(keys_sum)
     values_sum[...] = jnp.zeros_like(values_sum)
     for copy in pairs:
@@ -1209,10 +1244,7 @@
     out_job = square_scatter(
         at, lambda r, half: halves.at[r, pl.ds(2 * half, 2)], out_result, square_scratch, 0, prepare
     )
-    next(out_job)
-    drive(own_job)
-    gate_up_job = exchange(at, lambda b, p: gate_up.at[b], lambda b, p: pieces.at[b], gate_up_sems)
-    next(gate_up_job)
+    steps(out_job, 3)
     for i in range(blocks):
         rows = slice(i * QROWS, (i + 1) * QROWS)
         count = (i + 1) * QROWS
@@ -1264,13 +1296,12 @@
     for b in range(8):
         for r in range(4):
             source = slice((8 * r + b) * hidden, (8 * r + b + 1) * hidden)
-            gate_result[:, source] = pieces[b, :, r * hidden : (r + 1) * hidden].astype(jnp.float32)
-            up_result[:, source] = pieces[b, :, (4 + r) * hidden : (5 + r) * hidden].astype(jnp.float32)
+            gate_result[:, source] = pieces[b, :, r * hidden : (r + 1) * hidden]
+            up_result[:, source] = pieces[b, :, (4 + r) * hidden : (5 + r) * hidden]
 
 
 def attend_backward(
-    grad_second, resid_mid, cotangent, feed_gain, queries, keys, values, attended, log_total,
-    start, tables, mixed_heads, gate_up, w_out,
+    grad, grad_mid, queries, keys, values, attended, log_total, start, tables, mixed_heads, gate_up
 ):
     length, local = queries.shape
     bf, f32 = jnp.bfloat16, jnp.float32
@@ -1278,39 +1309,43 @@
     rows, width = mixed_heads.shape
     quarter = [VMEM((4, depth, width), bf)] * 2 + [VMEM((2, depth, width), bf)] * 4
     flat, spans = pack_sems(
-        [
-            exchange_sems(), quarter + [DMA((6,)), DMA((6,))], [DMA((2,)), DMA((2,))], exchange_sems(),
-            [DMA],
-        ]
+        [quarter + [DMA((6,)), DMA((6,))], [DMA((2,)), DMA((2,))], exchange_sems()]
     )
     shard = (depth, 4 * gate_up.shape[2])
-    outs = [((length, 3 * local), bf, VMEM), ((4, depth, width), bf, VMEM)] + [(shard, f32, VMEM)] * 2
-    outs += [((rows, width), f32, VMEM), ((2, width), f32, VMEM)]
-    scratch = [VMEM((rows, width), bf), VMEM((width, width), bf)]
-    scratch += [VMEM((length, local), bf), VMEM((length, local), f32), VMEM((length, local), f32)]
+    outs = [((length, 3 * local), bf, VMEM), ((4, depth, width), bf, VMEM)] + [(shard, bf, VMEM)] * 2
+    scratch = [VMEM((length, local), f32), VMEM((length, local), f32)]
     scratch += [VMEM(gate_up.shape, bf), VMEM((4, 4, depth, width), bf)]
     scratch += [VMEM((2 * rows, width), bf)] * 2 + [VMEM((2 * depth, width), f32)]
     return call(
-        grouped(attend_backward_kernel, 32, spans), [VMEM] * 14 + [HBM] * 2, outs, scratch + flat, 4,
-        grad_second, resid_mid, cotangent, feed_gain, queries, keys, values, attended, log_total,
-        start, *tables, mixed_heads, gate_up, w_out,
+        grouped(attend_backward_kernel, 24, spans), [VMEM] * 12 + [HBM], outs, scratch + flat, 4,
+        grad, grad_mid, queries, keys, values, attended, log_total, start, *tables, mixed_heads, gate_up,
     )
 
 
 def finish_kernel(
-    w_project, normed, grad_mixed, hidden, grad_out, out_part, x_ref, gain, grad_mid, feed_sums, bias_sums,
-    tokens_grad, project_grad, down_grad, out_grad, vector_out,
-    weight, weight_result, pieces, first, sums, arrived, summed, rows_in, down_partial, partial,
-    line_scratch, project_scratch, down_scratch, out_scratch, piece_sems, vector_sems, row_sems,
+    w_project, grad_mixed, out_part, x_ref, gain, feed_sums, bias_sums, normed_all, hidden_all,
+    grad_out_all, tokens_part, project_grad, down_grad, out_grad, vector_out,
+    weight, weight_result, pieces, first, sums, arrived, summed, rows_in, down_partial, partial, overlap,
+    normed, hidden, grad_out,
+    line_scratch, project_scratch, down_scratch, out_scratch, piece_sems, vector_sems, row_sems, load_sems,
 ):
     at = Place()
+    loads = [
+        pltpu.make_async_copy(*pair, load_sems[0].at[i])
+        for i, pair in enumerate(((normed_all, normed), (hidden_all, hidden), (grad_out_all, grad_out)))
+    ]
+    for load in loads:
+        load.start()
     at.barrier(diagonal=True)
     rows, width = first.shape
     depth = weight_result.shape[0]
 
     def prepare(r):
         spot = pl.ds(pl.multiple_of(r * depth, depth), depth)
-        weight[spot] = dot(normed[:, spot], grad_mixed[...], ((0,), (0,))).astype(jnp.bfloat16)
+        product = dot(normed[:, spot], grad_mixed[...], ((0,), (0,)))
+        weight[spot] = product.astype(jnp.bfloat16)
+        found = jnp.sum(product * w_project[spot].astype(jnp.float32), axis=1, keepdims=True)
+        overlap[spot] = jnp.broadcast_to(found, (depth, 128))
 
     def prepare_down(r):
         count = down_grad.shape[0]
@@ -1329,7 +1364,6 @@
         partial[spot] = dot(grad_mixed[spot], w_project[...], ((1,), (1,))).astype(jnp.bfloat16)
 
     line_job = line_scatter(at, rows_of(partial, rows), first, line_scratch, True, prepare_rows)
-    next(line_job)
     out_job = line_scatter(
         at, lambda z, c, k: out_part.at[z, pl.ds(k * size, size)], out_grad, out_scratch, False
     )
@@ -1349,20 +1383,16 @@
     )
 
     def vector_work():
-        x = x_ref[...].astype(jnp.float32)
-        centered = x - jnp.mean(x, axis=1, keepdims=True)
-        inverse = lax.rsqrt(jnp.mean(centered * centered, axis=1, keepdims=True) + epsilon)
-        unit = centered * inverse
-        incoming = first[...]
-        product = incoming * unit
-        parts = jnp.concatenate(
-            [
-                jnp.sum(product, axis=0, keepdims=True),
-                jnp.sum(incoming, axis=0, keepdims=True),
-                feed_sums[...],
-            ],
-            axis=0,
-        )
+        column = jnp.sum(grad_mixed[...].astype(jnp.float32), axis=0, keepdims=True)
+        high = column.astype(jnp.bfloat16)
+        low = (column - high.astype(jnp.float32)).astype(jnp.bfloat16)
+        row = lax.broadcasted_iota(jnp.int32, (16, column.shape[1]), 0)
+        both = jnp.where(row == 0, high, jnp.where(row == 1, low, jnp.zeros_like(low)))
+        plain = dot(both, w_project[...], ((1,), (1,)))
+        times = jnp.concatenate(
+            [jnp.transpose(overlap[t * 128 : t * 128 + 128])[0:1] for t in range(width // 128)], axis=1
+        )
+        parts = jnp.concatenate([times, plain[0:1] + plain[1:2], feed_sums[...]], axis=0)
         for b in range(8):
             for r in range(4):
                 lanes = slice((4 * r + b // 2) * 128, (4 * r + b // 2 + 1) * 128)
@@ -1371,12 +1401,7 @@
                 sums[b, r, 6:8] = jnp.zeros((2, 128), jnp.float32)
         spread = exchange(at, lambda b, p: sums.at[b], lambda b, p: arrived.at[b], vector_sems)
         next(spread)
-        unit_grad = incoming * gain[...]
-        tokens_grad[...] = grad_mid[...] + inverse * (
-            unit_grad
-            - jnp.mean(unit_grad, axis=1, keepdims=True)
-            - unit * jnp.mean(unit_grad * unit, axis=1, keepdims=True)
-        )
+        yield
         drive(spread)
         summed[...] = jnp.sum(arrived[...], axis=0)
         send, recv = row_sems
@@ -1386,37 +1411,57 @@
         ]
         for copy in copies:
             copy.start()
+        yield
         for copy in copies:
             copy.wait()
         vector_out[...] = summed[at.r] + rows_in[0] + rows_in[1] + rows_in[2]
 
+    def tokens_work():
+        unit, inverse = norm_stats(x_ref[...].astype(jnp.float32))
+        part, _, _ = norm_back(first[...], unit, inverse, gain[...])
+        tokens_part[...] = part
+
+    vector_job = vector_work()
+    next(out_job)
+    next(out_job)
+    next(line_job)
+    next(out_job)
+    loads[0].wait()
     steps(project_job, 3)
-    steps(line_job, 2)
+    next(out_job)
+    next(line_job)
+    next(out_job)
+    next(line_job)
     next(project_job)
-    steps(line_job, 1)
+    loads[1].wait()
+    loads[2].wait()
+    steps(down_job, 3)
+    next(out_job)
+    next(line_job)
     next(project_job)
-    steps(line_job, 1)
+    next(vector_job)
+    next(line_job)
     next(project_job)
     next(out_job)
+    next(vector_job)
+    next(line_job)
     next(down_job)
-    drive(line_job, out_job, limited(down_job, 3))
-    vector_work()
-    drive(down_job, project_job)
+    next(line_job)
+    drive(out_job)
+    drive(vector_job)
+    drive(line_job)
+    tokens_work()
+    drive(down_job)
+    drive(project_job)
     inner = pieces.shape[2] // 3
     for b in range(8):
         for p in range(3):
             lanes = slice(p * width + b * inner, p * width + (b + 1) * inner)
-            project_grad[:, lanes] = pieces[b, :, p * inner : (p + 1) * inner].astype(jnp.float32)
-
-
-def limited(job, count):
-    for _ in range(count):
-        next(job)
-        yield
+            project_grad[:, lanes] = pieces[b, :, p * inner : (p + 1) * inner]
 
 
 def finish(
-    w_project, normed, grad_mixed, hidden, grad_out, out_part, x, gain, grad_mid, feed_sums, bias_sums
+    w_project, normed, grad_mixed, hidden, grad_out, out_part, x, gain, feed_sums, bias_sums
 ):
     bf, f32 = jnp.bfloat16, jnp.float32
     rows, width = x.shape
@@ -1430,23 +1475,43 @@
             square_scatter_scratch(depth, inner),
             square_scatter_scratch(*down_owned, 1),
             line_scatter_scratch(shard, width),
-            exchange_sems(), exchange_sems(), [DMA((3,)), DMA((3,))],
+            exchange_sems(), exchange_sems(), [DMA((3,)), DMA((3,))], [DMA((3,))],
         ]
     )
     outs = [
-        ((rows, width), f32, VMEM), ((shard, 8 * inner), f32, VMEM), (down_owned, f32, VMEM),
-        ((shard, width), f32, VMEM), ((8, 128), f32, VMEM),
+        ((rows, width), f32, VMEM), ((shard, 8 * inner), bf, VMEM), (down_owned, bf, VMEM),
+        ((shard, width), bf, VMEM), ((8, 128), f32, VMEM),
     ]
     scratch = [
         VMEM((width, inner), bf), VMEM((depth, inner), bf), VMEM((8, shard, inner), bf),
         VMEM((rows, width), f32), VMEM((8, 4, 8, 128), f32), VMEM((8, 4, 8, 128), f32),
         VMEM((4, 8, 128), f32), VMEM((3, 8, 128), f32),
         VMEM((hidden.shape[1], width), bf), VMEM((8 * rows, width), bf),
+        VMEM((width, 128), f32), VMEM(normed.shape, bf), VMEM(hidden.shape, bf), VMEM(grad_out.shape, bf),
     ]
     return call(
-        grouped(finish_kernel, 26, spans), [VMEM] * 11, outs, scratch + flat, 5,
-        w_project, normed, grad_mixed, hidden, grad_out, out_part, x, gain, grad_mid, feed_sums, bias_sums,
-    )
+        grouped(finish_kernel, 29, spans), [VMEM] * 7 + [HBM] * 3, outs, scratch + flat, 5,
+        w_project, grad_mixed, out_part, x, gain, feed_sums, bias_sums, normed, hidden, grad_out,
+    )
+
+
+def widen_kernel(part, base, *refs):
+    count = len(refs) // 2
+    sources, total, results = refs[:count], refs[count], refs[count + 1 :]
+    total[...] = part[...] + base[...]
+    for source, result in zip(sources, results):
+        result[...] = source[...].astype(jnp.float32)
+
+
+def widen(part, base, *arrays):
+    kinds = [jax.ShapeDtypeStruct(array.shape, jnp.float32) for array in (part,) + arrays]
+    return pl.pallas_call(
+        widen_kernel,
+        out_shape=kinds,
+        in_specs=[pl.BlockSpec(memory_space=VMEM)] * (2 + len(arrays)),
+        out_specs=[pl.BlockSpec(memory_space=VMEM)] * len(kinds),
+        compiler_params=pltpu.CompilerParams(vmem_limit_bytes=LIMIT),
+    )(part, base, *arrays)
 
 
 def fast_body(
@@ -1489,26 +1554,30 @@
     ) = attend_forward(
         normed_first, w_project, bias, start, tables, tokens[0], jnp.stack([f_gain, f_shift]), gate_up, w_out
     )
-    grad_out, hidden_low, output, grad_second, gate_up_grad = feed(
-        normed_second, gate_up.reshape(8 * shard, 8 * hidden), cotangent[0], w_down
-    )
-    output = (resid_mid + output).astype(bf)
-    grad_mixed, out_part, gate_grad, up_grad, grad_mid, feed_sums = attend_backward(
-        grad_second, resid_mid, cotangent[0], f_gain[None], queries, keys, values, attended, log_total,
-        start, tables, attended_low, gate_up_grad.reshape(8, shard, 8 * hidden), w_out.reshape(width, width),
+    grad_out, hidden_low, output, gate_up_grad, grad_mid, feed_sums, grad = feed(
+        normed_second, gate_up.reshape(8 * shard, 8 * hidden), cotangent[0], w_down, resid_mid, f_gain[None],
+        w_out.reshape(width, width),
+    )
+    grad_mixed, out_part, gate_grad, up_grad = attend_backward(
+        grad, grad_mid, queries, keys, values, attended, log_total, start, tables, attended_low,
+        gate_up_grad.reshape(8, shard, 8 * hidden),
     )
 
     bias_part = jnp.sum(grad_mixed.astype(f32), axis=0).reshape(3, 1, local)
     bias_part = jnp.where(jnp.arange(8)[None, :, None] == b, bias_part, 0.0)
     bias_part = jnp.pad(bias_part.reshape(32, 3 * shard), ((0, 0), (0, 64)))
     bias_part = bias_part.reshape(4, 8, 2, 128).transpose(1, 0, 2, 3)
-    grad_tokens, project_grad, down_grad, out_grad, vector = finish(
+    tokens_part, project_grad, down_grad, out_grad, vector = finish(
         w_project, normed_first, grad_mixed, hidden_low, grad_out, out_part, tokens[0], a_gain[None],
-        grad_mid, feed_sums, bias_part,
+        feed_sums, bias_part,
+    )
+    grad_tokens, project_grad, down_grad, out_grad, gate_grad, up_grad = widen(
+        tokens_part, grad_mid, project_grad, down_grad, out_grad, gate_grad, up_grad
     )
     gains = jnp.where(b % 2 == 0, vector[:4, :shard], vector[:4, shard:])
+    gain_grad = (gains[0] - attend_shift.astype(f32) * gains[1]) / attend_gain.astype(f32)
     return (
-        output[None], grad_tokens[None], gains[0], gains[1], project_grad,
+        output[None], grad_tokens[None], gain_grad, gains[1], project_grad,
         vector[4:6].reshape(-1)[: 3 * shard], out_grad, gains[2], gains[3], gate_grad, up_grad, down_grad,
     )
 

time: 524 us -> 503 us (0.960)
  Pallas kernels: 493 us -> 480 us
  local copies, waits for them, and re-layouts: 13.6 us -> 5.07 us
    pallas_call x5, Pallas kernels: 493 us -> 475 us  [call(): pl.pallas_call(kernel, out_shape=[jax.ShapeDtypeStruct(shape, kind) for s...]
    unnamed x21 -> x10, local copies, waits for them, and re-layouts: 9.34 us -> 0.82 us
    pallas_call x0 -> x1, Pallas kernels: none -> 5.69 us  [widen(): pl.pallas_call(widen_kernel, out_shape=kinds, in_specs=[pl.BlockSpec(memo...]
where the time goes in v5:
time: 503 us; the launch traced here: 494 us
  Pallas kernels  480 us (95%)
  other arithmetic  8.05 us (2%)
  local copies, waits for them, and re-layouts  5.07 us (1%)
    pallas_call x5, Pallas kernels, call(): pl.pallas_call(kernel, out_shape=[jax.ShapeDtypeStruct(shape, kind) for s...  475 us

profile of v5, /device:TPU:0, one launch (start us, length us, event | category | flops | bytes accessed | tf_op | source)
XLA Modules:
  0.0 494.5 jit_solution(228457320517319816)
XLA Ops:
  0.7 0.7 convert_element_type.39
  1.3 0.7 pad_bitcast_fusion.1
  2.0 0.1 pad.17.clone
  2.1 0.7 pad_maximum_fusion.1
  2.8 0.1 pad_select_fusion
  2.9 0.7 maximum_maximum_fusion.refs_1_
  3.5 78.5 %shard_map.220 = (bf16[32,16,128]{2,1,0:T(8,128)(2,1)}, bf16[1024,2048]{1,0:T(8,128)(2,1)}, bf16[512,768]{1,0:T(8,128)(2,1)}, bf16[2048,768]{1,0:T(8,128)(2,1)},...) custom-call(bf16[128,2048]{1,0:T(8,128)(2,1)} %bitcast.52, ...), custom_call_target="tpu_custom_call" | custom-call | tf_op jit(solution)/shard_map/pallas_call | solution.py:720
  82.1 0.9 slice.58
  82.9 1.0 slice_convert_fusion
  83.9 0.1 reshape.138
  84.0 0.6 convert.4.refs_2_
  84.7 0.6 add.62
  85.3 0.0 copy-start.1
  85.3 0.6 pad_maximum_fusion.refs_8_
  85.9 53.5 %shard_map.221 = (bf16[1024,256]{1,0:T(8,128)(2,1)}, bf16[1024,256]{1,0:T(8,128)(2,1)}, bf16[1024,256]{1,0:T(8,128)(2,1)}, f32[1024,256]{1,0:T(8,128)}, f32[1024...) custom-call(bf16[1024,2048]{1,0:T(8,128)(2,1)} %get-tuple-element.54, ...), custom_call_target="tpu_custom_call" | custom-call | tf_op jit(solution)/shard_map/pallas_call | solution.py:720
  139.5 0.0 copy-done.1
  139.5 191.8 %shard_map.222 = (bf16[1024,2048]{1,0:T(8,128)(2,1)}, bf16[1024,704]{1,0:T(8,128)(2,1)}, bf16[128,2048]{1,0:T(8,128)(2,1)}, bf16[512,1408]{1,0:T(8,128)(2,1)}, f...) custom-call(bf16[128,2048]{1,0:T(8,128)(2,1)} %get-tuple-element.63.refs_0_, ...), custom_call_target="tpu_custom_call" | custom-call | tf_op jit(solution)/shard_map/pallas_call | solution.py:720
  331.3 52.7 %shard_map.223 = (bf16[1024,768]{1,0:T(8,128)(2,1)}, bf16[4,64,2048]{2,1,0:T(8,128)(2,1)}, bf16[64,5632]{1,0:T(8,128)(2,1)}, bf16[64,5632]{1,0:T(8,128)(2,1)}) custom-call(bf16[1024,256]{1,0:T(8,128)(2,1)} %get-tuple-element.69.refs_0_, f32[128,2048]{1,0:T(8,128)} %get-tuple-element.70.refs_1_.base, bf16[1024,256]{1,0:T(8,128)(2,1)} %get-tuple-element.71.refs_2_, ...), custom_call_target="tpu_custom_call" | custom-call | tf_op jit(solution)/shard_map/pallas_call | solution.py:720
  384.0 1.7 convert_reduce_fusion
  385.7 0.1 broadcast_select_fusion
  385.8 0.1 select_n.42
  385.9 0.6 copy.47
  386.5 98.1 %shard_map.224 = (f32[128,2048]{1,0:T(8,128)}, bf16[64,6144]{1,0:T(8,128)(2,1)}, bf16[176,2048]{1,0:T(8,128)(2,1)}, bf16[64,2048]{1,0:T(8,128)(2,1)}, f32[8,128]{1,0:T(8,128)}) custom-call(bf16[2048,768]{1,0:T(8,128)(2,1)} %get-tuple-element.55.refs_1_.refs_0_, bf16[1024,768]{1,0:T(8,128)(2,1)} %get-tuple-element.78.refs_1_, ...), custom_call_target="tpu_custom_call" | custom-call | tf_op jit(solution)/shard_map/pallas_call | solution.py:720
  484.6 1.2 slice_bitcast_fusion
  485.9 0.8 slice_select_fusion
  486.7 0.5 slice_bitcast_fusion.1
  487.2 0.0 copy-done.2
  487.3 0.0 copy-done.3
  487.3 0.5 fusion
  487.8 5.7 %shard_map.225 = (f32[128,2048]{1,0:T(8,128)}, f32[64,6144]{1,0:T(8,128)}, f32[176,2048]{1,0:T(8,128)}, f32[64,2048]{1,0:T(8,128)}, f32[64,5632]{1,0:T(8,128)}, /*index=5*/f32[64,5632]{1,0:T(8,128)}) custom-call(f32[128,2048]{1,0:T(8,128)} %get-tuple-element.83.part, f32[128,2048]{1,0:T(8,128)} %get-tuple-element.70.refs_1_.base, ...), custom_call_target="tpu_custom_call" | custom-call | tf_op jit(solution)/shard_map/pallas_call | solution.py:1508
  493.5 0.0 copy-done
  493.5 0.8 copy.50
  (14 shorter events, 0.1 us)
Async XLA Ops:
  85.3 54.2 %copy-start.1 = (f32[16,1,128]{2,0,1:T(8,128)}, f32[16,1,128]{2,0,1:T(8,128)S(1)}, u32[]{:S(2)}) copy-start(f32[16,1,128]{2,0,1:T(8,128)S(1)} %add.58) | copy-start | bytes 24580
  386.5 100.7 %copy-start.2 = (bf16[64]{0:T(256)(128)(2,1)S(1)}, bf16[64]{0:T(256)(128)(2,1)}, u32[]{:S(2)}) copy-start(bf16[64]{0:T(256)(128)(2,1)} %param.17) | copy-start | bytes 388
  386.5 100.8 %copy-start.3 = (bf16[64]{0:T(256)(128)(2,1)S(1)}, bf16[64]{0:T(256)(128)(2,1)}, u32[]{:S(2)}) copy-start(bf16[64]{0:T(256)(128)(2,1)} %param.16) | copy-start | bytes 388
  487.8 5.7 %copy-start = (bf16[128,2048]{1,0:T(8,128)(2,1)S(1)}, bf16[128,2048]{1,0:T(8,128)(2,1)}, u32[]{:S(2)}) copy-start(bf16[128,2048]{1,0:T(8,128)(2,1)} %get-tuple-element.68) | copy-start | bytes 1572868

commit v6 on v5

--- a/solution.py
+++ b/solution.py
@@ -915,11 +915,17 @@
 
 
 def attend_forward_kernel(
-    x_ref, w_ref, bias, start, cosine, minus, plus, tokens, feed_set, gate_up, out_ref,
+    x_all, w_all, bias, start, cosine, minus, plus, tokens, feed_set, gate_up, out_ref,
     queries, keys, values, attended, log_total, mixed_heads, resid_mid, normed, gate_up_all, w_out,
-    low, own_sems, gate_up_sems, square_sems, pair_sems,
+    low, x_ref, w_ref, own_sems, gate_up_sems, square_sems, pair_sems, load_sems,
 ):
     at = Place()
+    loads = [
+        pltpu.make_async_copy(*pair_, load_sems[0].at[i])
+        for i, pair_ in enumerate(((x_all, x_ref), (w_all, w_ref)))
+    ]
+    for load in loads:
+        load.start()
     at.barrier()
     pair_send, pair_recv = pair_sems
 
@@ -947,6 +953,8 @@
     next(gate_up_job)
     scale = 1.0 / math.sqrt(local * 8 // HEADS)
     blocks = length // QROWS
+    for load in loads:
+        load.wait()
 
     @pl.loop(0, blocks)
     def _(i):
@@ -1043,14 +1051,17 @@
     length, local = x.shape[0], w.shape[1] // 3
     bf, f32 = jnp.bfloat16, jnp.float32
     flat, spans = pack_sems(
-        [[DMA((8,)), DMA((8,)), DMA], exchange_sems(), square_gather_sems(), [DMA((4,)), DMA((4,))]]
+        [
+            [DMA((8,)), DMA((8,)), DMA], exchange_sems(), square_gather_sems(), [DMA((4,)), DMA((4,))],
+            [DMA((2,))],
+        ]
     )
     outs = [((length, local), bf, VMEM)] * 3 + [((length, local), f32, VMEM)] * 2
     outs += [(tokens.shape, bf, VMEM), (tokens.shape, f32, VMEM), (tokens.shape, bf, VMEM)]
     outs += [(gate_up.shape, bf, HBM), ((4, 4, 2) + w_out.shape[1:], bf, VMEM)]
     return call(
-        grouped(attend_forward_kernel, 22, spans), [VMEM] * 9 + [HBM, HBM], outs,
-        [VMEM((length, local), bf)] + flat, 1,
+        grouped(attend_forward_kernel, 24, spans), [HBM] * 2 + [VMEM] * 7 + [HBM] * 2, outs,
+        [VMEM((length, local), bf), VMEM(x.shape, bf), VMEM(w.shape, bf)] + flat, 1,
         x, w, bias, start, *tables, tokens, feed_set, gate_up, w_out,
     )
 
@@ -1422,35 +1433,34 @@
         tokens_part[...] = part
 
     vector_job = vector_work()
-    next(out_job)
-    next(out_job)
     next(line_job)
-    next(out_job)
     loads[0].wait()
     steps(project_job, 3)
-    next(out_job)
     next(line_job)
     next(out_job)
     next(line_job)
     next(project_job)
+    next(out_job)
+    next(line_job)
     loads[1].wait()
     loads[2].wait()
     steps(down_job, 3)
     next(out_job)
-    next(line_job)
     next(project_job)
-    next(vector_job)
     next(line_job)
     next(project_job)
     next(out_job)
     next(vector_job)
     next(line_job)
+    next(out_job)
+    next(line_job)
     next(down_job)
-    next(line_job)
+    next(vector_job)
+    drive(line_job)
+    next(out_job)
+    tokens_work()
     drive(out_job)
     drive(vector_job)
-    drive(line_job)
-    tokens_work()
     drive(down_job)
     drive(project_job)
     inner = pieces.shape[2] // 3

time: 503 us -> 502 us (level)
  no operation moved by 1% of the time
where the time goes in v6:
time: 502 us; the launch traced here: 494 us
  Pallas kernels  479 us (95%)
  other arithmetic  8.05 us (2%)
  local copies, waits for them, and re-layouts  5.07 us (1%)
    pallas_call x5, Pallas kernels, call(): pl.pallas_call(kernel, out_shape=[jax.ShapeDtypeStruct(shape, kind) for s...  474 us

profile of v6, /device:TPU:0, one launch (start us, length us, event | category | flops | bytes accessed | tf_op | source)
XLA Modules:
  0.0 493.7 jit_solution(1988306832975329461)
XLA Ops:
  0.7 0.7 convert_element_type.39
  1.3 0.7 pad_bitcast_fusion.1
  2.0 0.1 pad.17.clone
  2.1 0.7 pad_maximum_fusion.1
  2.8 0.1 pad_select_fusion
  2.9 0.7 maximum_maximum_fusion.refs_1_
  3.5 78.5 %shard_map.220 = (bf16[32,16,128]{2,1,0:T(8,128)(2,1)}, bf16[1024,2048]{1,0:T(8,128)(2,1)}, bf16[512,768]{1,0:T(8,128)(2,1)}, bf16[2048,768]{1,0:T(8,128)(2,1)},...) custom-call(bf16[128,2048]{1,0:T(8,128)(2,1)} %bitcast.52, ...), custom_call_target="tpu_custom_call" | custom-call | tf_op jit(solution)/shard_map/pallas_call | solution.py:720
  82.1 0.9 slice.58
  82.9 1.0 slice_convert_fusion
  83.9 0.1 reshape.138
  84.0 0.6 convert.4.refs_2_
  84.7 0.6 add.62
  85.3 0.0 copy-start.1
  85.3 0.6 pad_maximum_fusion.refs_8_
  85.9 51.4 %shard_map.221 = (bf16[1024,256]{1,0:T(8,128)(2,1)}, bf16[1024,256]{1,0:T(8,128)(2,1)}, bf16[1024,256]{1,0:T(8,128)(2,1)}, f32[1024,256]{1,0:T(8,128)}, f32[1024...) custom-call(bf16[1024,2048]{1,0:T(8,128)(2,1)} %get-tuple-element.54, ...), custom_call_target="tpu_custom_call" | custom-call | tf_op jit(solution)/shard_map/pallas_call | solution.py:720
  137.4 0.0 copy-done.1
  137.4 191.8 %shard_map.222 = (bf16[1024,2048]{1,0:T(8,128)(2,1)}, bf16[1024,704]{1,0:T(8,128)(2,1)}, bf16[128,2048]{1,0:T(8,128)(2,1)}, bf16[512,1408]{1,0:T(8,128)(2,1)}, f...) custom-call(bf16[128,2048]{1,0:T(8,128)(2,1)} %get-tuple-element.63.refs_0_, ...), custom_call_target="tpu_custom_call" | custom-call | tf_op jit(solution)/shard_map/pallas_call | solution.py:720
  329.2 52.9 %shard_map.223 = (bf16[1024,768]{1,0:T(8,128)(2,1)}, bf16[4,64,2048]{2,1,0:T(8,128)(2,1)}, bf16[64,5632]{1,0:T(8,128)(2,1)}, bf16[64,5632]{1,0:T(8,128)(2,1)}) custom-call(bf16[1024,256]{1,0:T(8,128)(2,1)} %get-tuple-element.69.refs_0_, f32[128,2048]{1,0:T(8,128)} %get-tuple-element.70.refs_1_.base, bf16[1024,256]{1,0:T(8,128)(2,1)} %get-tuple-element.71.refs_2_, ...), custom_call_target="tpu_custom_call" | custom-call | tf_op jit(solution)/shard_map/pallas_call | solution.py:720
  382.0 1.7 convert_reduce_fusion
  383.7 0.1 broadcast_select_fusion
  383.8 0.1 select_n.42
  383.9 0.6 copy.47
  384.5 99.1 %shard_map.224 = (f32[128,2048]{1,0:T(8,128)}, bf16[64,6144]{1,0:T(8,128)(2,1)}, bf16[176,2048]{1,0:T(8,128)(2,1)}, bf16[64,2048]{1,0:T(8,128)(2,1)}, f32[8,128]{1,0:T(8,128)}) custom-call(bf16[2048,768]{1,0:T(8,128)(2,1)} %get-tuple-element.55.refs_1_.refs_0_, bf16[1024,768]{1,0:T(8,128)(2,1)} %get-tuple-element.78.refs_1_, ...), custom_call_target="tpu_custom_call" | custom-call | tf_op jit(solution)/shard_map/pallas_call | solution.py:720
  483.6 1.2 slice_bitcast_fusion
  484.8 0.8 slice_select_fusion
  485.7 0.5 slice_bitcast_fusion.1
  486.2 0.0 copy-done.2
  486.2 0.0 copy-done.3
  486.2 0.5 fusion
  486.7 5.7 %shard_map.225 = (f32[128,2048]{1,0:T(8,128)}, f32[64,6144]{1,0:T(8,128)}, f32[176,2048]{1,0:T(8,128)}, f32[64,2048]{1,0:T(8,128)}, f32[64,5632]{1,0:T(8,128)}, /*index=5*/f32[64,5632]{1,0:T(8,128)}) custom-call(f32[128,2048]{1,0:T(8,128)} %get-tuple-element.83.part, f32[128,2048]{1,0:T(8,128)} %get-tuple-element.70.refs_1_.base, ...), custom_call_target="tpu_custom_call" | custom-call | tf_op jit(solution)/shard_map/pallas_call | solution.py:1518
  492.4 0.0 copy-done
  492.4 0.8 copy.50
  (14 shorter events, 0.1 us)
Async XLA Ops:
  85.3 52.1 %copy-start.1 = (f32[16,1,128]{2,0,1:T(8,128)}, f32[16,1,128]{2,0,1:T(8,128)S(1)}, u32[]{:S(2)}) copy-start(f32[16,1,128]{2,0,1:T(8,128)S(1)} %add.58) | copy-start | bytes 24580
  384.5 101.7 %copy-start.2 = (bf16[64]{0:T(256)(128)(2,1)S(1)}, bf16[64]{0:T(256)(128)(2,1)}, u32[]{:S(2)}) copy-start(bf16[64]{0:T(256)(128)(2,1)} %param.17) | copy-start | bytes 388
  384.5 101.7 %copy-start.3 = (bf16[64]{0:T(256)(128)(2,1)S(1)}, bf16[64]{0:T(256)(128)(2,1)}, u32[]{:S(2)}) copy-start(bf16[64]{0:T(256)(128)(2,1)} %param.16) | copy-start | bytes 388
  486.7 5.7 %copy-start = (bf16[128,2048]{1,0:T(8,128)(2,1)S(1)}, bf16[128,2048]{1,0:T(8,128)(2,1)}, u32[]{:S(2)}) copy-start(bf16[128,2048]{1,0:T(8,128)(2,1)} %get-tuple-element.68) | copy-start | bytes 1572868
